TPU v7x, 128 devices: a whole 4x4x4 slice. The times are simulated.
128 devices in a mesh: ctx: 64 (over z, x, y_hi, core), head: 2 (over y_lo).
Axes of the slice: x: 4, y: 4 (y_hi: 2, y_lo: 2; y = y_hi * 2 + y_lo), z: 4, core: 2. Of those that a mesh axis runs over, the one named last changes fastest.
Arguments:
- queries: bfloat16 [24576, 4096], P(('ctx', 'head')), may hold values from -6 to 6
- keys: bfloat16 [24576, 4096], P(('ctx', 'head')), may hold values from -6 to 6
- values: bfloat16 [24576, 4096], P(('ctx', 'head')), may hold values from -6 to 6
- grad_out: bfloat16 [24576, 4096], P(('ctx', 'head')), may hold values from -6 to 6
- pattern: int32 [64, 4], P('ctx'), may hold values 0 or 1
- phase: int32 [64, 4], P('ctx'), may hold values from 0 to 7
Outputs:
- grad_queries: bfloat16 [24576, 4096], P(('ctx', 'head'))
- grad_keys: bfloat16 [24576, 4096], P(('ctx', 'head'))
- grad_values: bfloat16 [24576, 4096], P(('ctx', 'head'))
All inputs are finite; a program needn't handle non-finite values. No bound on the sum of `pattern` on one device may be relied on, other than what follows from the above.
Results may differ from a plain program's by a relative error of at most 0.04.
Values may be sent and summed in bfloat16 or wider, within the bound.
No kernel may reach another device: no remote copies, remote signals or barrier semaphores. Data moves between devices by JAX's collectives and lax.ppermute only.
A program may use at most 192 MiB of HBM per device.

v0:
```python
import math

import jax
import jax.numpy as jnp
from jax import lax
from jax.sharding import PartitionSpec as P

HD = 128
LEVELS = 4


NEG_FILL = -1e30


def passed_along(value, axis, steps):
    count = lax.axis_size(axis)
    initial, last = (max(0, -steps), min(count, count - steps))
    return lax.ppermute(value, axis, [(source, source + steps) for source in range(initial, last)])


def for_sending(value):
    return jax.tree.map(lambda a: a.astype(jnp.bfloat16) if a.dtype == jnp.float32 else a, value)


def guarded(is_active, worker, operand):
    if is_active is None:
        return worker(operand)
    return worker(operand)


def body(queries, keys, values, grad_out, pattern, phase):
    queries_here, keys_here, values_here, grads_here = (
        lax.all_to_all(queries, "head", split_axis=1, concat_axis=0, tiled=True),
        lax.all_to_all(keys, "head", split_axis=1, concat_axis=0, tiled=True),
        lax.all_to_all(values, "head", split_axis=1, concat_axis=0, tiled=True),
        lax.all_to_all(grad_out, "head", split_axis=1, concat_axis=0, tiled=True),
    )
    row_count, feat_width = queries_here.shape
    head_count = feat_width // HD
    group_size = math.gcd(head_count, 2)
    group_count = head_count // group_size
    scale_factor = HD ** (-0.5)
    block_id = lax.axis_index("ctx")
    remote = []
    for level_num in range(LEVELS):
        remote.append(passed_along((keys_here, values_here), "ctx", 2**level_num))
    position = jnp.arange(row_count, dtype=jnp.int32)
    causal = position[:, None] >= position[None, :]
    actives = []
    keeps = []
    for level_num in range(LEVELS):
        distance = 2**level_num
        is_active = (block_id >= distance) & (pattern[0, level_num] == 1)
        actives.append(is_active)
        keeps.append((is_active & (position % distance == phase[0, level_num] % distance))[None, :])

    def split_heads(array):
        return array.reshape(row_count, group_count, group_size, HD).transpose(1, 0, 2, 3)

    def join_heads(array):
        return array.transpose(1, 0, 2, 3).reshape(row_count, feat_width)

    far_key_stack = jnp.stack([split_heads(pair[0]) for pair in remote], axis=1)
    far_value_stack = jnp.stack([split_heads(pair[1]) for pair in remote], axis=1)

    def group_work(items):
        query_grp, key_grp, value_grp, grad_grp, far_keys, far_values = items
        tile_list = [(key_grp, value_grp, causal, None)]
        for level_num in range(LEVELS):
            tile_list.append(
                (far_keys[level_num], far_values[level_num], keeps[level_num], actives[level_num])
            )
        stored = []
        for key_tile, value_tile, allowed, is_active in tile_list:

            def scores(unused, key_tile=key_tile, value_tile=value_tile, allowed=allowed):
                logits = (
                    jnp.einsum(
                        "qhe,khe->hqk", query_grp, key_tile, preferred_element_type=jnp.float32
                    )
                    * scale_factor
                )
                logits = jnp.where(allowed[None], logits, NEG_FILL)
                dprobs = jnp.einsum(
                    "qhe,khe->hqk", grad_grp, value_tile, preferred_element_type=jnp.float32
                )
                return (logits, dprobs)

            stored.append(guarded(is_active, scores, 0))
        row_max = stored[0][0].max(axis=2, keepdims=True)
        for logits, dprobs in stored[1:]:
            row_max = jnp.maximum(row_max, jnp.max(logits, axis=2, keepdims=True))
        row_sum = jnp.zeros((group_size, row_count, 1), jnp.float32)
        for logits, dprobs in stored:
            row_sum = row_sum + jnp.sum(jnp.exp(logits - row_max), axis=2, keepdims=True)
        log_total = row_max + jnp.log(row_sum)
        prob_list = []
        delta = jnp.zeros((group_size, row_count, 1), jnp.float32)
        for logits, dprobs in stored:
            probs = jnp.exp(logits - log_total)
            rounded = probs.astype(jnp.bfloat16)
            prob_list.append((probs, rounded))
            delta = delta + jnp.sum(rounded.astype(jnp.float32) * dprobs, axis=2, keepdims=True)
        zero_tile = jnp.zeros((row_count, group_size, HD), jnp.float32)
        dq_total = zero_tile
        tile_grads = []
        for index_num in range(len(tile_list)):
            key_tile, value_tile, allowed, is_active = tile_list[index_num]

            def gradients(operand, key_tile=key_tile):
                probs, rounded, dprobs = operand
                dscores = (probs * (dprobs - delta)).astype(jnp.bfloat16)
                dq_part = (
                    jnp.einsum(
                        "hqk,khe->qhe", dscores, key_tile, preferred_element_type=jnp.float32
                    )
                    * scale_factor
                )
                dk_part = (
                    jnp.einsum(
                        "hqk,qhe->khe", dscores, query_grp, preferred_element_type=jnp.float32
                    )
                    * scale_factor
                )
                dv_part = jnp.einsum(
                    "hqk,qhe->khe", rounded, grad_grp, preferred_element_type=jnp.float32
                )
                return (dq_part, dk_part, dv_part)

            operand = (prob_list[index_num][0], prob_list[index_num][1], stored[index_num][1])
            dq_part, dk_part, dv_part = guarded(is_active, gradients, operand)
            dq_total = dq_total + dq_part
            tile_grads.append((dk_part, dv_part))
        dk_far = jnp.stack([pair[0].astype(jnp.bfloat16) for pair in tile_grads[1:]], axis=0)
        dv_far = jnp.stack([pair[1].astype(jnp.bfloat16) for pair in tile_grads[1:]], axis=0)
        return (dq_total, tile_grads[0][0], tile_grads[0][1], dk_far, dv_far)

    dq_groups, dk_own, dv_own, dk_far, dv_far = lax.map(
        group_work,
        (
            split_heads(queries_here),
            split_heads(keys_here),
            split_heads(values_here),
            split_heads(grads_here),
            far_key_stack,
            far_value_stack,
        ),
    )
    dk_sum = join_heads(dk_own)
    dv_sum = join_heads(dv_own)
    for level_num in range(LEVELS):
        back_keys, back_values = passed_along(
            (
                for_sending(join_heads(dk_far[:, level_num])),
                for_sending(join_heads(dv_far[:, level_num])),
            ),
            "ctx",
            -(2**level_num),
        )
        dk_sum = dk_sum + back_keys.astype(jnp.float32)
        dv_sum = dv_sum + back_values.astype(jnp.float32)
    grad_queries, grad_keys, grad_values = (
        lax.all_to_all(
            join_heads(dq_groups).astype(jnp.bfloat16),
            "head",
            split_axis=0,
            concat_axis=1,
            tiled=True,
        ),
        lax.all_to_all(
            dk_sum.astype(jnp.bfloat16), "head", split_axis=0, concat_axis=1, tiled=True
        ),
        lax.all_to_all(
            dv_sum.astype(jnp.bfloat16), "head", split_axis=0, concat_axis=1, tiled=True
        ),
    )
    return (grad_queries, grad_keys, grad_values)


def solution(mesh):
    placed = (
        P(("ctx", "head"), None),
        P(("ctx", "head"), None),
        P(("ctx", "head"), None),
        P(("ctx", "head"), None),
        P("ctx", None),
        P("ctx", None),
    )
    return jax.shard_map(
        body,
        mesh=mesh,
        in_specs=placed,
        out_specs=(P(("ctx", "head"), None), P(("ctx", "head"), None), P(("ctx", "head"), None)),
        check_vma=False,
    )
```

profile of v0, /device:TPU:38, one launch (start us, length us, event | category | flops | bytes accessed | tf_op | source)
XLA Modules:
  0.0 809.4 jit_solution(14755189165377655987)
XLA Ops:
  2.2 22.1 %all_to_all.124 = bf16[192,2,2048]{2,0,1:T(8,128)(2,1)S(1)} all-to-all(bf16[192,2,2048]{2,0,1:T(8,128)(2,1)S(1)} %bitcast.442), channel_id=1, replica_groups=mesh['ctx'=64,'head'=2] {'head'}, dimensions={1} | all-to-all | bytes 3145728 | tf_op jit(solution)/shard_map/all_to_all | solution.py:35
  24.3 4.7 collective-permute-start.7
  28.9 4.0 collective-permute-start.6
  33.0 5.1 collective-permute-start.5
  39.3 3.7 all-to-all-start
  45.7 41.8 %all-to-all-done = bf16[192,2,2048]{2,0,1:T(8,128)(2,1)S(1)} async-done(((bf16[192,2,2048]{2,0,1:T(8,128)(2,1)}), bf16[192,2,2048]{2,0,1:T(8,128)(2,1)S(1)}, u32[]{:S(2)}, u32[]{:S(2)}) %all-to-all-start) | async-done | bytes 1572896 | tf_op jit(solution)/shard_map/all_to_all | solution.py:34
  87.6 4.6 all-to-all-start.1
  97.0 4.6 collective-permute-start.2
  103.6 30.8 %collective-permute-done.5 = bf16[384,2048]{1,0:T(8,128)(2,1)} collective-permute-done((bf16[384,2048]{1,0:T(8,128)(2,1)S(1)}, bf16[384,2048]{1,0:T(8,128)(2,1)}, u32[]{:S(2)}, u32[]{:S(2)}) %collective-permute-start.5) | collective-permute-done | bytes 1572896 | tf_op jit(solution)/shard_map/ppermute | solution.py:18
  139.0 4.8 all-to-all-start.2
  153.6 3.8 reshape.198
  164.5 3.8 reshape.203
  181.4 27.8 %collective-permute-done.2 = bf16[384,2048]{1,0:T(8,128)(2,1)} collective-permute-done((bf16[384,2048]{1,0:T(8,128)(2,1)S(1)}, bf16[384,2048]{1,0:T(8,128)(2,1)}, u32[]{:S(2)}, u32[]{:S(2)}) %collective-permute-start.2) | collective-permute-done | bytes 1572896 | tf_op jit(solution)/shard_map/ppermute | solution.py:18
  211.8 23.7 %collective-permute-done.1 = bf16[384,2048]{1,0:T(8,128)(2,1)} collective-permute-done((bf16[384,2048]{1,0:T(8,128)(2,1)S(1)}, bf16[384,2048]{1,0:T(8,128)(2,1)}, u32[]{:S(2)}, u32[]{:S(2)}) %collective-permute-start.1) | collective-permute-done | bytes 1572896 | tf_op jit(solution)/shard_map/ppermute | solution.py:18
  238.1 29.0 %collective-permute-done = bf16[384,2048]{1,0:T(8,128)(2,1)} collective-permute-done((bf16[384,2048]{1,0:T(8,128)(2,1)S(1)}, bf16[384,2048]{1,0:T(8,128)(2,1)}, u32[]{:S(2)}, u32[]{:S(2)}) %collective-permute-start) | collective-permute-done | bytes 1572896 | tf_op jit(solution)/shard_map/ppermute | solution.py:18
  269.8 9.3 %pad_maximum_fusion = (bf16[8,4,384,2,128]{2,4,3,0,1:T(8,128)(2,1)}, bf16[8,4,384,2,128]{2,4,3,0,1:T(8,128)(2,1)}) fusion(bf16[8,1,384,2,128]{2,4,3,0,1:T(8,128)(2,1)} %bitcast.428, bf16[8,1,384,2,128]{2,4,3,0,1:T(8,128)(2,1)} %bitcast.430, bf16[8,1,384,2,128]{2,4,3,0,1:T(8,128)(2,1)} %bitcast.431, bf16[8,1,384,2,128]{2,4,3,0,1:T(8,128)(2,1)} %bitcast.434, ...), kind=kLoop, calls=%fused_computation.135 | loop fusion | flops 18874368 | bytes 25165824 | tf_op jit(solution)/shard_map/stack | solution.py:63
  279.1 246.8 %while.19 = (s32[]{:T(128)}, bf16[8,384,2,128]{1,3,2,0:T(8,128)(2,1)}, f32[8,384,2,128]{1,3,2,0:T(8,128)}, f32[8,384,2,128]{1,3,2,0:T(8,128)}, bf16[8,4,384,2,12...) while((s32[]{:T(128)}, ...), condition=%wide.region_16.17_spmd.clone, body=%wide.region_0.16_spmd.clone.sunk | while | flops 1919245824 | bytes 72783480 | solution.py:138
  526.0 5.4 fusion.83
  536.7 4.2 collective-permute-start.15
  544.5 16.6 %collective-permute-start.14 = (bf16[384,2048]{1,0:T(8,128)(2,1)}, bf16[384,2048]{1,0:T(8,128)(2,1)}, u32[]{:S(2)}, u32[]{:S(2)}) collective-permute-start(bf16[384,2048]{1,0:T(8,128)(2,1)} %copy.261), channel_id=1, source_target_pairs={{8,0},{10,2},{12,4},{14,6},{16,8},{18,10},{20,12},{22,14},{24,16},... | collective-permute-start | bytes 4718600 | tf_op jit(solution)/shard_map/ppermute | solution.py:18
  564.6 5.4 fusion.84
  581.1 4.3 collective-permute-start.9
  585.4 24.3 %collective-permute-done.13 = bf16[384,2048]{1,0:T(8,128)(2,1)} collective-permute-done((bf16[384,2048]{1,0:T(8,128)(2,1)}, bf16[384,2048]{1,0:T(8,128)(2,1)}, u32[]{:S(2)}, u32[]{:S(2)}) %collective-permute-start.13) | collective-permute-done | bytes 1572896 | tf_op jit(solution)/shard_map/ppermute | solution.py:18
  611.6 59.1 %collective-permute-done.14 = bf16[384,2048]{1,0:T(8,128)(2,1)} collective-permute-done((bf16[384,2048]{1,0:T(8,128)(2,1)}, bf16[384,2048]{1,0:T(8,128)(2,1)}, u32[]{:S(2)}, u32[]{:S(2)}) %collective-permute-start.14) | collective-permute-done | bytes 1572896 | tf_op jit(solution)/shard_map/ppermute | solution.py:18
  676.7 4.6 all-to-all-start.4
  683.7 5.5 add_convert_fusion
  689.2 31.3 %all-to-all-done.4 = bf16[2,192,2048]{2,1,0:T(8,128)(2,1)} async-done(((bf16[2,192,2048]{2,1,0:T(8,128)(2,1)}), bf16[2,192,2048]{2,1,0:T(8,128)(2,1)}, u32[]{:S(2)}, u32[]{:S(2)}) %all-to-all-start.4) | async-done | bytes 1572896 | tf_op jit(solution)/shard_map/all_to_all | solution.py:163
  720.6 4.6 all-to-all-start.6
  729.2 52.7 %collective-permute-done.10 = bf16[384,2048]{1,0:T(8,128)(2,1)} collective-permute-done((bf16[384,2048]{1,0:T(8,128)(2,1)}, bf16[384,2048]{1,0:T(8,128)(2,1)}, u32[]{:S(2)}, u32[]{:S(2)}) %collective-permute-start.10) | collective-permute-done | bytes 1572896 | tf_op jit(solution)/shard_map/ppermute | solution.py:18
  781.9 5.5 add_convert_fusion.1
  787.3 3.7 all-to-all-start.5
  796.5 11.6 %all-to-all-done.5 = bf16[2,192,2048]{2,1,0:T(8,128)(2,1)S(1)} async-done(((bf16[2,192,2048]{2,1,0:T(8,128)(2,1)}), bf16[2,192,2048]{2,1,0:T(8,128)(2,1)S(1)}, u32[]{:S(2)}, u32[]{:S(2)}) %all-to-all-start.5) | async-done | bytes 1572896 | tf_op jit(solution)/shard_map/all_to_all | solution.py:170
  (381 shorter events, 336.2 us)
Async XLA Ops:
  2.1 35.9 %copy-start.2 = (bf16[192,4096]{1,0:T(8,128)(2,1)S(1)}, bf16[192,4096]{1,0:T(8,128)(2,1)}, u32[]{:S(2)}) copy-start(bf16[192,4096]{1,0:T(8,128)(2,1)} %param.9) | copy-start | bytes 4718596
  24.3 72.7 %collective-permute-start.7 = (bf16[384,2048]{1,0:T(8,128)(2,1)S(1)}, bf16[384,2048]{1,0:T(8,128)(2,1)}, u32[]{:S(2)}, u32[]{:S(2)}) collective-permute-start(bf16[384,2048]{1,0:T(8,128)(2,1)S(1)} %bitcast.417), channel_id=1, source_target_pairs={{0,16},{2,18},{4,20},{6,22},{8,24},{10,26},{12,28},{14,30},{16,32}... | collective-permute-start | bytes 4718600 | tf_op jit(solution)/shard_map/ppermute | solution.py:18
  28.9 72.7 %collective-permute-start.6 = (bf16[384,2048]{1,0:T(8,128)(2,1)S(1)}, bf16[384,2048]{1,0:T(8,128)(2,1)}, u32[]{:S(2)}, u32[]{:S(2)}) collective-permute-start(bf16[384,2048]{1,0:T(8,128)(2,1)S(1)} %bitcast.418), channel_id=1, source_target_pairs={{0,8},{2,10},{4,12},{6,14},{8,16},{10,18},{12,20},{14,22},{16,24},... | collective-permute-start | bytes 4718600 | tf_op jit(solution)/shard_map/ppermute | solution.py:18
  33.0 101.4 %collective-permute-start.5 = (bf16[384,2048]{1,0:T(8,128)(2,1)S(1)}, bf16[384,2048]{1,0:T(8,128)(2,1)}, u32[]{:S(2)}, u32[]{:S(2)}) collective-permute-start(bf16[384,2048]{1,0:T(8,128)(2,1)S(1)} %bitcast.419), channel_id=1, source_target_pairs={{0,4},{2,6},{4,8},{6,10},{8,12},{10,14},{12,16},{14,18},{16,20},{1... | collective-permute-start | bytes 4718600 | tf_op jit(solution)/shard_map/ppermute | solution.py:18
  39.3 48.3 %all-to-all-start = ((bf16[192,2,2048]{2,0,1:T(8,128)(2,1)}), bf16[192,2,2048]{2,0,1:T(8,128)(2,1)S(1)}, u32[]{:S(2)}, u32[]{:S(2)}) async-start(bf16[192,2,2048]{2,0,1:T(8,128)(2,1)} %bitcast.439), calls=%async_computation | async-start | bytes 3145728 | tf_op jit(solution)/shard_map/all_to_all | solution.py:34
  87.6 51.4 %all-to-all-start.1 = ((bf16[192,2,2048]{2,0,1:T(8,128)(2,1)}), bf16[192,2,2048]{2,0,1:T(8,128)(2,1)}, u32[]{:S(2)}, u32[]{:S(2)}) async-start(bf16[192,2,2048]{2,0,1:T(8,128)(2,1)} %bitcast.423), calls=%async_computation.1 | async-start | bytes 3145728 | tf_op jit(solution)/shard_map/all_to_all | solution.py:33
  92.2 84.0 %collective-permute-start.4 = (bf16[384,2048]{1,0:T(8,128)(2,1)S(1)}, bf16[384,2048]{1,0:T(8,128)(2,1)}, u32[]{:S(2)}, u32[]{:S(2)}) collective-permute-start(bf16[384,2048]{1,0:T(8,128)(2,1)S(1)} %bitcast.420), channel_id=1, source_target_pairs={{0,2},{2,4},{4,6},{6,8},{8,10},{10,12},{12,14},{14,16},{16,18},{18... | collective-permute-start | bytes 4718600 | tf_op jit(solution)/shard_map/ppermute | solution.py:18
  94.1 84.6 %collective-permute-start.3 = (bf16[384,2048]{1,0:T(8,128)(2,1)S(1)}, bf16[384,2048]{1,0:T(8,128)(2,1)}, u32[]{:S(2)}, u32[]{:S(2)}) collective-permute-start(bf16[384,2048]{1,0:T(8,128)(2,1)S(1)} %bitcast.412), channel_id=1, source_target_pairs={{0,16},{2,18},{4,20},{6,22},{8,24},{10,26},{12,28},{14,30},{16,32}... | collective-permute-start | bytes 4718600 | tf_op jit(solution)/shard_map/ppermute | solution.py:18
  97.0 112.1 %collective-permute-start.2 = (bf16[384,2048]{1,0:T(8,128)(2,1)S(1)}, bf16[384,2048]{1,0:T(8,128)(2,1)}, u32[]{:S(2)}, u32[]{:S(2)}) collective-permute-start(bf16[384,2048]{1,0:T(8,128)(2,1)S(1)} %bitcast.413), channel_id=1, source_target_pairs={{0,8},{2,10},{4,12},{6,14},{8,16},{10,18},{12,20},{14,22},{16,24},... | collective-permute-start | bytes 4718600 | tf_op jit(solution)/shard_map/ppermute | solution.py:18
  101.7 133.9 %collective-permute-start.1 = (bf16[384,2048]{1,0:T(8,128)(2,1)S(1)}, bf16[384,2048]{1,0:T(8,128)(2,1)}, u32[]{:S(2)}, u32[]{:S(2)}) collective-permute-start(bf16[384,2048]{1,0:T(8,128)(2,1)S(1)} %bitcast.414), channel_id=1, source_target_pairs={{0,4},{2,6},{4,8},{6,10},{8,12},{10,14},{12,16},{14,18},{16,20},{1... | collective-permute-start | bytes 4718600 | tf_op jit(solution)/shard_map/ppermute | solution.py:18
  134.4 132.8 %collective-permute-start = (bf16[384,2048]{1,0:T(8,128)(2,1)S(1)}, bf16[384,2048]{1,0:T(8,128)(2,1)}, u32[]{:S(2)}, u32[]{:S(2)}) collective-permute-start(bf16[384,2048]{1,0:T(8,128)(2,1)S(1)} %bitcast.415), channel_id=1, source_target_pairs={{0,2},{2,4},{4,6},{6,8},{8,10},{10,12},{12,14},{14,16},{16,18},{18... | collective-permute-start | bytes 4718600 | tf_op jit(solution)/shard_map/ppermute | solution.py:18
  139.0 4.8 copy-start.5
  139.0 11.3 %copy-start.4 = (s32[1,4]{1,0:T(1,128)S(1)}, s32[1,4]{1,0:T(1,128)}, u32[]{:S(2)}) copy-start(s32[1,4]{1,0:T(1,128)} %param.12) | copy-start | bytes 52
  139.0 25.5 %all-to-all-start.2 = ((bf16[192,2,2048]{2,0,1:T(8,128)(2,1)}), bf16[192,2,2048]{2,0,1:T(8,128)(2,1)}, u32[]{:S(2)}, u32[]{:S(2)}) async-start(bf16[192,2,2048]{2,0,1:T(8,128)(2,1)} %bitcast.422), calls=%async_computation.2 | async-start | bytes 3145728 | tf_op jit(solution)/shard_map/all_to_all | solution.py:36
  238.1 31.7 %copy-start = (bf16[384,2048]{0,1:T(8,128)(2,1)S(1)}, bf16[384,2048]{0,1:T(8,128)(2,1)}, u32[]{:S(2)}) copy-start(bf16[384,2048]{0,1:T(8,128)(2,1)} %copy.202) | copy-start | bytes 4718596
  267.2 2.7 copy-start.1
  536.7 44.4 %collective-permute-start.15 = (bf16[384,2048]{1,0:T(8,128)(2,1)}, bf16[384,2048]{1,0:T(8,128)(2,1)}, u32[]{:S(2)}, u32[]{:S(2)}) collective-permute-start(bf16[384,2048]{1,0:T(8,128)(2,1)} %copy.262), channel_id=1, source_target_pairs={{16,0},{18,2},{20,4},{22,6},{24,8},{26,10},{28,12},{30,14},{32,16}... | collective-permute-start | bytes 4718600 | tf_op jit(solution)/shard_map/ppermute | solution.py:18
  540.9 68.9 %collective-permute-start.13 = (bf16[384,2048]{1,0:T(8,128)(2,1)}, bf16[384,2048]{1,0:T(8,128)(2,1)}, u32[]{:S(2)}, u32[]{:S(2)}) collective-permute-start(bf16[384,2048]{1,0:T(8,128)(2,1)} %copy.260), channel_id=1, source_target_pairs={{4,0},{6,2},{8,4},{10,6},{12,8},{14,10},{16,12},{18,14},{20,16},{2... | collective-permute-start | bytes 4718600 | tf_op jit(solution)/shard_map/ppermute | solution.py:18
  544.5 126.3 %collective-permute-start.14 = (bf16[384,2048]{1,0:T(8,128)(2,1)}, bf16[384,2048]{1,0:T(8,128)(2,1)}, u32[]{:S(2)}, u32[]{:S(2)}) collective-permute-start(bf16[384,2048]{1,0:T(8,128)(2,1)} %copy.261), channel_id=1, source_target_pairs={{8,0},{10,2},{12,4},{14,6},{16,8},{18,10},{20,12},{22,14},{24,16},... | collective-permute-start | bytes 4718600 | tf_op jit(solution)/shard_map/ppermute | solution.py:18
  562.7 121.0 %collective-permute-start.12 = (bf16[384,2048]{1,0:T(8,128)(2,1)}, bf16[384,2048]{1,0:T(8,128)(2,1)}, u32[]{:S(2)}, u32[]{:S(2)}) collective-permute-start(bf16[384,2048]{1,0:T(8,128)(2,1)} %copy.259), channel_id=1, source_target_pairs={{2,0},{4,2},{6,4},{8,6},{10,8},{12,10},{14,12},{16,14},{18,16},{20... | collective-permute-start | bytes 4718600 | tf_op jit(solution)/shard_map/ppermute | solution.py:18
  577.0 95.7 %copy-start.3 = (bf16[8,384,2,128]{1,3,2,0:T(8,128)(2,1)S(1)}, bf16[8,384,2,128]{1,3,2,0:T(8,128)(2,1)}, u32[]{:S(2)}) copy-start(bf16[8,384,2,128]{1,3,2,0:T(8,128)(2,1)} %get-tuple-element.94) | copy-start | bytes 4718596
  578.6 149.0 %collective-permute-start.11 = (bf16[384,2048]{1,0:T(8,128)(2,1)}, bf16[384,2048]{1,0:T(8,128)(2,1)}, u32[]{:S(2)}, u32[]{:S(2)}) collective-permute-start(bf16[384,2048]{1,0:T(8,128)(2,1)} %copy.257), channel_id=1, source_target_pairs={{16,0},{18,2},{20,4},{22,6},{24,8},{26,10},{28,12},{30,14},{32,16}... | collective-permute-start | bytes 4718600 | tf_op jit(solution)/shard_map/ppermute | solution.py:18
  581.1 148.1 %collective-permute-start.9 = (bf16[384,2048]{1,0:T(8,128)(2,1)}, bf16[384,2048]{1,0:T(8,128)(2,1)}, u32[]{:S(2)}, u32[]{:S(2)}) collective-permute-start(bf16[384,2048]{1,0:T(8,128)(2,1)} %copy.255), channel_id=1, source_target_pairs={{4,0},{6,2},{8,4},{10,6},{12,8},{14,10},{16,12},{18,14},{20,16},{2... | collective-permute-start | bytes 4718600 | tf_op jit(solution)/shard_map/ppermute | solution.py:18
  609.7 172.2 %collective-permute-start.10 = (bf16[384,2048]{1,0:T(8,128)(2,1)}, bf16[384,2048]{1,0:T(8,128)(2,1)}, u32[]{:S(2)}, u32[]{:S(2)}) collective-permute-start(bf16[384,2048]{1,0:T(8,128)(2,1)} %copy.256), channel_id=1, source_target_pairs={{8,0},{10,2},{12,4},{14,6},{16,8},{18,10},{20,12},{22,14},{24,16},... | collective-permute-start | bytes 4718600 | tf_op jit(solution)/shard_map/ppermute | solution.py:18
  670.7 111.1 %collective-permute-start.8 = (bf16[384,2048]{1,0:T(8,128)(2,1)}, bf16[384,2048]{1,0:T(8,128)(2,1)}, u32[]{:S(2)}, u32[]{:S(2)}) collective-permute-start(bf16[384,2048]{1,0:T(8,128)(2,1)} %copy.254), channel_id=1, source_target_pairs={{2,0},{4,2},{6,4},{8,6},{10,8},{12,10},{14,12},{16,14},{18,16},{20... | collective-permute-start | bytes 4718600 | tf_op jit(solution)/shard_map/ppermute | solution.py:18
  676.7 43.9 %all-to-all-start.4 = ((bf16[2,192,2048]{2,1,0:T(8,128)(2,1)}), bf16[2,192,2048]{2,1,0:T(8,128)(2,1)}, u32[]{:S(2)}, u32[]{:S(2)}) async-start(bf16[2,192,2048]{2,1,0:T(8,128)(2,1)} %convert_element_type.135), calls=%async_computation.4 | async-start | bytes 3145728 | tf_op jit(solution)/shard_map/all_to_all | solution.py:163
  720.6 66.8 %all-to-all-start.6 = ((bf16[2,192,2048]{2,1,0:T(8,128)(2,1)}), bf16[2,192,2048]{2,1,0:T(8,128)(2,1)}, u32[]{:S(2)}, u32[]{:S(2)}) async-start(bf16[2,192,2048]{2,1,0:T(8,128)(2,1)} %bitcast.443), calls=%async_computation.6 | async-start | bytes 3145728 | tf_op jit(solution)/shard_map/all_to_all | solution.py:173
  787.3 20.8 %all-to-all-start.5 = ((bf16[2,192,2048]{2,1,0:T(8,128)(2,1)}), bf16[2,192,2048]{2,1,0:T(8,128)(2,1)S(1)}, u32[]{:S(2)}, u32[]{:S(2)}) async-start(bf16[2,192,2048]{2,1,0:T(8,128)(2,1)} %bitcast.444), calls=%async_computation.5 | async-start | bytes 3145728 | tf_op jit(solution)/shard_map/all_to_all | solution.py:170
where the time goes:
time: 825 us; the launch traced here: 809 us
  waiting for transfers between devices  336 us (41%)
  matrix products  184 us (22%)
  local copies, waits for them, and re-layouts  120 us (15%)
  starting transfers between devices  88.2 us (11%)
  other arithmetic  47.8 us (6%)
  blocking collectives  22.1 us (3%)
  between operations  9.46 us (1%)
    ppermute x16, waiting for transfers between devices, passed_along(): lax.ppermute(value, axis, [(source, source + steps) for source in range(i...  249 us
    ppermute x16, starting transfers between devices, passed_along(): lax.ppermute(value, axis, [(source, source + steps) for source in range(i...  62.2 us
    dot_general x40, matrix products, scores(): jnp.einsum('qhe,khe->hqk', grad_grp, value_tile, preferred_element_type=j...  50.4 us
    dot_general x40, matrix products, gradients(): jnp.einsum('hqk,khe->qhe', dscores, key_tile, preferred_element_type=jnp....  47 us
    dot_general x40, matrix products, scores(): jnp.einsum('qhe,khe->hqk', query_grp, key_tile, preferred_element_type=jn...  45.1 us
    all_to_all x1, waiting for transfers between devices, body(): lax.all_to_all(keys, 'head', split_axis=1, concat_axis=0, tiled=True)  41.8 us
    dynamic_slice x32, local copies, waits for them, and re-layouts, body(): lax.map(group_work, (split_heads(queries_here), split_heads(keys_here), s...  34.2 us
    all_to_all x1, waiting for transfers between devices, body(): lax.all_to_all(join_heads(dq_groups).astype(jnp.bfloat16), 'head', split_...  31.3 us
  transfers between devices with their start and end apart: 22, of which 12 were waited for; matrix products, arithmetic and copies ran while one was open for 10% of the time, Pallas kernels for 0%

commit v1 on v0

v1 whole, which is shorter than its diff:
```python
import functools
import math

import jax
import jax.numpy as jnp
from jax import lax
from jax.experimental import pallas as pl
from jax.experimental.pallas import tpu as pltpu
from jax.sharding import Mesh, PartitionSpec as P

HD = 128
BLK = 384
HALF = 192
LEVELS = 4
LINE = 8
GROUP = 4
CHUNKS = 4
NEG = -1e30
SCALE = HD**-0.5
LOG2E = math.log2(math.e)
NEXT_L1 = BLK
NEXT_L2 = BLK + BLK // 2
NEXT_ROWS = NEXT_L2 + 3 * (BLK // 4)
FAR_ROWS = GROUP * (BLK // 8)
KEYS = BLK + BLK + BLK // 2 + BLK // 4 + BLK // 8
SEG = [0, BLK, 2 * BLK, 2 * BLK + BLK // 2, 2 * BLK + BLK // 2 + BLK // 4, KEYS]
OWN, NXT, AFT = 16, 32, 48
LINE_AXES = ("yh", "core", "yl")
GROUP_AXES = ("z", "x")
F32 = jnp.float32
BF16 = jnp.bfloat16


def dot(a, b, dims):
    return lax.dot_general(a, b, ((dims[0], dims[1]), ((), ())), preferred_element_type=F32)


def picker(stride, phase):
    rows = BLK // stride
    row = lax.broadcasted_iota(jnp.int32, (rows, BLK), 0)
    col = lax.broadcasted_iota(jnp.int32, (rows, BLK), 1)
    return jnp.where(col == row * stride + (phase & (stride - 1)), 1.0, 0.0).astype(BF16)


def spreader(stride, phase):
    cols = BLK // stride
    row = lax.broadcasted_iota(jnp.int32, (BLK, cols), 0)
    col = lax.broadcasted_iota(jnp.int32, (BLK, cols), 1)
    return jnp.where(row == col * stride + (phase & (stride - 1)), 1.0, 0.0).astype(BF16)


def pick(stride, phase, rows):
    return dot(picker(stride, phase), rows, ((1,), (0,))).astype(BF16)


def spread(stride, phase, rows):
    return dot(spreader(stride, phase), rows, ((1,), (0,)))


def kv_of(y_ref, block):
    at = pl.ds(2 * block, 2)
    return jnp.concatenate(
        [y_ref[at, 0, 0].reshape(BLK, HD), y_ref[at, 0, 1].reshape(BLK, HD)], axis=1
    )


def send_kernel(meta, y_ref, next_ref, far_ref):
    next_ref[0, 0:BLK] = kv_of(y_ref, 3)
    next_ref[0, NEXT_L1:NEXT_L2] = pick(2, meta[NXT + 1], kv_of(y_ref, 2))
    for b in range(3):
        lo = NEXT_L2 + b * 96
        next_ref[0, lo : lo + 96] = pick(4, meta[NXT + 4 * b + 2], kv_of(y_ref, b))
    for b in range(GROUP):
        far_ref[0, 48 * b : 48 * b + 48] = pick(8, meta[AFT + 4 * b + 3], kv_of(y_ref, b))


def main_kernel(meta, y_ref, next_ref, far_ref, dq_ref, acc_ref, rnext_ref, rfar_ref, kv, s, dp, p, ds, prev):
    b = pl.program_id(1)

    @pl.when(b == 0)
    def _():
        prev[...] = jnp.zeros_like(prev)
        p[0:BLK] = jnp.zeros((BLK, BLK), BF16)
        ds[0:BLK] = jnp.zeros((BLK, BLK), BF16)

    kv[0:BLK] = kv_of(y_ref, b)

    @pl.when(b == 0)
    def _():
        kv[SEG[1] : SEG[2]] = next_ref[0, 0:BLK]
        kv[SEG[2] : SEG[3]] = next_ref[0, NEXT_L1:NEXT_L2]

    @pl.when(b > 0)
    def _():
        kv[SEG[1] : SEG[2]] = kv_of(y_ref, b - 1)

    @pl.when(b == 1)
    def _():
        kv[SEG[2] : SEG[3]] = pick(2, meta[OWN + 4 * b + 1], next_ref[0, 0:BLK])

    @pl.when(b > 1)
    def _():
        kv[SEG[2] : SEG[3]] = pick(2, meta[OWN + 4 * b + 1], kv_of(y_ref, b - 2))

    l2_at = pl.ds(pl.multiple_of(NEXT_L2 + 96 * jnp.minimum(b, 2), 32), 96)
    l3_at = pl.ds(pl.multiple_of(48 * b, 16), 48)

    @pl.when(b < 3)
    def _():
        kv[SEG[3] : SEG[4]] = next_ref[0, l2_at]

    @pl.when(b == 3)
    def _():
        kv[SEG[3] : SEG[4]] = pick(4, meta[OWN + 4 * b + 2], next_ref[0, 0:BLK])

    kv[SEG[4] : SEG[5]] = far_ref[0, l3_at]

    at = pl.ds(2 * b, 2)
    q = y_ref[at, 0, 2].reshape(BLK, HD)
    do = y_ref[at, 0, 3].reshape(BLK, HD)
    s[...] = dot(kv[:, :HD], q, ((1,), (1,)))
    dp[...] = dot(kv[:, HD:], do, ((1,), (1,)))

    biases = [None] + [jnp.where(meta[4 * b + k] == 1, 0.0, NEG).astype(F32) for k in range(LEVELS)]
    row = lax.broadcasted_iota(jnp.int32, (128, 128), 0)
    col = lax.broadcasted_iota(jnp.int32, (128, 128), 1)
    upper = row <= col
    c = SCALE * LOG2E
    for i in range(3):
        lanes = slice(128 * i, 128 * i + 128)
        tiles = [(128 * j, 128 * j + 128, 0) for j in range(i + 1)]
        tiles += [(BLK + 128 * j, BLK + 128 * j + 128, 1) for j in range(3)]
        tiles += [(SEG[2], SEG[2] + 96, 2), (SEG[2] + 96, SEG[3], 2), (SEG[3], SEG[4], 3), (SEG[4], SEG[5], 4)]
        m = None
        for lo, hi, seg in tiles:
            t = s[lo:hi, lanes]
            if seg == 0 and lo == 128 * i:
                t = jnp.where(upper, t, NEG)
                s[lo:hi, lanes] = t
            t = jnp.max(t, axis=0, keepdims=True)
            if biases[seg] is not None:
                t = t + biases[seg]
            m = t if m is None else jnp.maximum(m, t)
        m = m * c
        total = jnp.zeros((1, 128), F32)
        delta = jnp.zeros((1, 128), F32)
        for lo, hi, seg in tiles:
            shift = m if biases[seg] is None else m - biases[seg]
            e = jnp.exp2(s[lo:hi, lanes] * c - shift)
            s[lo:hi, lanes] = e
            total = total + jnp.sum(e, axis=0, keepdims=True)
            delta = delta + jnp.sum(e * dp[lo:hi, lanes], axis=0, keepdims=True)
        inv = 1.0 / total
        delta = delta * inv
        for lo, hi, seg in tiles:
            prob = s[lo:hi, lanes] * inv
            p[lo:hi, lanes] = prob.astype(BF16)
            ds[lo:hi, lanes] = (prob * (dp[lo:hi, lanes] - delta)).astype(BF16)

    dq_ref[0, 0] = (dot(ds[...], kv[:, :HD], ((0,), (0,))) * SCALE).astype(BF16)

    def grads(k):
        rows = slice(SEG[k], SEG[k + 1])
        dk = dot(ds[rows], q, ((1,), (0,))) * SCALE
        dv = dot(p[rows], do, ((1,), (0,)))
        return jnp.concatenate([dk, dv], axis=1)

    acc_ref[0, b] = grads(0)
    near = grads(1)

    @pl.when(b == 0)
    def _():
        prev[...] += near

    @pl.when(b > 0)
    def _():
        acc_ref[0, b - 1] += near

    term = grads(2).astype(BF16)

    @pl.when(b == 0)
    def _():
        rnext_ref[0, NEXT_L1:NEXT_L2] = term

    @pl.when(b == 1)
    def _():
        prev[...] += spread(2, meta[OWN + 4 * b + 1], term)

    @pl.when(b > 1)
    def _():
        acc_ref[0, b - 2] += spread(2, meta[OWN + 4 * b + 1], term)

    term2 = grads(3).astype(BF16)

    @pl.when(b < 3)
    def _():
        rnext_ref[0, l2_at] = term2

    @pl.when(b == 3)
    def _():
        rnext_ref[0, 0:BLK] = (prev[...] + spread(4, meta[OWN + 4 * b + 2], term2)).astype(BF16)

    rfar_ref[0, l3_at] = grads(4).astype(BF16)


def join_kernel(meta, acc_ref, dq_ref, rnext_ref, rfar_ref, z_ref, t):
    b = pl.program_id(1)
    l2_at = pl.ds(pl.multiple_of(NEXT_L2 + 96 * jnp.minimum(b, 2), 32), 96)
    l3_at = pl.ds(pl.multiple_of(48 * b, 16), 48)
    t[...] = acc_ref[0, 0] + spread(8, meta[AFT + 4 * b + 3], rfar_ref[0, l3_at])

    @pl.when(b < 3)
    def _():
        t[...] += spread(4, meta[NXT + 4 * b + 2], rnext_ref[0, l2_at])

    @pl.when(b == 2)
    def _():
        t[...] += spread(2, meta[NXT + 1], rnext_ref[0, NEXT_L1:NEXT_L2])

    @pl.when(b == 3)
    def _():
        t[...] += rnext_ref[0, 0:BLK].astype(F32)

    z_ref[:, 0, 0] = dq_ref[0, 0].reshape(2, HALF, HD)
    z_ref[:, 0, 1] = t[:, :HD].astype(BF16).reshape(2, HALF, HD)
    z_ref[:, 0, 2] = t[:, HD:].astype(BF16).reshape(2, HALF, HD)


SMEM = pl.BlockSpec(memory_space=pltpu.SMEM)


def params(mib):
    return pltpu.CompilerParams(
        dimension_semantics=("arbitrary", "arbitrary"), vmem_limit_bytes=mib * 2**20
    )


def whole(shape):
    return pl.BlockSpec((1, *shape), lambda h, b: (h,) + (0,) * len(shape))


def y_spec(arrays):
    return pl.BlockSpec((LINE, 1, arrays, HALF, HD), lambda h, b: (0, h, 0, 0, 0))


def rows_to_send(meta, y):
    heads = y.shape[1]
    return pl.pallas_call(
        send_kernel,
        grid=(heads, 1),
        in_specs=[SMEM, y_spec(2)],
        out_specs=[whole((NEXT_ROWS, 2 * HD)), whole((FAR_ROWS, 2 * HD))],
        out_shape=[
            jax.ShapeDtypeStruct((heads, NEXT_ROWS, 2 * HD), BF16),
            jax.ShapeDtypeStruct((heads, FAR_ROWS, 2 * HD), BF16),
        ],
        compiler_params=params(16),
        cost_estimate=pl.CostEstimate(flops=heads * 2**27, bytes_accessed=heads * 2**21, transcendentals=0),
        name="rows_to_send",
    )(meta, y)


def attention(meta, y, near, far):
    heads = y.shape[1]
    return pl.pallas_call(
        main_kernel,
        grid=(heads, GROUP),
        in_specs=[SMEM, y_spec(4), whole((NEXT_ROWS, 2 * HD)), whole((FAR_ROWS, 2 * HD))],
        out_specs=[
            pl.BlockSpec((1, 1, BLK, HD), lambda h, b: (h, b, 0, 0)),
            whole((GROUP, BLK, 2 * HD)),
            whole((NEXT_ROWS, 2 * HD)),
            whole((FAR_ROWS, 2 * HD)),
        ],
        out_shape=[
            jax.ShapeDtypeStruct((heads, GROUP, BLK, HD), BF16),
            jax.ShapeDtypeStruct((heads, GROUP, BLK, 2 * HD), F32),
            jax.ShapeDtypeStruct((heads, NEXT_ROWS, 2 * HD), BF16),
            jax.ShapeDtypeStruct((heads, FAR_ROWS, 2 * HD), BF16),
        ],
        scratch_shapes=[
            pltpu.VMEM((KEYS, 2 * HD), BF16),
            pltpu.VMEM((KEYS, BLK), F32),
            pltpu.VMEM((KEYS, BLK), F32),
            pltpu.VMEM((KEYS, BLK), BF16),
            pltpu.VMEM((KEYS, BLK), BF16),
            pltpu.VMEM((BLK, 2 * HD), F32),
        ],
        compiler_params=params(32),
        cost_estimate=pl.CostEstimate(
            flops=heads * GROUP * BLK * KEYS * HD * 10 * 4,
            bytes_accessed=heads * 5 * 2**20,
            transcendentals=heads * GROUP * BLK * KEYS,
        ),
        name="attention",
    )(meta, y, near, far)


def joined(meta, acc, dq, near, far):
    heads = acc.shape[0]
    return pl.pallas_call(
        join_kernel,
        grid=(heads, GROUP),
        in_specs=[
            SMEM,
            pl.BlockSpec((1, 1, BLK, 2 * HD), lambda h, b: (h, b, 0, 0)),
            pl.BlockSpec((1, 1, BLK, HD), lambda h, b: (h, b, 0, 0)),
            whole((NEXT_ROWS, 2 * HD)),
            whole((FAR_ROWS, 2 * HD)),
        ],
        out_specs=pl.BlockSpec((2, 1, 3, HALF, HD), lambda h, b: (b, h, 0, 0, 0)),
        out_shape=jax.ShapeDtypeStruct((LINE, heads, 3, HALF, HD), BF16),
        scratch_shapes=[pltpu.VMEM((BLK, 2 * HD), F32)],
        compiler_params=params(16),
        cost_estimate=pl.CostEstimate(flops=heads * 2**28, bytes_accessed=heads * 2**22, transcendentals=0),
        name="joined",
    )(meta, acc, dq, near, far)


def shift(value, steps):
    count = lax.axis_size(GROUP_AXES)
    pairs = [(i, i + steps) for i in range(count) if 0 <= i + steps < count]
    return lax.ppermute(value, GROUP_AXES, pairs)


def both(value, axis):
    other = lax.ppermute(value, axis, [(0, 1), (1, 0)])
    first = lax.axis_index(axis) == 0
    return jnp.stack([jnp.where(first, value, other), jnp.where(first, other, value)])


def meta_of(pattern, phase):
    own = jnp.concatenate([pattern, phase], axis=1)
    rows = jnp.concatenate([own, shift(own, -1), shift(own, -2)], axis=0)
    rows = both(both(rows, "core"), "yh").reshape(GROUP, 3, 2 * LEVELS)
    block = lax.axis_index(GROUP_AXES) * GROUP + jnp.arange(GROUP)
    distance = 2 ** jnp.arange(LEVELS)
    active = (rows[:, 0, :LEVELS] == 1) & (block[:, None] >= distance[None, :])
    phases = rows[:, :, LEVELS:].transpose(1, 0, 2)
    return jnp.concatenate([active.astype(jnp.int32).reshape(-1), phases.reshape(-1)])


def body(queries, keys, values, grad_out, pattern, phase):
    meta = meta_of(pattern, phase)
    width = queries.shape[1] // CHUNKS
    heads = width // (LINE * HD)
    results = []
    for chunk in range(CHUNKS):
        cols = slice(chunk * width, (chunk + 1) * width)
        x = jnp.stack([a[:, cols] for a in (keys, values, queries, grad_out)])
        x = x.reshape(4, HALF, LINE, heads, HD).transpose(2, 3, 0, 1, 4)
        y = lax.all_to_all(x, LINE_AXES, 0, 0, tiled=True)
        near, far = rows_to_send(meta, y)
        near, far = shift(near, 1), shift(far, 2)
        dq, acc, near, far = attention(meta, y, near, far)
        near, far = shift(near, -1), shift(far, -2)
        z = joined(meta, acc, dq, near, far)
        w = lax.all_to_all(z, LINE_AXES, 0, 0, tiled=True)
        results.append(w.transpose(2, 3, 0, 1, 4).reshape(3, HALF, width))
    return tuple(jnp.concatenate([r[i] for r in results], axis=1) for i in range(3))


def solution(mesh):
    sizes = (4, 4, 2, 2, 2)
    line = Mesh(mesh.devices.reshape(sizes), ("z", "x", "yh", "core", "yl"))
    ctx = ("z", "x", "yh", "core")
    tokens = P((*ctx, "yl"), None)
    return jax.shard_map(
        body,
        mesh=line,
        in_specs=(tokens,) * 4 + (P(ctx, None),) * 2,
        out_specs=(tokens,) * 3,
        check_vma=False,
    )
```

time: 825 us -> 291 us (0.35); the launches traced: 809 us -> 288 us
  waiting for transfers between devices: 336 us -> 61.5 us
  matrix products: 184 us -> 0 us
  local copies, waits for them, and re-layouts: 120 us -> 25.3 us
  Pallas kernels: 0 us -> 73.3 us
  other arithmetic: 47.8 us -> 10.1 us
  starting transfers between devices: 88.2 us -> 116 us
  blocking collectives: 22.1 us -> 0 us
    ppermute x16 -> x20, waiting for transfers between devices: 249 us -> 25.7 us  [the longest x18 19.5 us: shift(): return lax.ppermute(value, GROUP_AXES, pairs)]
    dot_general x200 -> x0, matrix products: 184 us -> none  [the longest x40 50.4 us: scores(): jnp.einsum('qhe,khe->hqk', grad_grp, value_tile, preferred_element_type=j...]
    pallas_call x0 -> x12, Pallas kernels: none -> 73.3 us  [the longest x4 54.5 us: attention(): pl.pallas_call(main_kernel, grid=(heads, GROUP), in_specs=[SMEM, y_spec(4...]
    all_to_all x6 -> x8, waiting for transfers between devices: 87.3 us -> 35.8 us  [the longest x4 27.6 us: body(): y = lax.all_to_all(x, LINE_AXES, 0, 0, tiled=True)]
    dynamic_slice x32 -> x0, local copies, waits for them, and re-layouts: 34.2 us -> none  [body(): lax.map(group_work, (split_heads(queries_here), split_heads(keys_here), s...]
    reshape x14 -> x1, local copies, waits for them, and re-layouts: 34.1 us -> 0.09 us  [meta_of(): phases.reshape(-1)]
    all_to_all x1 -> x0, blocking collectives: 22.1 us -> none  [body(): lax.all_to_all(values, 'head', split_axis=1, concat_axis=0, tiled=True)]
    ppermute x8 -> x0, local copies, waits for them, and re-layouts: 20.9 us -> none  [passed_along(): lax.ppermute(value, axis, [(source, source + steps) for source in range(i...]
  transfers between devices with their start and end apart: 22 -> 28, of which waited for: 12 -> 11; matrix products, arithmetic and copies ran while one was open for 10% -> 6% of each run, Pallas kernels for 0% -> 25%
where the time goes in v1:
time: 291 us; the launch traced here: 288 us
  starting transfers between devices  116 us (40%)
  Pallas kernels  73.3 us (25%)
  waiting for transfers between devices  61.5 us (21%)
  local copies, waits for them, and re-layouts  25.3 us (9%)
  other arithmetic  10.1 us (3%)
    ppermute x18, starting transfers between devices, shift(): return lax.ppermute(value, GROUP_AXES, pairs)  77.1 us
    pallas_call x4, Pallas kernels, attention(): pl.pallas_call(main_kernel, grid=(heads, GROUP), in_specs=[SMEM, y_spec(4...  54.5 us
    all_to_all x4, waiting for transfers between devices, body(): y = lax.all_to_all(x, LINE_AXES, 0, 0, tiled=True)  27.6 us
    ppermute x18, waiting for transfers between devices, shift(): return lax.ppermute(value, GROUP_AXES, pairs)  19.5 us
    all_to_all x4, starting transfers between devices, body(): w = lax.all_to_all(z, LINE_AXES, 0, 0, tiled=True)  18.8 us
    unnamed x60, local copies, waits for them, and re-layouts  17 us
    all_to_all x4, starting transfers between devices, body(): y = lax.all_to_all(x, LINE_AXES, 0, 0, tiled=True)  16.7 us
    pallas_call x4, Pallas kernels, joined(): pl.pallas_call(join_kernel, grid=(heads, GROUP), in_specs=[SMEM, pl.Block...  13.1 us
  transfers between devices with their start and end apart: 28, of which 11 were waited for; matrix products, arithmetic and copies ran while one was open for 6% of the time, Pallas kernels for 25%

profile of v1, /device:TPU:38, one launch (start us, length us, event | category | flops | bytes accessed | tf_op | source)
XLA Modules:
  0.0 287.7 jit_solution(10129399500634842735)
XLA Ops:
  11.8 4.5 %all-to-all-start = ((bf16[8,1,4,192,128]{4,3,2,1,0:T(8,128)(2,1)}), bf16[8,1,4,192,128]{4,3,2,1,0:T(8,128)(2,1)S(1)}, u32[]{:S(2)}, u32[]{:S(2)}) async-start(bf16[8,1,4,192,128]{4,3,2,1,0:T(8,128)(2,1)} %maximum_bitcast_fusion), calls=%async_computation | async-start | bytes 3145728 | tf_op jit(solution)/shard_map/all_to_all | solution.py:352
  18.1 19.8 %all-to-all-done.y_ref = bf16[8,1,4,192,128]{4,3,2,1,0:T(8,128)(2,1)S(1)} async-done(((bf16[8,1,4,192,128]{4,3,2,1,0:T(8,128)(2,1)}), bf16[8,1,4,192,128]{4,3,2,1,0:T(8,128)(2,1)S(1)}, u32[]{:S(2)}, u32[]{:S(2)}) %all-to-all-start) | async-done | bytes 1572896 | tf_op jit(solution)/shard_map/all_to_all | solution.py:352
  37.9 3.6 %all-to-all-start.4 = ((bf16[8,1,4,192,128]{4,3,2,1,0:T(8,128)(2,1)}), bf16[8,1,4,192,128]{4,3,2,1,0:T(8,128)(2,1)S(1)}, u32[]{:S(2)}, u32[]{:S(2)}) async-start(bf16[8,1,4,192,128]{4,3,2,1,0:T(8,128)(2,1)} %maximum_bitcast_fusion.2), calls=%async_computation.4 | async-start | bytes 3145728 | tf_op jit(solution)/shard_map/all_to_all | solution.py:352
  42.1 3.3 %collective-permute-start.1 = (s32[1,8]{1,0:T(1,128)}, s32[1,8]{1,0:T(1,128)S(1)}, u32[]{:S(2)}, u32[]{:S(2)}) collective-permute-start(s32[1,8]{1,0:T(1,128)} %pad_add_fusion.3), channel_id=1, source_target_pairs={{16,0},{24,8},{32,16},{40,24},{48,32},{56,40},{64,48},{72,56},{80,... | collective-permute-start | bytes 104 | tf_op jit(solution)/shard_map/ppermute | solution.py:323
  54.5 3.5 %collective-permute-start.3 = (s32[2,3,8]{2,1,0:T(4,128)S(1)}, s32[2,3,8]{2,1,0:T(4,128)S(1)}, u32[]{:S(2)}, u32[]{:S(2)}) collective-permute-start(s32[2,3,8]{2,1,0:T(4,128)S(1)} %pad_add_fusion.1), channel_id=1, source_target_pairs={{0,4},{4,0},{1,5},{5,1},{2,6},{6,2},{3,7},{7,3},{8,12},{12,8},{9,1... | collective-permute-start | bytes 584 | tf_op jit(solution)/shard_map/ppermute | solution.py:327
  58.0 5.1 %collective-permute-done.3 = s32[2,3,8]{2,1,0:T(4,128)S(1)} collective-permute-done((s32[2,3,8]{2,1,0:T(4,128)S(1)}, s32[2,3,8]{2,1,0:T(4,128)S(1)}, u32[]{:S(2)}, u32[]{:S(2)}) %collective-permute-start.3) | collective-permute-done | bytes 224 | tf_op jit(solution)/shard_map/ppermute | solution.py:327
  63.1 4.3 %all-to-all-start.6 = ((bf16[8,1,4,192,128]{4,3,2,1,0:T(8,128)(2,1)}), bf16[8,1,4,192,128]{4,3,2,1,0:T(8,128)(2,1)}, u32[]{:S(2)}, u32[]{:S(2)}) async-start(bf16[8,1,4,192,128]{4,3,2,1,0:T(8,128)(2,1)} %maximum_bitcast_fusion.3), calls=%async_computation.6 | async-start | bytes 3145728 | tf_op jit(solution)/shard_map/all_to_all | solution.py:352
  69.4 3.7 %collective-permute-start.12 = (bf16[1,864,256]{2,1,0:T(8,128)(2,1)}, bf16[1,864,256]{2,1,0:T(8,128)(2,1)}, u32[]{:S(2)}, u32[]{:S(2)}) collective-permute-start(bf16[1,864,256]{2,1,0:T(8,128)(2,1)} %get-tuple-element.39), channel_id=1, source_target_pairs={{0,8},{8,16},{16,24},{24,32},{32,40},{40,48},{48,56},{56,64},{64,7... | collective-permute-start | bytes 1327112 | tf_op jit(solution)/shard_map/ppermute | solution.py:323
  75.5 4.3 %collective-permute-start.13 = (bf16[1,192,256]{2,1,0:T(8,128)(2,1)S(1)}, bf16[1,192,256]{2,1,0:T(8,128)(2,1)S(1)}, u32[]{:S(2)}, u32[]{:S(2)}) collective-permute-start(bf16[1,192,256]{2,1,0:T(8,128)(2,1)S(1)} %get-tuple-element.40), channel_id=1, source_target_pairs={{0,16},{8,24},{16,32},{24,40},{32,48},{40,56},{48,64},{56,72},{64,... | collective-permute-start | bytes 294920 | tf_op jit(solution)/shard_map/ppermute | solution.py:323
  81.2 7.9 %all-to-all-done.6.y_ref = bf16[8,1,4,192,128]{4,3,2,1,0:T(8,128)(2,1)} async-done(((bf16[8,1,4,192,128]{4,3,2,1,0:T(8,128)(2,1)}), bf16[8,1,4,192,128]{4,3,2,1,0:T(8,128)(2,1)}, u32[]{:S(2)}, u32[]{:S(2)}) %all-to-all-start.6) | async-done | bytes 1572896 | tf_op jit(solution)/shard_map/all_to_all | solution.py:352
  89.0 4.3 %all-to-all-start.2 = ((bf16[8,1,4,192,128]{4,3,2,1,0:T(8,128)(2,1)}), bf16[8,1,4,192,128]{4,3,2,1,0:T(8,128)(2,1)}, u32[]{:S(2)}, u32[]{:S(2)}) async-start(bf16[8,1,4,192,128]{4,3,2,1,0:T(8,128)(2,1)} %maximum_bitcast_fusion.1), calls=%async_computation.2 | async-start | bytes 3145728 | tf_op jit(solution)/shard_map/all_to_all | solution.py:352
  93.4 13.5 %attention.6 = (bf16[1,4,384,128]{3,2,1,0:T(8,128)(2,1)S(1)}, f32[1,4,384,256]{3,2,1,0:T(8,128)S(1)}, bf16[1,864,256]{2,1,0:T(8,128)(2,1)S(1)}, bf16[1,192,256]{2,1,0:T(8,128)(2,1)S(1)}) custom-call(s32[64]{0:T(128)S(1)} %pad_add_fusion.4.meta, bf16[8,1,4,192,128]{4,3,2,1,0:T(8,128)(2,1)S(1)} %all-to-all-done.4.y_ref, ...), custom_call_target="tpu_custom_call" | custom-call | flops 8682209280 | bytes 5242880 | tf_op jit(solution)/shard_map/attention/pallas_call | solution.py:265
  111.3 5.2 %collective-permute-start.16 = (bf16[1,864,256]{2,1,0:T(8,128)(2,1)S(1)}, bf16[1,864,256]{2,1,0:T(8,128)(2,1)S(1)}, u32[]{:S(2)}, u32[]{:S(2)}) collective-permute-start(bf16[1,864,256]{2,1,0:T(8,128)(2,1)S(1)} %get-tuple-element.45), channel_id=1, source_target_pairs={{0,8},{8,16},{16,24},{24,32},{32,40},{40,48},{48,56},{56,64},{64,7... | collective-permute-start | bytes 1327112 | tf_op jit(solution)/shard_map/ppermute | solution.py:323
  118.4 6.3 %collective-permute-start.17 = (bf16[1,192,256]{2,1,0:T(8,128)(2,1)S(1)}, bf16[1,192,256]{2,1,0:T(8,128)(2,1)S(1)}, u32[]{:S(2)}, u32[]{:S(2)}) collective-permute-start(bf16[1,192,256]{2,1,0:T(8,128)(2,1)S(1)} %get-tuple-element.46), channel_id=1, source_target_pairs={{0,16},{8,24},{16,32},{24,40},{32,48},{40,56},{48,64},{56,72},{64,... | collective-permute-start | bytes 294920 | tf_op jit(solution)/shard_map/ppermute | solution.py:323
  128.8 4.6 %all-to-all-start.5 = ((bf16[8,1,3,192,128]{4,3,2,1,0:T(8,128)(2,1)}), bf16[8,1,3,192,128]{4,3,2,1,0:T(8,128)(2,1)}, u32[]{:S(2)}, u32[]{:S(2)}) async-start(bf16[8,1,3,192,128]{4,3,2,1,0:T(8,128)(2,1)} %joined.6), calls=%async_computation.5 | async-start | bytes 2359296 | tf_op jit(solution)/shard_map/all_to_all | solution.py:358
  133.4 13.9 %attention.7 = (bf16[1,4,384,128]{3,2,1,0:T(8,128)(2,1)S(1)}, f32[1,4,384,256]{3,2,1,0:T(8,128)S(1)}, bf16[1,864,256]{2,1,0:T(8,128)(2,1)S(1)}, bf16[1,192,256]{2,1,0:T(8,128)(2,1)S(1)}) custom-call(s32[64]{0:T(128)S(1)} %pad_add_fusion.4.meta, bf16[8,1,4,192,128]{4,3,2,1,0:T(8,128)(2,1)} %all-to-all-done.6.y_ref, ...), custom_call_target="tpu_custom_call" | custom-call | flops 8682209280 | bytes 5242880 | tf_op jit(solution)/shard_map/attention/pallas_call | solution.py:265
  147.4 6.9 %collective-permute-start.18 = (bf16[1,864,256]{2,1,0:T(8,128)(2,1)S(1)}, bf16[1,864,256]{2,1,0:T(8,128)(2,1)S(1)}, u32[]{:S(2)}, u32[]{:S(2)}) collective-permute-start(bf16[1,864,256]{2,1,0:T(8,128)(2,1)S(1)} %get-tuple-element.49), channel_id=1, source_target_pairs={{8,0},{16,8},{24,16},{32,24},{40,32},{48,40},{56,48},{64,56},{72,6... | collective-permute-start | bytes 1327112 | tf_op jit(solution)/shard_map/ppermute | solution.py:323
  155.8 3.9 %collective-permute-start.8 = (bf16[1,864,256]{2,1,0:T(8,128)(2,1)S(1)}, bf16[1,864,256]{2,1,0:T(8,128)(2,1)S(1)}, u32[]{:S(2)}, u32[]{:S(2)}) collective-permute-start(bf16[1,864,256]{2,1,0:T(8,128)(2,1)S(1)} %get-tuple-element.33), channel_id=1, source_target_pairs={{0,8},{8,16},{16,24},{24,32},{32,40},{40,48},{48,56},{56,64},{64,7... | collective-permute-start | bytes 1327112 | tf_op jit(solution)/shard_map/ppermute | solution.py:323
  161.7 6.2 %collective-permute-start.9 = (bf16[1,192,256]{2,1,0:T(8,128)(2,1)S(1)}, bf16[1,192,256]{2,1,0:T(8,128)(2,1)S(1)}, u32[]{:S(2)}, u32[]{:S(2)}) collective-permute-start(bf16[1,192,256]{2,1,0:T(8,128)(2,1)S(1)} %get-tuple-element.34), channel_id=1, source_target_pairs={{0,16},{8,24},{16,32},{24,40},{32,48},{40,56},{48,64},{56,72},{64,... | collective-permute-start | bytes 294920 | tf_op jit(solution)/shard_map/ppermute | solution.py:323
  174.0 4.8 %all-to-all-start.7 = ((bf16[8,1,3,192,128]{4,3,2,1,0:T(8,128)(2,1)}), bf16[8,1,3,192,128]{4,3,2,1,0:T(8,128)(2,1)}, u32[]{:S(2)}, u32[]{:S(2)}) async-start(bf16[8,1,3,192,128]{4,3,2,1,0:T(8,128)(2,1)} %joined.7), calls=%async_computation.7 | async-start | bytes 2359296 | tf_op jit(solution)/shard_map/all_to_all | solution.py:358
  178.9 13.9 %attention.5 = (bf16[1,4,384,128]{3,2,1,0:T(8,128)(2,1)S(1)}, f32[1,4,384,256]{3,2,1,0:T(8,128)S(1)}, bf16[1,864,256]{2,1,0:T(8,128)(2,1)S(1)}, bf16[1,192,256]{2,1,0:T(8,128)(2,1)S(1)}) custom-call(s32[64]{0:T(128)S(1)} %pad_add_fusion.4.meta, bf16[8,1,4,192,128]{4,3,2,1,0:T(8,128)(2,1)} %all-to-all-done.2.y_ref, ...), custom_call_target="tpu_custom_call" | custom-call | flops 8682209280 | bytes 5242880 | tf_op jit(solution)/shard_map/attention/pallas_call | solution.py:265
  192.8 6.8 %collective-permute-start.10 = (bf16[1,864,256]{2,1,0:T(8,128)(2,1)S(1)}, bf16[1,864,256]{2,1,0:T(8,128)(2,1)S(1)}, u32[]{:S(2)}, u32[]{:S(2)}) collective-permute-start(bf16[1,864,256]{2,1,0:T(8,128)(2,1)S(1)} %get-tuple-element.37), channel_id=1, source_target_pairs={{8,0},{16,8},{24,16},{32,24},{40,32},{48,40},{56,48},{64,56},{72,6... | collective-permute-start | bytes 1327112 | tf_op jit(solution)/shard_map/ppermute | solution.py:323
  206.5 5.5 %collective-permute-start.5 = (bf16[1,192,256]{2,1,0:T(8,128)(2,1)S(1)}, bf16[1,192,256]{2,1,0:T(8,128)(2,1)S(1)}, u32[]{:S(2)}, u32[]{:S(2)}) collective-permute-start(bf16[1,192,256]{2,1,0:T(8,128)(2,1)S(1)} %get-tuple-element.28), channel_id=1, source_target_pairs={{0,16},{8,24},{16,32},{24,40},{32,48},{40,56},{48,64},{56,72},{64,... | collective-permute-start | bytes 294920 | tf_op jit(solution)/shard_map/ppermute | solution.py:323
  212.0 3.3 %collective-permute-done.11.rfar_ref = bf16[1,192,256]{2,1,0:T(8,128)(2,1)S(1)} collective-permute-done((bf16[1,192,256]{2,1,0:T(8,128)(2,1)S(1)}, bf16[1,192,256]{2,1,0:T(8,128)(2,1)S(1)}, u32[]{:S(2)}, u32[]{:S(2)}) %collective-permute-start.11) | collective-permute-done | bytes 98336 | tf_op jit(solution)/shard_map/ppermute | solution.py:323
  215.3 3.3 %joined.5 = bf16[8,1,3,192,128]{4,3,2,1,0:T(8,128)(2,1)} custom-call(s32[64]{0:T(128)S(1)} %pad_add_fusion.4.meta, f32[1,4,384,256]{3,2,1,0:T(8,128)S(1)} %get-tuple-element.35.acc_ref, bf16[1,4,384,128]{3,2,1,0:T(8,128)(2,1)S(1)} %get-tuple-element.36.dq_ref, bf16[1,864,256]{2,1,0:T(8,128)(2,1)S(1)} %collective-permute-done.10.rnext_ref, ...), custom_call_target="tpu_custom_call" | custom-call | flops 268435456 | bytes 4194304 | tf_op jit(solution)/shard_map/joined/pallas_call | solution.py:301
  218.6 4.9 %all-to-all-start.3 = ((bf16[8,1,3,192,128]{4,3,2,1,0:T(8,128)(2,1)}), bf16[8,1,3,192,128]{4,3,2,1,0:T(8,128)(2,1)}, u32[]{:S(2)}, u32[]{:S(2)}) async-start(bf16[8,1,3,192,128]{4,3,2,1,0:T(8,128)(2,1)} %joined.5), calls=%async_computation.3 | async-start | bytes 2359296 | tf_op jit(solution)/shard_map/all_to_all | solution.py:358
  223.5 13.1 %attention.4 = (bf16[1,4,384,128]{3,2,1,0:T(8,128)(2,1)S(1)}, f32[1,4,384,256]{3,2,1,0:T(8,128)S(1)}, bf16[1,864,256]{2,1,0:T(8,128)(2,1)S(1)}, bf16[1,192,256]{2,1,0:T(8,128)(2,1)S(1)}) custom-call(s32[64]{0:T(128)S(1)} %pad_add_fusion.4.meta, bf16[8,1,4,192,128]{4,3,2,1,0:T(8,128)(2,1)S(1)} %all-to-all-done.y_ref, ...), custom_call_target="tpu_custom_call" | custom-call | flops 8682209280 | bytes 5242880 | tf_op jit(solution)/shard_map/attention/pallas_call | solution.py:265
  236.5 6.2 %collective-permute-start.6 = (bf16[1,864,256]{2,1,0:T(8,128)(2,1)S(1)}, bf16[1,864,256]{2,1,0:T(8,128)(2,1)S(1)}, u32[]{:S(2)}, u32[]{:S(2)}) collective-permute-start(bf16[1,864,256]{2,1,0:T(8,128)(2,1)S(1)} %get-tuple-element.31), channel_id=1, source_target_pairs={{8,0},{16,8},{24,16},{32,24},{40,32},{48,40},{56,48},{64,56},{72,6... | collective-permute-start | bytes 1327112 | tf_op jit(solution)/shard_map/ppermute | solution.py:323
  242.7 4.2 %collective-permute-start.7 = (bf16[1,192,256]{2,1,0:T(8,128)(2,1)S(1)}, bf16[1,192,256]{2,1,0:T(8,128)(2,1)S(1)}, u32[]{:S(2)}, u32[]{:S(2)}) collective-permute-start(bf16[1,192,256]{2,1,0:T(8,128)(2,1)S(1)} %get-tuple-element.32), channel_id=1, source_target_pairs={{16,0},{24,8},{32,16},{40,24},{48,32},{56,40},{64,48},{72,56},{80,... | collective-permute-start | bytes 294920 | tf_op jit(solution)/shard_map/ppermute | solution.py:323
  246.9 10.4 %collective-permute-done.7.rfar_ref = bf16[1,192,256]{2,1,0:T(8,128)(2,1)S(1)} collective-permute-done((bf16[1,192,256]{2,1,0:T(8,128)(2,1)S(1)}, bf16[1,192,256]{2,1,0:T(8,128)(2,1)S(1)}, u32[]{:S(2)}, u32[]{:S(2)}) %collective-permute-start.7) | collective-permute-done | bytes 98336 | tf_op jit(solution)/shard_map/ppermute | solution.py:323
  260.6 4.4 %all-to-all-start.1 = ((bf16[8,1,3,192,128]{4,3,2,1,0:T(8,128)(2,1)}), bf16[8,1,3,192,128]{4,3,2,1,0:T(8,128)(2,1)S(1)}, u32[]{:S(2)}, u32[]{:S(2)}) async-start(bf16[8,1,3,192,128]{4,3,2,1,0:T(8,128)(2,1)} %joined.4), calls=%async_computation.1 | async-start | bytes 2359296 | tf_op jit(solution)/shard_map/all_to_all | solution.py:358
  274.3 8.2 %all-to-all-done.1 = bf16[8,1,3,192,128]{4,3,2,1,0:T(8,128)(2,1)S(1)} async-done(((bf16[8,1,3,192,128]{4,3,2,1,0:T(8,128)(2,1)}), bf16[8,1,3,192,128]{4,3,2,1,0:T(8,128)(2,1)S(1)}, u32[]{:S(2)}, u32[]{:S(2)}) %all-to-all-start.1) | async-done | bytes 1179680 | tf_op jit(solution)/shard_map/all_to_all | solution.py:358
  (152 shorter events, 72.4 us)
Async XLA Ops:
  2.9 1.4 copy-start
  11.8 26.1 %all-to-all-start = ((bf16[8,1,4,192,128]{4,3,2,1,0:T(8,128)(2,1)}), bf16[8,1,4,192,128]{4,3,2,1,0:T(8,128)(2,1)S(1)}, u32[]{:S(2)}, u32[]{:S(2)}) async-start(bf16[8,1,4,192,128]{4,3,2,1,0:T(8,128)(2,1)} %maximum_bitcast_fusion), calls=%async_computation | async-start | bytes 3145728 | tf_op jit(solution)/shard_map/all_to_all | solution.py:352
  18.1 23.4 %copy-start.12 = (s32[1,4]{1,0:T(1,128)S(1)}, s32[1,4]{1,0:T(1,128)}, u32[]{:S(2)}) copy-start(s32[1,4]{1,0:T(1,128)} %param.11) | copy-start | bytes 52
  18.1 23.4 %copy-start.13 = (s32[1,4]{1,0:T(1,128)S(1)}, s32[1,4]{1,0:T(1,128)}, u32[]{:S(2)}) copy-start(s32[1,4]{1,0:T(1,128)} %param.10) | copy-start | bytes 52
  37.9 25.2 %all-to-all-start.4 = ((bf16[8,1,4,192,128]{4,3,2,1,0:T(8,128)(2,1)}), bf16[8,1,4,192,128]{4,3,2,1,0:T(8,128)(2,1)S(1)}, u32[]{:S(2)}, u32[]{:S(2)}) async-start(bf16[8,1,4,192,128]{4,3,2,1,0:T(8,128)(2,1)} %maximum_bitcast_fusion.2), calls=%async_computation.4 | async-start | bytes 3145728 | tf_op jit(solution)/shard_map/all_to_all | solution.py:352
  42.1 8.8 %collective-permute-start.1 = (s32[1,8]{1,0:T(1,128)}, s32[1,8]{1,0:T(1,128)S(1)}, u32[]{:S(2)}, u32[]{:S(2)}) collective-permute-start(s32[1,8]{1,0:T(1,128)} %pad_add_fusion.3), channel_id=1, source_target_pairs={{16,0},{24,8},{32,16},{40,24},{48,32},{56,40},{64,48},{72,56},{80,... | collective-permute-start | bytes 104 | tf_op jit(solution)/shard_map/ppermute | solution.py:323
  45.4 7.8 %collective-permute-start = (s32[1,8]{1,0:T(1,128)}, s32[1,8]{1,0:T(1,128)S(1)}, u32[]{:S(2)}, u32[]{:S(2)}) collective-permute-start(s32[1,8]{1,0:T(1,128)} %pad_add_fusion.3), channel_id=1, source_target_pairs={{8,0},{16,8},{24,16},{32,24},{40,32},{48,40},{56,48},{64,56},{72,6... | collective-permute-start | bytes 104 | tf_op jit(solution)/shard_map/ppermute | solution.py:323
  53.2 1.2 collective-permute-start.2
  54.5 8.6 %collective-permute-start.3 = (s32[2,3,8]{2,1,0:T(4,128)S(1)}, s32[2,3,8]{2,1,0:T(4,128)S(1)}, u32[]{:S(2)}, u32[]{:S(2)}) collective-permute-start(s32[2,3,8]{2,1,0:T(4,128)S(1)} %pad_add_fusion.1), channel_id=1, source_target_pairs={{0,4},{4,0},{1,5},{5,1},{2,6},{6,2},{3,7},{7,3},{8,12},{12,8},{9,1... | collective-permute-start | bytes 584 | tf_op jit(solution)/shard_map/ppermute | solution.py:327
  63.1 25.9 %all-to-all-start.6 = ((bf16[8,1,4,192,128]{4,3,2,1,0:T(8,128)(2,1)}), bf16[8,1,4,192,128]{4,3,2,1,0:T(8,128)(2,1)}, u32[]{:S(2)}, u32[]{:S(2)}) async-start(bf16[8,1,4,192,128]{4,3,2,1,0:T(8,128)(2,1)} %maximum_bitcast_fusion.3), calls=%async_computation.6 | async-start | bytes 3145728 | tf_op jit(solution)/shard_map/all_to_all | solution.py:352
  67.8 6.6 %copy-start.3 = (bf16[24,8,8,128]{3,1,2,0:T(8,128)(2,1)S(1)}, bf16[24,8,8,128]{3,1,2,0:T(8,128)(2,1)}, u32[]{:S(2)}) copy-start(bf16[24,8,8,128]{3,1,2,0:T(8,128)(2,1)} %get-tuple-element.52) | copy-start | bytes 1179652
  69.4 23.9 %collective-permute-start.12 = (bf16[1,864,256]{2,1,0:T(8,128)(2,1)}, bf16[1,864,256]{2,1,0:T(8,128)(2,1)}, u32[]{:S(2)}, u32[]{:S(2)}) collective-permute-start(bf16[1,864,256]{2,1,0:T(8,128)(2,1)} %get-tuple-element.39), channel_id=1, source_target_pairs={{0,8},{8,16},{16,24},{24,32},{32,40},{40,48},{48,56},{56,64},{64,7... | collective-permute-start | bytes 1327112 | tf_op jit(solution)/shard_map/ppermute | solution.py:323
  75.5 17.8 %collective-permute-start.13 = (bf16[1,192,256]{2,1,0:T(8,128)(2,1)S(1)}, bf16[1,192,256]{2,1,0:T(8,128)(2,1)S(1)}, u32[]{:S(2)}, u32[]{:S(2)}) collective-permute-start(bf16[1,192,256]{2,1,0:T(8,128)(2,1)S(1)} %get-tuple-element.40), channel_id=1, source_target_pairs={{0,16},{8,24},{16,32},{24,40},{32,48},{40,56},{48,64},{56,72},{64,... | collective-permute-start | bytes 294920 | tf_op jit(solution)/shard_map/ppermute | solution.py:323
  89.0 39.7 %all-to-all-start.2 = ((bf16[8,1,4,192,128]{4,3,2,1,0:T(8,128)(2,1)}), bf16[8,1,4,192,128]{4,3,2,1,0:T(8,128)(2,1)}, u32[]{:S(2)}, u32[]{:S(2)}) async-start(bf16[8,1,4,192,128]{4,3,2,1,0:T(8,128)(2,1)} %maximum_bitcast_fusion.1), calls=%async_computation.2 | async-start | bytes 3145728 | tf_op jit(solution)/shard_map/all_to_all | solution.py:352
  106.9 18.6 %collective-permute-start.14 = (bf16[1,864,256]{2,1,0:T(8,128)(2,1)S(1)}, bf16[1,864,256]{2,1,0:T(8,128)(2,1)S(1)}, u32[]{:S(2)}, u32[]{:S(2)}) collective-permute-start(bf16[1,864,256]{2,1,0:T(8,128)(2,1)S(1)} %get-tuple-element.43), channel_id=1, source_target_pairs={{8,0},{16,8},{24,16},{32,24},{40,32},{48,40},{56,48},{64,56},{72,6... | collective-permute-start | bytes 1327112 | tf_op jit(solution)/shard_map/ppermute | solution.py:323
  111.3 22.2 %collective-permute-start.16 = (bf16[1,864,256]{2,1,0:T(8,128)(2,1)S(1)}, bf16[1,864,256]{2,1,0:T(8,128)(2,1)S(1)}, u32[]{:S(2)}, u32[]{:S(2)}) collective-permute-start(bf16[1,864,256]{2,1,0:T(8,128)(2,1)S(1)} %get-tuple-element.45), channel_id=1, source_target_pairs={{0,8},{8,16},{16,24},{24,32},{32,40},{40,48},{48,56},{56,64},{64,7... | collective-permute-start | bytes 1327112 | tf_op jit(solution)/shard_map/ppermute | solution.py:323
  116.5 8.9 %collective-permute-start.15 = (bf16[1,192,256]{2,1,0:T(8,128)(2,1)S(1)}, bf16[1,192,256]{2,1,0:T(8,128)(2,1)S(1)}, u32[]{:S(2)}, u32[]{:S(2)}) collective-permute-start(bf16[1,192,256]{2,1,0:T(8,128)(2,1)S(1)} %get-tuple-element.44), channel_id=1, source_target_pairs={{16,0},{24,8},{32,16},{40,24},{48,32},{56,40},{64,48},{72,56},{80,... | collective-permute-start | bytes 294920 | tf_op jit(solution)/shard_map/ppermute | solution.py:323
  118.4 15.0 %collective-permute-start.17 = (bf16[1,192,256]{2,1,0:T(8,128)(2,1)S(1)}, bf16[1,192,256]{2,1,0:T(8,128)(2,1)S(1)}, u32[]{:S(2)}, u32[]{:S(2)}) collective-permute-start(bf16[1,192,256]{2,1,0:T(8,128)(2,1)S(1)} %get-tuple-element.46), channel_id=1, source_target_pairs={{0,16},{8,24},{16,32},{24,40},{32,48},{40,56},{48,64},{56,72},{64,... | collective-permute-start | bytes 294920 | tf_op jit(solution)/shard_map/ppermute | solution.py:323
  128.8 45.2 %all-to-all-start.5 = ((bf16[8,1,3,192,128]{4,3,2,1,0:T(8,128)(2,1)}), bf16[8,1,3,192,128]{4,3,2,1,0:T(8,128)(2,1)}, u32[]{:S(2)}, u32[]{:S(2)}) async-start(bf16[8,1,3,192,128]{4,3,2,1,0:T(8,128)(2,1)} %joined.6), calls=%async_computation.5 | async-start | bytes 2359296 | tf_op jit(solution)/shard_map/all_to_all | solution.py:358
  147.4 23.3 %collective-permute-start.18 = (bf16[1,864,256]{2,1,0:T(8,128)(2,1)S(1)}, bf16[1,864,256]{2,1,0:T(8,128)(2,1)S(1)}, u32[]{:S(2)}, u32[]{:S(2)}) collective-permute-start(bf16[1,864,256]{2,1,0:T(8,128)(2,1)S(1)} %get-tuple-element.49), channel_id=1, source_target_pairs={{8,0},{16,8},{24,16},{32,24},{40,32},{48,40},{56,48},{64,56},{72,6... | collective-permute-start | bytes 1327112 | tf_op jit(solution)/shard_map/ppermute | solution.py:323
  155.8 23.0 %collective-permute-start.8 = (bf16[1,864,256]{2,1,0:T(8,128)(2,1)S(1)}, bf16[1,864,256]{2,1,0:T(8,128)(2,1)S(1)}, u32[]{:S(2)}, u32[]{:S(2)}) collective-permute-start(bf16[1,864,256]{2,1,0:T(8,128)(2,1)S(1)} %get-tuple-element.33), channel_id=1, source_target_pairs={{0,8},{8,16},{16,24},{24,32},{32,40},{40,48},{48,56},{56,64},{64,7... | collective-permute-start | bytes 1327112 | tf_op jit(solution)/shard_map/ppermute | solution.py:323
  159.7 11.0 %collective-permute-start.19 = (bf16[1,192,256]{2,1,0:T(8,128)(2,1)S(1)}, bf16[1,192,256]{2,1,0:T(8,128)(2,1)S(1)}, u32[]{:S(2)}, u32[]{:S(2)}) collective-permute-start(bf16[1,192,256]{2,1,0:T(8,128)(2,1)S(1)} %get-tuple-element.50), channel_id=1, source_target_pairs={{16,0},{24,8},{32,16},{40,24},{48,32},{56,40},{64,48},{72,56},{80,... | collective-permute-start | bytes 294920 | tf_op jit(solution)/shard_map/ppermute | solution.py:323
  161.7 17.1 %collective-permute-start.9 = (bf16[1,192,256]{2,1,0:T(8,128)(2,1)S(1)}, bf16[1,192,256]{2,1,0:T(8,128)(2,1)S(1)}, u32[]{:S(2)}, u32[]{:S(2)}) collective-permute-start(bf16[1,192,256]{2,1,0:T(8,128)(2,1)S(1)} %get-tuple-element.34), channel_id=1, source_target_pairs={{0,16},{8,24},{16,32},{24,40},{32,48},{40,56},{48,64},{56,72},{64,... | collective-permute-start | bytes 294920 | tf_op jit(solution)/shard_map/ppermute | solution.py:323
  174.0 44.6 %all-to-all-start.7 = ((bf16[8,1,3,192,128]{4,3,2,1,0:T(8,128)(2,1)}), bf16[8,1,3,192,128]{4,3,2,1,0:T(8,128)(2,1)}, u32[]{:S(2)}, u32[]{:S(2)}) async-start(bf16[8,1,3,192,128]{4,3,2,1,0:T(8,128)(2,1)} %joined.7), calls=%async_computation.7 | async-start | bytes 2359296 | tf_op jit(solution)/shard_map/all_to_all | solution.py:358
  192.8 22.5 %collective-permute-start.10 = (bf16[1,864,256]{2,1,0:T(8,128)(2,1)S(1)}, bf16[1,864,256]{2,1,0:T(8,128)(2,1)S(1)}, u32[]{:S(2)}, u32[]{:S(2)}) collective-permute-start(bf16[1,864,256]{2,1,0:T(8,128)(2,1)S(1)} %get-tuple-element.37), channel_id=1, source_target_pairs={{8,0},{16,8},{24,16},{32,24},{40,32},{48,40},{56,48},{64,56},{72,6... | collective-permute-start | bytes 1327112 | tf_op jit(solution)/shard_map/ppermute | solution.py:323
  200.6 22.9 %collective-permute-start.4 = (bf16[1,864,256]{2,1,0:T(8,128)(2,1)S(1)}, bf16[1,864,256]{2,1,0:T(8,128)(2,1)S(1)}, u32[]{:S(2)}, u32[]{:S(2)}) collective-permute-start(bf16[1,864,256]{2,1,0:T(8,128)(2,1)S(1)} %get-tuple-element.27), channel_id=1, source_target_pairs={{0,8},{8,16},{16,24},{24,32},{32,40},{40,48},{48,56},{56,64},{64,7... | collective-permute-start | bytes 1327112 | tf_op jit(solution)/shard_map/ppermute | solution.py:323
  203.7 11.6 %collective-permute-start.11 = (bf16[1,192,256]{2,1,0:T(8,128)(2,1)S(1)}, bf16[1,192,256]{2,1,0:T(8,128)(2,1)S(1)}, u32[]{:S(2)}, u32[]{:S(2)}) collective-permute-start(bf16[1,192,256]{2,1,0:T(8,128)(2,1)S(1)} %get-tuple-element.38), channel_id=1, source_target_pairs={{16,0},{24,8},{32,16},{40,24},{48,32},{56,40},{64,48},{72,56},{80,... | collective-permute-start | bytes 294920 | tf_op jit(solution)/shard_map/ppermute | solution.py:323
  206.5 17.0 %collective-permute-start.5 = (bf16[1,192,256]{2,1,0:T(8,128)(2,1)S(1)}, bf16[1,192,256]{2,1,0:T(8,128)(2,1)S(1)}, u32[]{:S(2)}, u32[]{:S(2)}) collective-permute-start(bf16[1,192,256]{2,1,0:T(8,128)(2,1)S(1)} %get-tuple-element.28), channel_id=1, source_target_pairs={{0,16},{8,24},{16,32},{24,40},{32,48},{40,56},{48,64},{56,72},{64,... | collective-permute-start | bytes 294920 | tf_op jit(solution)/shard_map/ppermute | solution.py:323
  218.6 42.0 %all-to-all-start.3 = ((bf16[8,1,3,192,128]{4,3,2,1,0:T(8,128)(2,1)}), bf16[8,1,3,192,128]{4,3,2,1,0:T(8,128)(2,1)}, u32[]{:S(2)}, u32[]{:S(2)}) async-start(bf16[8,1,3,192,128]{4,3,2,1,0:T(8,128)(2,1)} %joined.5), calls=%async_computation.3 | async-start | bytes 2359296 | tf_op jit(solution)/shard_map/all_to_all | solution.py:358
  236.5 20.8 %collective-permute-start.6 = (bf16[1,864,256]{2,1,0:T(8,128)(2,1)S(1)}, bf16[1,864,256]{2,1,0:T(8,128)(2,1)S(1)}, u32[]{:S(2)}, u32[]{:S(2)}) collective-permute-start(bf16[1,864,256]{2,1,0:T(8,128)(2,1)S(1)} %get-tuple-element.31), channel_id=1, source_target_pairs={{8,0},{16,8},{24,16},{32,24},{40,32},{48,40},{56,48},{64,56},{72,6... | collective-permute-start | bytes 1327112 | tf_op jit(solution)/shard_map/ppermute | solution.py:323
  242.7 14.6 %collective-permute-start.7 = (bf16[1,192,256]{2,1,0:T(8,128)(2,1)S(1)}, bf16[1,192,256]{2,1,0:T(8,128)(2,1)S(1)}, u32[]{:S(2)}, u32[]{:S(2)}) collective-permute-start(bf16[1,192,256]{2,1,0:T(8,128)(2,1)S(1)} %get-tuple-element.32), channel_id=1, source_target_pairs={{16,0},{24,8},{32,16},{40,24},{48,32},{56,40},{64,48},{72,56},{80,... | collective-permute-start | bytes 294920 | tf_op jit(solution)/shard_map/ppermute | solution.py:323
  260.6 21.9 %all-to-all-start.1 = ((bf16[8,1,3,192,128]{4,3,2,1,0:T(8,128)(2,1)}), bf16[8,1,3,192,128]{4,3,2,1,0:T(8,128)(2,1)S(1)}, u32[]{:S(2)}, u32[]{:S(2)}) async-start(bf16[8,1,3,192,128]{4,3,2,1,0:T(8,128)(2,1)} %joined.4), calls=%async_computation.1 | async-start | bytes 2359296 | tf_op jit(solution)/shard_map/all_to_all | solution.py:358
  (10 other events, 11.8 us)

commit v2 on v1

v2 whole, which is shorter than its diff:
```python
import functools
import math

import jax
import jax.numpy as jnp
from jax import lax
from jax.experimental import pallas as pl
from jax.experimental.pallas import tpu as pltpu
from jax.sharding import Mesh, PartitionSpec as P

HD = 128
BLK = 384
HALF = 192
LEVELS = 4
LINE = 8
GROUP = 4
HEADS = 4
PAIR = 2
NEG = -1e30
SCALE = HD**-0.5
LOG2E = math.log2(math.e)
NEXT_L1 = BLK
NEXT_L2 = BLK + BLK // 2
NEXT_ROWS = NEXT_L2 + 3 * (BLK // 4)
FAR_ROWS = GROUP * (BLK // 8)
KEYS = BLK + BLK + BLK // 2 + BLK // 4 + BLK // 8
SEG = [0, BLK, 2 * BLK, 2 * BLK + BLK // 2, 2 * BLK + BLK // 2 + BLK // 4, KEYS]
OWN, NXT, AFT = 16, 32, 48
LINE_AXES = ("yh", "core", "yl")
GROUP_AXES = ("z", "x")
F32 = jnp.float32
BF16 = jnp.bfloat16


def dot(a, b, dims):
    return lax.dot_general(a, b, ((dims[0], dims[1]), ((), ())), preferred_element_type=F32)


def picker(stride, phase):
    rows = BLK // stride
    row = lax.broadcasted_iota(jnp.int32, (rows, BLK), 0)
    col = lax.broadcasted_iota(jnp.int32, (rows, BLK), 1)
    return jnp.where(col == row * stride + (phase & (stride - 1)), 1.0, 0.0).astype(BF16)


def spreader(stride, phase):
    cols = BLK // stride
    row = lax.broadcasted_iota(jnp.int32, (BLK, cols), 0)
    col = lax.broadcasted_iota(jnp.int32, (BLK, cols), 1)
    return jnp.where(row == col * stride + (phase & (stride - 1)), 1.0, 0.0).astype(BF16)


def pick(stride, phase, rows):
    return dot(picker(stride, phase), rows, ((1,), (0,))).astype(BF16)


def spread(stride, phase, rows):
    return dot(spreader(stride, phase), rows, ((1,), (0,)))


def kv_of(y_ref, block):
    at = slice(2 * block, 2 * block + 2)
    return jnp.concatenate([y_ref[at, 0].reshape(BLK, HD), y_ref[at, 1].reshape(BLK, HD)], axis=1)


def send_kernel(pair, meta, y_ref, *refs):
    outs = refs[-PAIR - (pair == 0) :]
    for i in range(PAIR):
        h = pair * PAIR + i
        y, near_ref = y_ref.at[:, :, :, h * HD : (h + 1) * HD], outs[i]
        near_ref[0, 0:BLK] = kv_of(y, 3)
        near_ref[0, NEXT_L1:NEXT_L2] = pick(2, meta[NXT + 1], kv_of(y, 2))
        for b in range(3):
            lo = NEXT_L2 + b * 96
            near_ref[0, lo : lo + 96] = pick(4, meta[NXT + 4 * b + 2], kv_of(y, b))
    if pair == 0:
        for h in range(HEADS):
            y = y_ref.at[:, :, :, h * HD : (h + 1) * HD]
            for b in range(GROUP):
                outs[PAIR][h, 48 * b : 48 * b + 48] = pick(8, meta[AFT + 4 * b + 3], kv_of(y, b))


def emit(pieces):
    for piece in pieces:
        piece()


def main_kernel(meta, y_ref, w_ref, next_ref, far_ref, *refs):
    dq_ref, acc_ref, rnext_ref, rfar_ref, kvs, ss, dps, ps, dss, prev = refs[-10:]
    row_tiles = [(lo, min(lo + 128, KEYS)) for lo in range(0, KEYS, 128)]

    def q_of(b):
        return w_ref[2 * b : 2 * b + 2, 0].reshape(BLK, HD)

    def g_of(b):
        return w_ref[2 * b : 2 * b + 2, 1].reshape(BLK, HD)

    def gather(b):
        kv = kvs.at[b % 2]
        last = [None, lambda: next_ref[0, 0:BLK]] + [functools.partial(kv_of, y_ref, i) for i in range(b + 1)]
        own, one, two = last[b + 2], last[b + 1], last[b]
        kv[0:BLK] = own()
        kv[SEG[1] : SEG[2]] = one()
        if two is None:
            kv[SEG[2] : SEG[3]] = next_ref[0, NEXT_L1:NEXT_L2]
        else:
            kv[SEG[2] : SEG[3]] = pick(2, meta[OWN + 4 * b + 1], two())
        if b < 3:
            kv[SEG[3] : SEG[4]] = next_ref[0, NEXT_L2 + 96 * b : NEXT_L2 + 96 * b + 96]
        else:
            kv[SEG[3] : SEG[4]] = pick(4, meta[OWN + 4 * b + 2], next_ref[0, 0:BLK])
        kv[SEG[4] : SEG[5]] = far_ref[0, 48 * b : 48 * b + 48]

    def products(b):
        kv, s, dp = kvs.at[b % 2], ss.at[b % 2], dps.at[b % 2]
        yield lambda: gather(b)

        def tile(lo, hi, which):
            if which:
                dp[lo:hi] = dot(kv[lo:hi, HD:], g_of(b), ((1,), (1,)))
            else:
                s[lo:hi] = dot(kv[lo:hi, :HD], q_of(b), ((1,), (1,)))

        for which in (0, 1):
            for lo, hi in row_tiles:
                yield functools.partial(tile, lo, hi, which)

    def softmax(b):
        s, dp, p, ds = ss.at[b % 2], dps.at[b % 2], ps.at[b % 2], dss.at[b % 2]
        biases = [None] + [jnp.where(meta[4 * b + k] == 1, 0.0, NEG).astype(F32) for k in range(LEVELS)]
        row = lax.broadcasted_iota(jnp.int32, (128, 128), 0)
        col = lax.broadcasted_iota(jnp.int32, (128, 128), 1)
        upper = row <= col
        c = SCALE * LOG2E
        for i in range(3):
            lanes = slice(128 * i, 128 * i + 128)
            tiles = [(128 * j, 128 * j + 128, 0) for j in range(i + 1)]
            tiles += [(BLK + 128 * j, BLK + 128 * j + 128, 1) for j in range(3)]
            tiles += [(SEG[2], SEG[2] + 96, 2), (SEG[2] + 96, SEG[3], 2), (SEG[3], SEG[4], 3), (SEG[4], SEG[5], 4)]
            st = dict(m=None, total=None, delta=None)

            def top(lo, hi, seg, i=i, lanes=lanes, st=st):
                t = s[lo:hi, lanes]
                if seg == 0 and lo == 128 * i:
                    t = jnp.where(upper, t, NEG)
                t = jnp.max(t, axis=0, keepdims=True)
                if biases[seg] is not None:
                    t = t + biases[seg]
                st["m"] = t if st["m"] is None else jnp.maximum(st["m"], t)

            def exps(lo, hi, seg, i=i, lanes=lanes, st=st):
                m = st["m"] * c
                shift = m if biases[seg] is None else m - biases[seg]
                t = s[lo:hi, lanes] * c - shift
                if seg == 0 and lo == 128 * i:
                    t = jnp.where(upper, t, NEG)
                e = jnp.exp2(t)
                s[lo:hi, lanes] = e
                total = jnp.sum(e, axis=0, keepdims=True)
                delta = jnp.sum(e * dp[lo:hi, lanes], axis=0, keepdims=True)
                st["total"] = total if st["total"] is None else st["total"] + total
                st["delta"] = delta if st["delta"] is None else st["delta"] + delta

            def norm(st=st):
                st["inv"] = 1.0 / st["total"]
                st["delta"] = st["delta"] * st["inv"]

            def scores(lo, hi, lanes=lanes, st=st):
                prob = s[lo:hi, lanes] * st["inv"]
                p[lo:hi, lanes] = prob.astype(BF16)
                ds[lo:hi, lanes] = (prob * (dp[lo:hi, lanes] - st["delta"])).astype(BF16)

            for lo, hi, seg in tiles:
                yield functools.partial(top, lo, hi, seg)
            for lo, hi, seg in tiles:
                yield functools.partial(exps, lo, hi, seg)
            yield norm
            for lo, hi, seg in tiles:
                yield functools.partial(scores, lo, hi)

    def gradients(b):
        kv, p, ds = kvs.at[b % 2], ps.at[b % 2], dss.at[b % 2]

        def queries(i):
            lanes = slice(128 * i, 128 * i + 128)
            part = dot(ds[:, lanes], kv[:, :HD], ((0,), (0,))) * SCALE
            dq_ref[0, b, lanes] = part.astype(BF16)

        def pair(lo, hi):
            dk = dot(ds[lo:hi], q_of(b), ((1,), (0,))) * SCALE
            dv = dot(p[lo:hi], g_of(b), ((1,), (0,)))
            return jnp.concatenate([dk, dv], axis=1)

        def own(j):
            acc_ref[0, b, 128 * j : 128 * j + 128] = pair(128 * j, 128 * j + 128)

        def near(j):
            rows = slice(128 * j, 128 * j + 128)
            term = pair(BLK + 128 * j, BLK + 128 * j + 128)
            if b == 0:
                prev[rows] = term
            else:
                acc_ref[0, b - 1, rows] += term

        def two():
            term = pair(SEG[2], SEG[3]).astype(BF16)
            if b == 0:
                rnext_ref[0, NEXT_L1:NEXT_L2] = term
            elif b == 1:
                prev[...] += spread(2, meta[OWN + 4 * b + 1], term)
            else:
                acc_ref[0, b - 2] += spread(2, meta[OWN + 4 * b + 1], term)

        def four():
            term = pair(SEG[3], SEG[4]).astype(BF16)
            if b < 3:
                rnext_ref[0, NEXT_L2 + 96 * b : NEXT_L2 + 96 * b + 96] = term
            else:
                rnext_ref[0, 0:BLK] = (prev[...] + spread(4, meta[OWN + 4 * b + 2], term)).astype(BF16)

        def eight():
            rfar_ref[0, 48 * b : 48 * b + 48] = pair(SEG[4], SEG[5]).astype(BF16)

        for j in range(3):
            yield functools.partial(own, j)
            yield functools.partial(near, j)
        yield two
        yield four
        yield eight
        for i in range(3):
            yield functools.partial(queries, i)

    for i in range(2):
        ps[i, 0:BLK] = jnp.zeros((BLK, BLK), BF16)
        dss[i, 0:BLK] = jnp.zeros((BLK, BLK), BF16)
    emit(products(0))
    for b in range(GROUP):
        emit(softmax(b))
        if b + 1 < GROUP:
            emit(products(b + 1))
        emit(gradients(b))


def join_kernel(meta, acc_ref, dq_ref, near_ref, far_ref, *refs):
    z_ref, t = refs[-2:]
    b = pl.program_id(0)
    l2_at = pl.ds(pl.multiple_of(NEXT_L2 + 96 * jnp.minimum(b, 2), 32), 96)
    l3_at = pl.ds(pl.multiple_of(48 * b, 16), 48)
    t[...] = acc_ref[0, 0] + spread(8, meta[AFT + 4 * b + 3], far_ref[0, l3_at])

    @pl.when(b < 3)
    def _():
        t[...] += spread(4, meta[NXT + 4 * b + 2], near_ref[0, l2_at])

    @pl.when(b == 2)
    def _():
        t[...] += spread(2, meta[NXT + 1], near_ref[0, NEXT_L1:NEXT_L2])

    @pl.when(b == 3)
    def _():
        t[...] += near_ref[0, 0:BLK].astype(F32)

    z_ref[:, 0] = dq_ref[0, 0].reshape(2, HALF, HD)
    z_ref[:, 1] = t[:, :HD].astype(BF16).reshape(2, HALF, HD)
    z_ref[:, 2] = t[:, HD:].astype(BF16).reshape(2, HALF, HD)


def columns(device, first, count):
    return pl.ds((device * HEADS + first) * HD, count * HD)


def pack_kernel(parts, *refs):
    arrays, outs, (held, ins, sems) = refs[:2], refs[2:-3], refs[-3:]
    reads = [pltpu.make_async_copy(a, held.at[i], ins.at[i]) for i, a in enumerate(arrays)]
    for read in reads:
        read.start()
    writes = []
    for i, read in enumerate(reads):
        read.wait()
        for j, part in enumerate(parts):
            for g in range(LINE):
                write = pltpu.make_async_copy(
                    held.at[i, :, columns(g, *part)], outs[j].at[g, i], sems.at[i, j, g]
                )
                write.start()
                writes.append(write)
    for write in writes:
        write.wait()


def unpack_kernel(head, w_ref, *refs):
    outs, (held, ins, sems) = refs[-6:-3], refs[-3:]
    reads = [pltpu.make_async_copy(w_ref.at[g], held.at[g], ins.at[g]) for g in range(LINE)]
    for read in reads:
        read.start()
    writes = []
    for g, read in enumerate(reads):
        read.wait()
        for i in range(3):
            write = pltpu.make_async_copy(held.at[g, i], outs[i].at[:, columns(g, head, 1)], sems.at[g, i])
            write.start()
            writes.append(write)
    for write in writes:
        write.wait()


SMEM = pl.BlockSpec(memory_space=pltpu.SMEM)
ANY = pl.BlockSpec(memory_space=pl.ANY)


def params(mib, axes=1):
    return pltpu.CompilerParams(
        dimension_semantics=("arbitrary",) * axes, vmem_limit_bytes=mib * 2**20
    )


def whole(shape):
    return pl.BlockSpec(shape, lambda b: (0,) * len(shape))


def y_spec(head, arrays):
    return pl.BlockSpec((LINE, 1, arrays, HALF, HD), lambda b: (0, head, 0, 0, 0))


def cost(flops, size, exps=0):
    return pl.CostEstimate(flops=int(flops), bytes_accessed=int(size), transcendentals=int(exps))


NEXT = jax.ShapeDtypeStruct((1, NEXT_ROWS, 2 * HD), BF16)
FAR = jax.ShapeDtypeStruct((1, FAR_ROWS, 2 * HD), BF16)


def packed(arrays, parts):
    widths = [count * HD for _, count in parts]
    return pl.pallas_call(
        functools.partial(pack_kernel, parts),
        in_specs=[ANY] * 2,
        out_specs=[ANY] * len(parts),
        out_shape=[jax.ShapeDtypeStruct((LINE, 2, HALF, width), BF16) for width in widths],
        scratch_shapes=[
            pltpu.VMEM((2, HALF, LINE * HEADS * HD), BF16),
            pltpu.SemaphoreType.DMA((2,)),
            pltpu.SemaphoreType.DMA((2, len(parts), LINE)),
        ],
        compiler_params=pltpu.CompilerParams(vmem_limit_bytes=60 * 2**20),
        cost_estimate=cost(0, 2**23),
        name="packed",
    )(*arrays)


def unpacked(w, head, into):
    into = tuple(into)
    return pl.pallas_call(
        functools.partial(unpack_kernel, head),
        in_specs=[ANY] * (1 + len(into)),
        out_specs=[ANY] * 3,
        out_shape=[jax.ShapeDtypeStruct((HALF, LINE * HEADS * HD), BF16)] * 3,
        input_output_aliases={1 + i: i for i in range(len(into))},
        scratch_shapes=[
            pltpu.VMEM((LINE, 3, HALF, HD), BF16),
            pltpu.SemaphoreType.DMA((LINE,)),
            pltpu.SemaphoreType.DMA((LINE, 3)),
        ],
        compiler_params=pltpu.CompilerParams(vmem_limit_bytes=60 * 2**20),
        cost_estimate=cost(0, 2**23),
        name="unpacked",
    )(w, *into)


def rows_to_send(meta, y, pair, after=()):
    far = (HEADS, FAR_ROWS, 2 * HD)
    first = pair == 0
    return pl.pallas_call(
        functools.partial(send_kernel, pair),
        grid=(1,),
        in_specs=[SMEM, whole(y.shape)] + [ANY] * len(after),
        out_specs=[whole(NEXT.shape)] * PAIR + [whole(far)] * first,
        out_shape=[NEXT] * PAIR + [jax.ShapeDtypeStruct(far, BF16)] * first,
        compiler_params=params(32),
        cost_estimate=cost(2**29, 2**23),
        name="rows_to_send",
    )(meta, y, *after)


def attention(meta, y, w, head, near, far, after=()):
    at = head % PAIR
    return pl.pallas_call(
        main_kernel,
        grid=(1,),
        in_specs=[
            SMEM,
            pl.BlockSpec((LINE, 2, HALF, HD), lambda b: (0, 0, 0, head)),
            pl.BlockSpec((LINE, 2, HALF, HD), lambda b: (0, 0, 0, at)),
            whole(NEXT.shape),
            pl.BlockSpec((1, FAR_ROWS, 2 * HD), lambda b: (head, 0, 0)),
        ]
        + [ANY] * len(after),
        out_specs=[
            whole((1, GROUP, BLK, HD)),
            whole((1, GROUP, BLK, 2 * HD)),
            whole(NEXT.shape),
            whole(FAR.shape),
        ],
        out_shape=[
            jax.ShapeDtypeStruct((1, GROUP, BLK, HD), BF16),
            jax.ShapeDtypeStruct((1, GROUP, BLK, 2 * HD), F32),
            NEXT,
            FAR,
        ],
        scratch_shapes=[
            pltpu.VMEM((2, KEYS, 2 * HD), BF16),
            pltpu.VMEM((2, KEYS, BLK), F32),
            pltpu.VMEM((2, KEYS, BLK), F32),
            pltpu.VMEM((2, KEYS, BLK), BF16),
            pltpu.VMEM((2, KEYS, BLK), BF16),
            pltpu.VMEM((BLK, 2 * HD), F32),
        ],
        compiler_params=params(32),
        cost_estimate=cost(GROUP * BLK * KEYS * HD * 30, 5 * 2**20, GROUP * BLK * KEYS),
        name="attention",
    )(meta, y, w, near, far, *after)


def joined(meta, acc, dq, near, far, after=()):
    return pl.pallas_call(
        join_kernel,
        grid=(GROUP,),
        in_specs=[
            SMEM,
            pl.BlockSpec((1, 1, BLK, 2 * HD), lambda b: (0, b, 0, 0)),
            pl.BlockSpec((1, 1, BLK, HD), lambda b: (0, b, 0, 0)),
            whole(NEXT.shape),
            whole(FAR.shape),
        ]
        + [ANY] * len(after),
        out_specs=pl.BlockSpec((2, 3, HALF, HD), lambda b: (b, 0, 0, 0)),
        out_shape=jax.ShapeDtypeStruct((LINE, 3, HALF, HD), BF16),
        scratch_shapes=[pltpu.VMEM((BLK, 2 * HD), F32)],
        compiler_params=params(16),
        cost_estimate=cost(2**29, 2**23),
        name="joined",
    )(meta, acc, dq, near, far, *after)


def shift(value, steps):
    count = lax.axis_size(GROUP_AXES)
    pairs = [(i, i + steps) for i in range(count) if 0 <= i + steps < count]
    return lax.ppermute(value, GROUP_AXES, pairs)


def both(value, axis):
    other = lax.ppermute(value, axis, [(0, 1), (1, 0)])
    first = lax.axis_index(axis) == 0
    return jnp.stack([jnp.where(first, value, other), jnp.where(first, other, value)])


def meta_of(pattern, phase):
    own = jnp.concatenate([pattern, phase], axis=1)
    rows = jnp.concatenate([own, shift(own, -1), shift(own, -2)], axis=0)
    rows = both(both(rows, "core"), "yh").reshape(GROUP, 3, 2 * LEVELS)
    block = lax.axis_index(GROUP_AXES) * GROUP + jnp.arange(GROUP)
    distance = 2 ** jnp.arange(LEVELS)
    active = (rows[:, 0, :LEVELS] == 1) & (block[:, None] >= distance[None, :])
    phases = rows[:, :, LEVELS:].transpose(1, 0, 2)
    return jnp.concatenate([active.astype(jnp.int32).reshape(-1), phases.reshape(-1)])


def exchange(x):
    return lax.all_to_all(x, LINE_AXES, 0, 0, tiled=True)


def body(queries, keys, values, grad_out, pattern, phase):
    (x,) = packed((keys, values), ((0, HEADS),))
    y = exchange(x)
    meta = meta_of(pattern, phase)
    w = [exchange(x) for x in packed((queries, grad_out), ((0, PAIR), (PAIR, PAIR)))]
    near0, near1, far = rows_to_send(meta, y, 0)
    far, near0, near1 = shift(far, 2), shift(near0, 1), shift(near1, 1)

    def grads(head, near, after=()):
        dq, acc, back, far_back = attention(meta, y, w[head // PAIR], head, near, far, after)
        return acc, dq, shift(back, -1), shift(far_back, -2)

    g0 = grads(0, near0)
    near2, near3 = rows_to_send(meta, y, 1, (g0[0],))
    near2, near3 = shift(near2, 1), shift(near3, 1)
    g1 = grads(1, near1, (g0[0],))
    z0 = joined(meta, *g0, (g1[0],))
    o0 = exchange(z0)
    g2 = grads(2, near2, (z0,))
    z1 = joined(meta, *g1, (g2[0],))
    o1 = exchange(z1)
    g3 = grads(3, near3, (z1, o0))
    z2 = joined(meta, *g2, (g3[0],))
    o2 = exchange(z2)
    z3 = joined(meta, *g3, (z2, o1))
    out = ()
    for head, o in enumerate((o0, o1, o2, exchange(z3))):
        out = unpacked(o, head, out)
    return tuple(out)


def solution(mesh):
    sizes = (4, 4, 2, 2, 2)
    line = Mesh(mesh.devices.reshape(sizes), ("z", "x", "yh", "core", "yl"))
    ctx = ("z", "x", "yh", "core")
    tokens = P((*ctx, "yl"), None)
    return jax.shard_map(
        body,
        mesh=line,
        in_specs=(tokens,) * 4 + (P(ctx, None),) * 2,
        out_specs=(tokens,) * 3,
        check_vma=False,
    )
```

time: 291 us -> 241 us (0.83)
  starting transfers between devices: 116 us -> 82.9 us
  other arithmetic: 10.1 us -> 0.42 us
  local copies, waits for them, and re-layouts: 25.3 us -> 18.3 us
    ppermute x18 -> x15, starting transfers between devices: 77.1 us -> 47.6 us  [shift(): return lax.ppermute(value, GROUP_AXES, pairs)]
    all_to_all x8 -> x7, waiting for transfers between devices: 35.8 us -> 20.6 us  [exchange(): return lax.all_to_all(x, LINE_AXES, 0, 0, tiled=True)]
    ppermute x2, waiting for transfers between devices: 6.23 us -> 20.5 us  [both(): other = lax.ppermute(value, axis, [(0, 1), (1, 0)])]
    slice x16 -> x0, local copies, waits for them, and re-layouts: 7.15 us -> none  [body(): r[i]]
    transpose x4 -> x0, other arithmetic: 5.35 us -> none  [body(): x = x.reshape(4, HALF, LINE, heads, HD).transpose(2, 3, 0, 1, 4)]
    concatenate x3 -> x0, other arithmetic: 3.81 us -> none  [body(): jnp.concatenate([r[i] for r in results], axis=1)]
    all_to_all x8 -> x7, starting transfers between devices: 35.4 us -> 31.7 us  [exchange(): return lax.all_to_all(x, LINE_AXES, 0, 0, tiled=True)]
    pallas_call x12 -> x16, Pallas kernels: 73.3 us -> 71.2 us  [the longest x4 41.3 us: attention(): pl.pallas_call(main_kernel, grid=(1,), in_specs=[SMEM, pl.BlockSpec((LINE...]
  transfers between devices with their start and end apart: 28 -> 24, of which waited for: 11 -> 8; matrix products, arithmetic and copies ran while one was open for 6% -> 0% of each run, Pallas kernels for 25% -> 28%
where the time goes in v2:
time: 241 us; the launch traced here: 236 us
  starting transfers between devices  82.9 us (34%)
  Pallas kernels  71.2 us (30%)
  waiting for transfers between devices  61.9 us (26%)
  local copies, waits for them, and re-layouts  18.3 us (8%)
    ppermute x15, starting transfers between devices, shift(): return lax.ppermute(value, GROUP_AXES, pairs)  47.6 us
    pallas_call x4, Pallas kernels, attention(): pl.pallas_call(main_kernel, grid=(1,), in_specs=[SMEM, pl.BlockSpec((LINE...  41.3 us
    all_to_all x7, starting transfers between devices, exchange(): return lax.all_to_all(x, LINE_AXES, 0, 0, tiled=True)  31.7 us
    ppermute x15, waiting for transfers between devices, shift(): return lax.ppermute(value, GROUP_AXES, pairs)  20.9 us
    all_to_all x7, waiting for transfers between devices, exchange(): return lax.all_to_all(x, LINE_AXES, 0, 0, tiled=True)  20.6 us
    ppermute x2, waiting for transfers between devices, both(): other = lax.ppermute(value, axis, [(0, 1), (1, 0)])  20.5 us
    unnamed x58, local copies, waits for them, and re-layouts  18 us
    pallas_call x4, Pallas kernels, joined(): pl.pallas_call(join_kernel, grid=(GROUP,), in_specs=[SMEM, pl.BlockSpec((...  10.2 us
  transfers between devices with their start and end apart: 24, of which 8 were waited for; matrix products, arithmetic and copies ran while one was open for 0% of the time, Pallas kernels for 28%

profile of v2, /device:TPU:38, one launch (start us, length us, event | category | flops | bytes accessed | tf_op | source)
XLA Modules:
  0.0 236.2 jit_solution(13881625386504156375)
XLA Ops:
  0.6 3.2 %packed.2 = bf16[8,2,192,512]{3,2,1,0:T(8,128)(2,1)} custom-call(bf16[192,4096]{1,0:T(8,128)(2,1)} %refs_0_.2, bf16[192,4096]{1,0:T(8,128)(2,1)} %refs_1_.2), custom_call_target="tpu_custom_call" | custom-call | bytes 8388608 | tf_op jit(solution)/shard_map/packed/pallas_call | solution.py:335
  3.9 4.5 %all-to-all-start = ((bf16[8,2,192,512]{3,2,1,0:T(8,128)(2,1)}), bf16[8,2,192,512]{3,2,1,0:T(8,128)(2,1)S(1)}, u32[]{:S(2)}, u32[]{:S(2)}) async-start(bf16[8,2,192,512]{3,2,1,0:T(8,128)(2,1)} %packed.2), calls=%async_computation | async-start | bytes 6291456 | tf_op jit(solution)/shard_map/all_to_all | solution.py:469
  8.5 3.3 %collective-permute-start.1 = (s32[1,8]{1,0:T(1,128)S(1)}, s32[1,8]{1,0:T(1,128)S(1)}, u32[]{:S(2)}, u32[]{:S(2)}) collective-permute-start(s32[1,8]{1,0:T(1,128)S(1)} %pad_add_fusion.3), channel_id=1, source_target_pairs={{16,0},{24,8},{32,16},{40,24},{48,32},{56,40},{64,48},{72,56},{80,... | collective-permute-start | bytes 104 | tf_op jit(solution)/shard_map/ppermute | solution.py:448
  13.8 2.5 %collective-permute-done.1 = s32[1,8]{1,0:T(1,128)S(1)} collective-permute-done((s32[1,8]{1,0:T(1,128)S(1)}, s32[1,8]{1,0:T(1,128)S(1)}, u32[]{:S(2)}, u32[]{:S(2)}) %collective-permute-start.1) | collective-permute-done | bytes 64 | tf_op jit(solution)/shard_map/ppermute | solution.py:448
  16.3 3.0 %collective-permute-done = s32[1,8]{1,0:T(1,128)S(1)} collective-permute-done((s32[1,8]{1,0:T(1,128)S(1)}, s32[1,8]{1,0:T(1,128)S(1)}, u32[]{:S(2)}, u32[]{:S(2)}) %collective-permute-start) | collective-permute-done | bytes 64 | tf_op jit(solution)/shard_map/ppermute | solution.py:448
  20.6 3.5 %collective-permute-start.3 = (s32[2,3,8]{2,1,0:T(4,128)S(1)}, s32[2,3,8]{2,1,0:T(4,128)S(1)}, u32[]{:S(2)}, u32[]{:S(2)}) collective-permute-start(s32[2,3,8]{2,1,0:T(4,128)S(1)} %pad_add_fusion.1), channel_id=1, source_target_pairs={{0,4},{4,0},{1,5},{5,1},{2,6},{6,2},{3,7},{7,3},{8,12},{12,8},{9,1... | collective-permute-start | bytes 584 | tf_op jit(solution)/shard_map/ppermute | solution.py:452
  24.2 3.3 %packed.3 = (bf16[8,2,192,256]{3,2,1,0:T(8,128)(2,1)}, bf16[8,2,192,256]{3,2,1,0:T(8,128)(2,1)}) custom-call(bf16[192,4096]{1,0:T(8,128)(2,1)} %refs_0_.3, bf16[192,4096]{1,0:T(8,128)(2,1)} %refs_1_.3), custom_call_target="tpu_custom_call" | custom-call | bytes 8388608 | tf_op jit(solution)/shard_map/packed/pallas_call | solution.py:335
  27.5 19.4 %collective-permute-done.3 = s32[2,3,8]{2,1,0:T(4,128)S(1)} collective-permute-done((s32[2,3,8]{2,1,0:T(4,128)S(1)}, s32[2,3,8]{2,1,0:T(4,128)S(1)}, u32[]{:S(2)}, u32[]{:S(2)}) %collective-permute-start.3) | collective-permute-done | bytes 224 | tf_op jit(solution)/shard_map/ppermute | solution.py:452
  46.9 4.3 %all-to-all-start.2 = ((bf16[8,2,192,256]{3,2,1,0:T(8,128)(2,1)}), bf16[8,2,192,256]{3,2,1,0:T(8,128)(2,1)}, u32[]{:S(2)}, u32[]{:S(2)}) async-start(bf16[8,2,192,256]{3,2,1,0:T(8,128)(2,1)} %get-tuple-element.36), calls=%async_computation.2 | async-start | bytes 3145728 | tf_op jit(solution)/shard_map/all_to_all | solution.py:469
  54.8 3.7 %collective-permute-start.4 = (bf16[1,864,256]{2,1,0:T(8,128)(2,1)}, bf16[1,864,256]{2,1,0:T(8,128)(2,1)}, u32[]{:S(2)}, u32[]{:S(2)}) collective-permute-start(bf16[1,864,256]{2,1,0:T(8,128)(2,1)} %get-tuple-element.37), channel_id=1, source_target_pairs={{0,8},{8,16},{16,24},{24,32},{32,40},{40,48},{48,56},{56,64},{64,7... | collective-permute-start | bytes 1327112 | tf_op jit(solution)/shard_map/ppermute | solution.py:448
  58.5 4.3 %collective-permute-start.5 = (bf16[4,192,256]{2,1,0:T(8,128)(2,1)}, bf16[4,192,256]{2,1,0:T(8,128)(2,1)S(1)}, u32[]{:S(2)}, u32[]{:S(2)}) collective-permute-start(bf16[4,192,256]{2,1,0:T(8,128)(2,1)} %get-tuple-element.38), channel_id=1, source_target_pairs={{0,16},{8,24},{16,32},{24,40},{32,48},{40,56},{48,64},{56,72},{64,... | collective-permute-start | bytes 1179656 | tf_op jit(solution)/shard_map/ppermute | solution.py:448
  62.9 10.0 %all-to-all-done.2.w_ref = bf16[8,2,192,256]{3,2,1,0:T(8,128)(2,1)} async-done(((bf16[8,2,192,256]{3,2,1,0:T(8,128)(2,1)}), bf16[8,2,192,256]{3,2,1,0:T(8,128)(2,1)}, u32[]{:S(2)}, u32[]{:S(2)}) %all-to-all-start.2) | async-done | bytes 1572896 | tf_op jit(solution)/shard_map/all_to_all | solution.py:469
  72.9 4.3 %all-to-all-start.1 = ((bf16[8,2,192,256]{3,2,1,0:T(8,128)(2,1)}), bf16[8,2,192,256]{3,2,1,0:T(8,128)(2,1)}, u32[]{:S(2)}, u32[]{:S(2)}) async-start(bf16[8,2,192,256]{3,2,1,0:T(8,128)(2,1)} %get-tuple-element.35), calls=%async_computation.1 | async-start | bytes 3145728 | tf_op jit(solution)/shard_map/all_to_all | solution.py:469
  77.2 4.3 %collective-permute-start.7 = (bf16[1,864,256]{2,1,0:T(8,128)(2,1)}, bf16[1,864,256]{2,1,0:T(8,128)(2,1)S(1)}, u32[]{:S(2)}, u32[]{:S(2)}) collective-permute-start(bf16[1,864,256]{2,1,0:T(8,128)(2,1)} %copy-done.15), channel_id=1, source_target_pairs={{0,8},{8,16},{16,24},{24,32},{32,40},{40,48},{48,56},{56,64},{64,7... | collective-permute-start | bytes 1327112 | tf_op jit(solution)/shard_map/ppermute | solution.py:448
  81.5 10.3 %attention.4 = (bf16[1,4,384,128]{3,2,1,0:T(8,128)(2,1)S(1)}, f32[1,4,384,256]{3,2,1,0:T(8,128)S(1)}, bf16[1,864,256]{2,1,0:T(8,128)(2,1)S(1)}, bf16[1,192,256]{2,1,0:T(8,128)(2,1)S(1)}) custom-call(s32[64]{0:T(128)S(1)} %pad_add_fusion.4.meta, bf16[8,2,192,512]{3,2,1,0:T(8,128)(2,1)S(1)} %all-to-all-done.y_ref, ...), custom_call_target="tpu_custom_call" | custom-call | flops 6511656960 | bytes 5242880 | tf_op jit(solution)/shard_map/attention/pallas_call | solution.py:387
  94.3 3.4 %collective-permute-start.10 = (bf16[1,864,256]{2,1,0:T(8,128)(2,1)}, bf16[1,864,256]{2,1,0:T(8,128)(2,1)}, u32[]{:S(2)}, u32[]{:S(2)}) collective-permute-start(bf16[1,864,256]{2,1,0:T(8,128)(2,1)} %get-tuple-element.46), channel_id=1, source_target_pairs={{0,8},{8,16},{16,24},{24,32},{32,40},{40,48},{48,56},{56,64},{64,7... | collective-permute-start | bytes 1327112 | tf_op jit(solution)/shard_map/ppermute | solution.py:448
  100.1 3.1 %collective-permute-start.12 = (bf16[1,192,256]{2,1,0:T(8,128)(2,1)S(1)}, bf16[1,192,256]{2,1,0:T(8,128)(2,1)S(1)}, u32[]{:S(2)}, u32[]{:S(2)}) collective-permute-start(bf16[1,192,256]{2,1,0:T(8,128)(2,1)S(1)} %get-tuple-element.49), channel_id=1, source_target_pairs={{16,0},{24,8},{32,16},{40,24},{48,32},{56,40},{64,48},{72,56},{80,... | collective-permute-start | bytes 294920 | tf_op jit(solution)/shard_map/ppermute | solution.py:448
  103.3 10.1 %attention.5 = (bf16[1,4,384,128]{3,2,1,0:T(8,128)(2,1)S(1)}, f32[1,4,384,256]{3,2,1,0:T(8,128)S(1)}, bf16[1,864,256]{2,1,0:T(8,128)(2,1)S(1)}, bf16[1,192,256]{2,1,0:T(8,128)(2,1)S(1)}) custom-call(s32[64]{0:T(128)S(1)} %pad_add_fusion.4.meta, bf16[8,2,192,512]{3,2,1,0:T(8,128)(2,1)S(1)} %all-to-all-done.y_ref, ...), custom_call_target="tpu_custom_call" | custom-call | flops 6511656960 | bytes 5242880 | tf_op jit(solution)/shard_map/attention/pallas_call | solution.py:387
  120.1 4.5 %all-to-all-start.3 = ((bf16[8,3,192,128]{3,2,1,0:T(8,128)(2,1)}), bf16[8,3,192,128]{3,2,1,0:T(8,128)(2,1)}, u32[]{:S(2)}, u32[]{:S(2)}) async-start(bf16[8,3,192,128]{3,2,1,0:T(8,128)(2,1)} %copy-done.6), calls=%async_computation.3 | async-start | bytes 2359296 | tf_op jit(solution)/shard_map/all_to_all | solution.py:469
  124.6 4.0 %collective-permute-start.6 = (bf16[1,864,256]{2,1,0:T(8,128)(2,1)}, bf16[1,864,256]{2,1,0:T(8,128)(2,1)}, u32[]{:S(2)}, u32[]{:S(2)}) collective-permute-start(bf16[1,864,256]{2,1,0:T(8,128)(2,1)} %copy-done.13), channel_id=1, source_target_pairs={{0,8},{8,16},{16,24},{24,32},{32,40},{40,48},{48,56},{56,64},{64,7... | collective-permute-start | bytes 1327112 | tf_op jit(solution)/shard_map/ppermute | solution.py:448
  130.5 3.7 %collective-permute-start.9 = (bf16[1,192,256]{2,1,0:T(8,128)(2,1)}, bf16[1,192,256]{2,1,0:T(8,128)(2,1)S(1)}, u32[]{:S(2)}, u32[]{:S(2)}) collective-permute-start(bf16[1,192,256]{2,1,0:T(8,128)(2,1)} %copy-done.23), channel_id=1, source_target_pairs={{16,0},{24,8},{32,16},{40,24},{48,32},{56,40},{64,48},{72,56},{80,... | collective-permute-start | bytes 294920 | tf_op jit(solution)/shard_map/ppermute | solution.py:448
  136.5 10.7 %attention.6 = (bf16[1,4,384,128]{3,2,1,0:T(8,128)(2,1)S(1)}, f32[1,4,384,256]{3,2,1,0:T(8,128)S(1)}, bf16[1,864,256]{2,1,0:T(8,128)(2,1)S(1)}, bf16[1,192,256]{2,1,0:T(8,128)(2,1)}) custom-call(s32[64]{0:T(128)S(1)} %pad_add_fusion.4.meta, bf16[8,2,192,512]{3,2,1,0:T(8,128)(2,1)S(1)} %all-to-all-done.y_ref, bf16[8,2,192,256]{3,2,1,0:T(8,128)(2,1)} %all-to-all-done.1.w_ref, ...), custom_call_target="tpu_custom_call" | custom-call | flops 6511656960 | bytes 5242880 | tf_op jit(solution)/shard_map/attention/pallas_call | solution.py:387
  153.1 4.8 %all-to-all-start.4 = ((bf16[8,3,192,128]{3,2,1,0:T(8,128)(2,1)}), bf16[8,3,192,128]{3,2,1,0:T(8,128)(2,1)}, u32[]{:S(2)}, u32[]{:S(2)}) async-start(bf16[8,3,192,128]{3,2,1,0:T(8,128)(2,1)} %copy-done.8), calls=%async_computation.4 | async-start | bytes 2359296 | tf_op jit(solution)/shard_map/all_to_all | solution.py:469
  157.9 4.1 %collective-permute-start.15 = (bf16[1,864,256]{2,1,0:T(8,128)(2,1)}, bf16[1,864,256]{2,1,0:T(8,128)(2,1)S(1)}, u32[]{:S(2)}, u32[]{:S(2)}) collective-permute-start(bf16[1,864,256]{2,1,0:T(8,128)(2,1)} %copy-done.16), channel_id=1, source_target_pairs={{8,0},{16,8},{24,16},{32,24},{40,32},{48,40},{56,48},{64,56},{72,6... | collective-permute-start | bytes 1327112 | tf_op jit(solution)/shard_map/ppermute | solution.py:448
  162.1 2.9 %collective-permute-start.16 = (bf16[1,192,256]{2,1,0:T(8,128)(2,1)}, bf16[1,192,256]{2,1,0:T(8,128)(2,1)S(1)}, u32[]{:S(2)}, u32[]{:S(2)}) collective-permute-start(bf16[1,192,256]{2,1,0:T(8,128)(2,1)} %get-tuple-element.57), channel_id=1, source_target_pairs={{16,0},{24,8},{32,16},{40,24},{48,32},{56,40},{64,48},{72,56},{80,... | collective-permute-start | bytes 294920 | tf_op jit(solution)/shard_map/ppermute | solution.py:448
  167.3 10.3 %attention.7 = (bf16[1,4,384,128]{3,2,1,0:T(8,128)(2,1)S(1)}, f32[1,4,384,256]{3,2,1,0:T(8,128)S(1)}, bf16[1,864,256]{2,1,0:T(8,128)(2,1)S(1)}, bf16[1,192,256]{2,1,0:T(8,128)(2,1)S(1)}) custom-call(s32[64]{0:T(128)S(1)} %pad_add_fusion.4.meta, bf16[8,2,192,512]{3,2,1,0:T(8,128)(2,1)S(1)} %all-to-all-done.y_ref, ...), custom_call_target="tpu_custom_call" | custom-call | flops 6511656960 | bytes 5242880 | tf_op jit(solution)/shard_map/attention/pallas_call | solution.py:387
  179.0 3.3 %joined.6.refs_0_ = bf16[8,3,192,128]{3,2,1,0:T(8,128)(2,1)} custom-call(s32[64]{0:T(128)S(1)} %pad_add_fusion.4.meta, f32[1,4,384,256]{3,2,1,0:T(8,128)S(1)} %copy-done.3, bf16[1,4,384,128]{3,2,1,0:T(8,128)(2,1)S(1)} %copy-done.12, bf16[1,864,256]{2,1,0:T(8,128)(2,1)S(1)} %collective-permute-done.15.near_ref, ...), custom_call_target="tpu_custom_call" | custom-call | flops 536870912 | bytes 8388608 | tf_op jit(solution)/shard_map/joined/pallas_call | solution.py:425
  183.4 4.9 %all-to-all-start.6 = ((bf16[8,3,192,128]{3,2,1,0:T(8,128)(2,1)}), bf16[8,3,192,128]{3,2,1,0:T(8,128)(2,1)}, u32[]{:S(2)}, u32[]{:S(2)}) async-start(bf16[8,3,192,128]{3,2,1,0:T(8,128)(2,1)} %joined.6.refs_0_), calls=%async_computation.6 | async-start | bytes 2359296 | tf_op jit(solution)/shard_map/all_to_all | solution.py:469
  190.3 2.5 %collective-permute-start.14 = (bf16[1,192,256]{2,1,0:T(8,128)(2,1)S(1)}, bf16[1,192,256]{2,1,0:T(8,128)(2,1)S(1)}, u32[]{:S(2)}, u32[]{:S(2)}) collective-permute-start(bf16[1,192,256]{2,1,0:T(8,128)(2,1)S(1)} %copy-done.25), channel_id=1, source_target_pairs={{16,0},{24,8},{32,16},{40,24},{48,32},{56,40},{64,48},{72,56},{80,... | collective-permute-start | bytes 294920 | tf_op jit(solution)/shard_map/ppermute | solution.py:448
  192.8 14.5 %collective-permute-done.14.far_ref = bf16[1,192,256]{2,1,0:T(8,128)(2,1)S(1)} collective-permute-done((bf16[1,192,256]{2,1,0:T(8,128)(2,1)S(1)}, bf16[1,192,256]{2,1,0:T(8,128)(2,1)S(1)}, u32[]{:S(2)}, u32[]{:S(2)}) %collective-permute-start.14) | collective-permute-done | bytes 98336 | tf_op jit(solution)/shard_map/ppermute | solution.py:448
  210.7 4.4 %all-to-all-start.5 = ((bf16[8,3,192,128]{3,2,1,0:T(8,128)(2,1)}), bf16[8,3,192,128]{3,2,1,0:T(8,128)(2,1)S(1)}, u32[]{:S(2)}, u32[]{:S(2)}) async-start(bf16[8,3,192,128]{3,2,1,0:T(8,128)(2,1)} %copy-done.10), calls=%async_computation.5 | async-start | bytes 2359296 | tf_op jit(solution)/shard_map/all_to_all | solution.py:469
  222.0 10.6 %all-to-all-done.5.w_ref = bf16[8,3,192,128]{3,2,1,0:T(8,128)(2,1)S(1)} async-done(((bf16[8,3,192,128]{3,2,1,0:T(8,128)(2,1)}), bf16[8,3,192,128]{3,2,1,0:T(8,128)(2,1)S(1)}, u32[]{:S(2)}, u32[]{:S(2)}) %all-to-all-start.5) | async-done | bytes 1179680 | tf_op jit(solution)/shard_map/all_to_all | solution.py:469
  (107 shorter events, 49.0 us)
Async XLA Ops:
  3.9 43.1 %all-to-all-start = ((bf16[8,2,192,512]{3,2,1,0:T(8,128)(2,1)}), bf16[8,2,192,512]{3,2,1,0:T(8,128)(2,1)S(1)}, u32[]{:S(2)}, u32[]{:S(2)}) async-start(bf16[8,2,192,512]{3,2,1,0:T(8,128)(2,1)} %packed.2), calls=%async_computation | async-start | bytes 6291456 | tf_op jit(solution)/shard_map/all_to_all | solution.py:469
  8.5 7.8 %collective-permute-start.1 = (s32[1,8]{1,0:T(1,128)S(1)}, s32[1,8]{1,0:T(1,128)S(1)}, u32[]{:S(2)}, u32[]{:S(2)}) collective-permute-start(s32[1,8]{1,0:T(1,128)S(1)} %pad_add_fusion.3), channel_id=1, source_target_pairs={{16,0},{24,8},{32,16},{40,24},{48,32},{56,40},{64,48},{72,56},{80,... | collective-permute-start | bytes 104 | tf_op jit(solution)/shard_map/ppermute | solution.py:448
  11.8 7.5 %collective-permute-start = (s32[1,8]{1,0:T(1,128)S(1)}, s32[1,8]{1,0:T(1,128)S(1)}, u32[]{:S(2)}, u32[]{:S(2)}) collective-permute-start(s32[1,8]{1,0:T(1,128)S(1)} %pad_add_fusion.3), channel_id=1, source_target_pairs={{8,0},{16,8},{24,16},{32,24},{40,32},{48,40},{56,48},{64,56},{72,6... | collective-permute-start | bytes 104 | tf_op jit(solution)/shard_map/ppermute | solution.py:448
  19.4 1.2 collective-permute-start.2
  20.6 26.3 %collective-permute-start.3 = (s32[2,3,8]{2,1,0:T(4,128)S(1)}, s32[2,3,8]{2,1,0:T(4,128)S(1)}, u32[]{:S(2)}, u32[]{:S(2)}) collective-permute-start(s32[2,3,8]{2,1,0:T(4,128)S(1)} %pad_add_fusion.1), channel_id=1, source_target_pairs={{0,4},{4,0},{1,5},{5,1},{2,6},{6,2},{3,7},{7,3},{8,12},{12,8},{9,1... | collective-permute-start | bytes 584 | tf_op jit(solution)/shard_map/ppermute | solution.py:452
  46.9 25.9 %all-to-all-start.2 = ((bf16[8,2,192,256]{3,2,1,0:T(8,128)(2,1)}), bf16[8,2,192,256]{3,2,1,0:T(8,128)(2,1)}, u32[]{:S(2)}, u32[]{:S(2)}) async-start(bf16[8,2,192,256]{3,2,1,0:T(8,128)(2,1)} %get-tuple-element.36), calls=%async_computation.2 | async-start | bytes 3145728 | tf_op jit(solution)/shard_map/all_to_all | solution.py:469
  54.8 26.7 %collective-permute-start.4 = (bf16[1,864,256]{2,1,0:T(8,128)(2,1)}, bf16[1,864,256]{2,1,0:T(8,128)(2,1)}, u32[]{:S(2)}, u32[]{:S(2)}) collective-permute-start(bf16[1,864,256]{2,1,0:T(8,128)(2,1)} %get-tuple-element.37), channel_id=1, source_target_pairs={{0,8},{8,16},{16,24},{24,32},{32,40},{40,48},{48,56},{56,64},{64,7... | collective-permute-start | bytes 1327112 | tf_op jit(solution)/shard_map/ppermute | solution.py:448
  58.5 22.9 %collective-permute-start.5 = (bf16[4,192,256]{2,1,0:T(8,128)(2,1)}, bf16[4,192,256]{2,1,0:T(8,128)(2,1)S(1)}, u32[]{:S(2)}, u32[]{:S(2)}) collective-permute-start(bf16[4,192,256]{2,1,0:T(8,128)(2,1)} %get-tuple-element.38), channel_id=1, source_target_pairs={{0,16},{8,24},{16,32},{24,40},{32,48},{40,56},{48,64},{56,72},{64,... | collective-permute-start | bytes 1179656 | tf_op jit(solution)/shard_map/ppermute | solution.py:448
  72.9 47.2 %all-to-all-start.1 = ((bf16[8,2,192,256]{3,2,1,0:T(8,128)(2,1)}), bf16[8,2,192,256]{3,2,1,0:T(8,128)(2,1)}, u32[]{:S(2)}, u32[]{:S(2)}) async-start(bf16[8,2,192,256]{3,2,1,0:T(8,128)(2,1)} %get-tuple-element.35), calls=%async_computation.1 | async-start | bytes 3145728 | tf_op jit(solution)/shard_map/all_to_all | solution.py:469
  77.2 26.1 %collective-permute-start.7 = (bf16[1,864,256]{2,1,0:T(8,128)(2,1)}, bf16[1,864,256]{2,1,0:T(8,128)(2,1)S(1)}, u32[]{:S(2)}, u32[]{:S(2)}) collective-permute-start(bf16[1,864,256]{2,1,0:T(8,128)(2,1)} %copy-done.15), channel_id=1, source_target_pairs={{0,8},{8,16},{16,24},{24,32},{32,40},{40,48},{48,56},{56,64},{64,7... | collective-permute-start | bytes 1327112 | tf_op jit(solution)/shard_map/ppermute | solution.py:448
  81.5 10.3 %copy-start.19 = (bf16[4,192,256]{2,1,0:T(8,128)(2,1)}, bf16[4,192,256]{2,1,0:T(8,128)(2,1)S(1)}, u32[]{:S(2)}) copy-start(bf16[4,192,256]{2,1,0:T(8,128)(2,1)S(1)} %collective-permute-done.5.far_ref) | copy-start | bytes 1179652
  91.8 11.5 %copy-start.20 = (bf16[4,192,256]{2,1,0:T(8,128)(2,1)S(1)}, bf16[4,192,256]{2,1,0:T(8,128)(2,1)}, u32[]{:S(2)}) copy-start(bf16[4,192,256]{2,1,0:T(8,128)(2,1)} %copy-done.19) | copy-start | bytes 1179652
  94.3 39.9 %collective-permute-start.10 = (bf16[1,864,256]{2,1,0:T(8,128)(2,1)}, bf16[1,864,256]{2,1,0:T(8,128)(2,1)}, u32[]{:S(2)}, u32[]{:S(2)}) collective-permute-start(bf16[1,864,256]{2,1,0:T(8,128)(2,1)} %get-tuple-element.46), channel_id=1, source_target_pairs={{0,8},{8,16},{16,24},{24,32},{32,40},{40,48},{48,56},{56,64},{64,7... | collective-permute-start | bytes 1327112 | tf_op jit(solution)/shard_map/ppermute | solution.py:448
  97.7 18.0 %collective-permute-start.11 = (bf16[1,864,256]{2,1,0:T(8,128)(2,1)S(1)}, bf16[1,864,256]{2,1,0:T(8,128)(2,1)S(1)}, u32[]{:S(2)}, u32[]{:S(2)}) collective-permute-start(bf16[1,864,256]{2,1,0:T(8,128)(2,1)S(1)} %get-tuple-element.48), channel_id=1, source_target_pairs={{8,0},{16,8},{24,16},{32,24},{40,32},{48,40},{56,48},{64,56},{72,6... | collective-permute-start | bytes 1327112 | tf_op jit(solution)/shard_map/ppermute | solution.py:448
  100.1 14.7 %collective-permute-start.12 = (bf16[1,192,256]{2,1,0:T(8,128)(2,1)S(1)}, bf16[1,192,256]{2,1,0:T(8,128)(2,1)S(1)}, u32[]{:S(2)}, u32[]{:S(2)}) collective-permute-start(bf16[1,192,256]{2,1,0:T(8,128)(2,1)S(1)} %get-tuple-element.49), channel_id=1, source_target_pairs={{16,0},{24,8},{32,16},{40,24},{48,32},{56,40},{64,48},{72,56},{80,... | collective-permute-start | bytes 294920 | tf_op jit(solution)/shard_map/ppermute | solution.py:448
  120.1 33.0 %all-to-all-start.3 = ((bf16[8,3,192,128]{3,2,1,0:T(8,128)(2,1)}), bf16[8,3,192,128]{3,2,1,0:T(8,128)(2,1)}, u32[]{:S(2)}, u32[]{:S(2)}) async-start(bf16[8,3,192,128]{3,2,1,0:T(8,128)(2,1)} %copy-done.6), calls=%async_computation.3 | async-start | bytes 2359296 | tf_op jit(solution)/shard_map/all_to_all | solution.py:469
  124.6 40.4 %collective-permute-start.6 = (bf16[1,864,256]{2,1,0:T(8,128)(2,1)}, bf16[1,864,256]{2,1,0:T(8,128)(2,1)}, u32[]{:S(2)}, u32[]{:S(2)}) collective-permute-start(bf16[1,864,256]{2,1,0:T(8,128)(2,1)} %copy-done.13), channel_id=1, source_target_pairs={{0,8},{8,16},{16,24},{24,32},{32,40},{40,48},{48,56},{56,64},{64,7... | collective-permute-start | bytes 1327112 | tf_op jit(solution)/shard_map/ppermute | solution.py:448
  128.6 20.1 %collective-permute-start.8 = (bf16[1,864,256]{2,1,0:T(8,128)(2,1)}, bf16[1,864,256]{2,1,0:T(8,128)(2,1)S(1)}, u32[]{:S(2)}, u32[]{:S(2)}) collective-permute-start(bf16[1,864,256]{2,1,0:T(8,128)(2,1)} %copy-done.14), channel_id=1, source_target_pairs={{8,0},{16,8},{24,16},{32,24},{40,32},{48,40},{56,48},{64,56},{72,6... | collective-permute-start | bytes 1327112 | tf_op jit(solution)/shard_map/ppermute | solution.py:448
  130.5 18.1 %copy-start.1 = (f32[1,4,384,256]{3,2,1,0:T(8,128)S(1)}, f32[1,4,384,256]{3,2,1,0:T(8,128)}, u32[]{:S(2)}) copy-start(f32[1,4,384,256]{3,2,1,0:T(8,128)} %copy-done) | copy-start | bytes 4718596
  130.5 18.1 %collective-permute-start.9 = (bf16[1,192,256]{2,1,0:T(8,128)(2,1)}, bf16[1,192,256]{2,1,0:T(8,128)(2,1)S(1)}, u32[]{:S(2)}, u32[]{:S(2)}) collective-permute-start(bf16[1,192,256]{2,1,0:T(8,128)(2,1)} %copy-done.23), channel_id=1, source_target_pairs={{16,0},{24,8},{32,16},{40,24},{48,32},{56,40},{64,48},{72,56},{80,... | collective-permute-start | bytes 294920 | tf_op jit(solution)/shard_map/ppermute | solution.py:448
  153.1 30.3 %all-to-all-start.4 = ((bf16[8,3,192,128]{3,2,1,0:T(8,128)(2,1)}), bf16[8,3,192,128]{3,2,1,0:T(8,128)(2,1)}, u32[]{:S(2)}, u32[]{:S(2)}) async-start(bf16[8,3,192,128]{3,2,1,0:T(8,128)(2,1)} %copy-done.8), calls=%async_computation.4 | async-start | bytes 2359296 | tf_op jit(solution)/shard_map/all_to_all | solution.py:469
  157.9 21.0 %collective-permute-start.15 = (bf16[1,864,256]{2,1,0:T(8,128)(2,1)}, bf16[1,864,256]{2,1,0:T(8,128)(2,1)S(1)}, u32[]{:S(2)}, u32[]{:S(2)}) collective-permute-start(bf16[1,864,256]{2,1,0:T(8,128)(2,1)} %copy-done.16), channel_id=1, source_target_pairs={{8,0},{16,8},{24,16},{32,24},{40,32},{48,40},{56,48},{64,56},{72,6... | collective-permute-start | bytes 1327112 | tf_op jit(solution)/shard_map/ppermute | solution.py:448
  162.1 16.9 %copy-start.3 = (f32[1,4,384,256]{3,2,1,0:T(8,128)S(1)}, f32[1,4,384,256]{3,2,1,0:T(8,128)}, u32[]{:S(2)}) copy-start(f32[1,4,384,256]{3,2,1,0:T(8,128)} %copy-done.2) | copy-start | bytes 4718596
  162.1 16.9 %collective-permute-start.16 = (bf16[1,192,256]{2,1,0:T(8,128)(2,1)}, bf16[1,192,256]{2,1,0:T(8,128)(2,1)S(1)}, u32[]{:S(2)}, u32[]{:S(2)}) collective-permute-start(bf16[1,192,256]{2,1,0:T(8,128)(2,1)} %get-tuple-element.57), channel_id=1, source_target_pairs={{16,0},{24,8},{32,16},{40,24},{48,32},{56,40},{64,48},{72,56},{80,... | collective-permute-start | bytes 294920 | tf_op jit(solution)/shard_map/ppermute | solution.py:448
  167.3 11.7 %copy-start.12 = (bf16[1,4,384,128]{3,2,1,0:T(8,128)(2,1)S(1)}, bf16[1,4,384,128]{3,2,1,0:T(8,128)(2,1)}, u32[]{:S(2)}) copy-start(bf16[1,4,384,128]{3,2,1,0:T(8,128)(2,1)} %copy-done.11) | copy-start | bytes 1179652
  183.4 5.0 %copy-start.18 = (bf16[1,864,256]{2,1,0:T(8,128)(2,1)S(1)}, bf16[1,864,256]{2,1,0:T(8,128)(2,1)}, u32[]{:S(2)}) copy-start(bf16[1,864,256]{2,1,0:T(8,128)(2,1)} %copy-done.17) | copy-start | bytes 1327108
  183.4 6.9 %copy-start.25 = (bf16[1,192,256]{2,1,0:T(8,128)(2,1)S(1)}, bf16[1,192,256]{2,1,0:T(8,128)(2,1)}, u32[]{:S(2)}) copy-start(bf16[1,192,256]{2,1,0:T(8,128)(2,1)} %copy-done.24) | copy-start | bytes 294916
  183.4 23.9 %copy-start.5 = (f32[1,4,384,256]{3,2,1,0:T(8,128)S(1)}, f32[1,4,384,256]{3,2,1,0:T(8,128)}, u32[]{:S(2)}) copy-start(f32[1,4,384,256]{3,2,1,0:T(8,128)} %copy-done.4) | copy-start | bytes 4718596
  183.4 27.3 %all-to-all-start.6 = ((bf16[8,3,192,128]{3,2,1,0:T(8,128)(2,1)}), bf16[8,3,192,128]{3,2,1,0:T(8,128)(2,1)}, u32[]{:S(2)}, u32[]{:S(2)}) async-start(bf16[8,3,192,128]{3,2,1,0:T(8,128)(2,1)} %joined.6.refs_0_), calls=%async_computation.6 | async-start | bytes 2359296 | tf_op jit(solution)/shard_map/all_to_all | solution.py:469
  188.4 19.0 %collective-permute-start.13 = (bf16[1,864,256]{2,1,0:T(8,128)(2,1)S(1)}, bf16[1,864,256]{2,1,0:T(8,128)(2,1)S(1)}, u32[]{:S(2)}, u32[]{:S(2)}) collective-permute-start(bf16[1,864,256]{2,1,0:T(8,128)(2,1)S(1)} %copy-done.18), channel_id=1, source_target_pairs={{8,0},{16,8},{24,16},{32,24},{40,32},{48,40},{56,48},{64,56},{72,6... | collective-permute-start | bytes 1327112 | tf_op jit(solution)/shard_map/ppermute | solution.py:448
  190.3 17.0 %collective-permute-start.14 = (bf16[1,192,256]{2,1,0:T(8,128)(2,1)S(1)}, bf16[1,192,256]{2,1,0:T(8,128)(2,1)S(1)}, u32[]{:S(2)}, u32[]{:S(2)}) collective-permute-start(bf16[1,192,256]{2,1,0:T(8,128)(2,1)S(1)} %copy-done.25), channel_id=1, source_target_pairs={{16,0},{24,8},{32,16},{40,24},{48,32},{56,40},{64,48},{72,56},{80,... | collective-permute-start | bytes 294920 | tf_op jit(solution)/shard_map/ppermute | solution.py:448
  210.7 21.9 %all-to-all-start.5 = ((bf16[8,3,192,128]{3,2,1,0:T(8,128)(2,1)}), bf16[8,3,192,128]{3,2,1,0:T(8,128)(2,1)S(1)}, u32[]{:S(2)}, u32[]{:S(2)}) async-start(bf16[8,3,192,128]{3,2,1,0:T(8,128)(2,1)} %copy-done.10), calls=%async_computation.5 | async-start | bytes 2359296 | tf_op jit(solution)/shard_map/all_to_all | solution.py:469
  (21 other events, 27.0 us)

commit v3 on v2

v3 whole, which is shorter than its diff:
```python
import functools
import math

import jax
import jax.numpy as jnp
from jax import lax
from jax.experimental import pallas as pl
from jax.experimental.pallas import tpu as pltpu
from jax.sharding import Mesh, PartitionSpec as P

HD = 128
BLK = 384
HALF = 192
LEVELS = 4
LINE = 8
GROUP = 4
PAIR = 2
NEG = -1e30
COST = 30
SCALE = HD**-0.5
LOG2E = math.log2(math.e)
NEXT_L1 = BLK
NEXT_L2 = BLK + BLK // 2
NEXT_ROWS = NEXT_L2 + 3 * (BLK // 4)
FAR_ROWS = GROUP * (BLK // 8)
KEYS = BLK + BLK + BLK // 2 + BLK // 4 + BLK // 8
SEG = [0, BLK, 2 * BLK, 2 * BLK + BLK // 2, 2 * BLK + BLK // 2 + BLK // 4, KEYS]
OWN, NXT, AFT = 16, 32, 48
LINE_AXES = ("yh", "core", "yl")
GROUP_AXES = ("z", "x")
F32 = jnp.float32
BF16 = jnp.bfloat16


def dot(a, b, dims):
    return lax.dot_general(a, b, ((dims[0], dims[1]), ((), ())), preferred_element_type=F32)


def picker(stride, phase):
    rows = BLK // stride
    row = lax.broadcasted_iota(jnp.int32, (rows, BLK), 0)
    col = lax.broadcasted_iota(jnp.int32, (rows, BLK), 1)
    return jnp.where(col == row * stride + (phase & (stride - 1)), 1.0, 0.0).astype(BF16)


def spreader(stride, phase):
    cols = BLK // stride
    row = lax.broadcasted_iota(jnp.int32, (BLK, cols), 0)
    col = lax.broadcasted_iota(jnp.int32, (BLK, cols), 1)
    return jnp.where(row == col * stride + (phase & (stride - 1)), 1.0, 0.0).astype(BF16)


def pick(stride, phase, rows):
    return dot(picker(stride, phase), rows, ((1,), (0,))).astype(BF16)


def spread(stride, phase, rows):
    return dot(spreader(stride, phase), rows, ((1,), (0,)))


def kv_of(y_ref, block):
    at = slice(2 * block, 2 * block + 2)
    return jnp.concatenate([y_ref[at, 0].reshape(BLK, HD), y_ref[at, 1].reshape(BLK, HD)], axis=1)


def send_kernel(meta, y_ref, near_ref, far_ref):
    for h in range(PAIR):
        y = y_ref.at[:, :, :, h * HD : (h + 1) * HD]
        near_ref[h, 0:BLK] = kv_of(y, 3)
        near_ref[h, NEXT_L1:NEXT_L2] = pick(2, meta[NXT + 1], kv_of(y, 2))
        for b in range(3):
            lo = NEXT_L2 + b * 96
            near_ref[h, lo : lo + 96] = pick(4, meta[NXT + 4 * b + 2], kv_of(y, b))
        for b in range(GROUP):
            far_ref[h, 48 * b : 48 * b + 48] = pick(8, meta[AFT + 4 * b + 3], kv_of(y, b))


def emit(pieces):
    for piece in pieces:
        piece()


def main_kernel(meta, y_ref, w_ref, next_ref, far_ref, *refs):
    dq_ref, acc_ref, rnext_ref, rfar_ref, kvs, ss, dps, ps, dss, prev = refs[-10:]

    def q_of(b):
        return w_ref[2 * b : 2 * b + 2, 0].reshape(BLK, HD)

    def g_of(b):
        return w_ref[2 * b : 2 * b + 2, 1].reshape(BLK, HD)

    def gather(b):
        kv = kvs.at[b % 2]
        last = [None, lambda: next_ref[0, 0:BLK]] + [functools.partial(kv_of, y_ref, i) for i in range(b + 1)]
        own, one, two = last[b + 2], last[b + 1], last[b]
        kv[0:BLK] = own()
        kv[SEG[1] : SEG[2]] = one()
        if two is None:
            kv[SEG[2] : SEG[3]] = next_ref[0, NEXT_L1:NEXT_L2]
        else:
            kv[SEG[2] : SEG[3]] = pick(2, meta[OWN + 4 * b + 1], two())
        if b < 3:
            kv[SEG[3] : SEG[4]] = next_ref[0, NEXT_L2 + 96 * b : NEXT_L2 + 96 * b + 96]
        else:
            kv[SEG[3] : SEG[4]] = pick(4, meta[OWN + 4 * b + 2], next_ref[0, 0:BLK])
        kv[SEG[4] : SEG[5]] = far_ref[0, 48 * b : 48 * b + 48]

    def products(b):
        kv, s, dp = kvs.at[b % 2], ss.at[b % 2], dps.at[b % 2]
        yield lambda: gather(b)

        def tile(lo, hi, which):
            if which:
                dp[lo:hi] = dot(kv[lo:hi, HD:], g_of(b), ((1,), (1,)))
            else:
                s[lo:hi] = dot(kv[lo:hi, :HD], q_of(b), ((1,), (1,)))

        for which in (0, 1):
            for lo, hi in ((0, BLK), (BLK, KEYS)):
                yield functools.partial(tile, lo, hi, which)

    def softmax(b):
        s, dp, p, ds = ss.at[b % 2], dps.at[b % 2], ps.at[b % 2], dss.at[b % 2]
        biases = [None] + [jnp.where(meta[4 * b + k] == 1, 0.0, NEG).astype(F32) for k in range(LEVELS)]
        row = lax.broadcasted_iota(jnp.int32, (128, 128), 0)
        col = lax.broadcasted_iota(jnp.int32, (128, 128), 1)
        upper = row <= col
        c = SCALE * LOG2E
        for i in range(3):
            lanes = slice(128 * i, 128 * i + 128)
            tiles = [(128 * j, 128 * j + 128, 0) for j in range(i + 1)]
            tiles += [(BLK + 128 * j, BLK + 128 * j + 128, 1) for j in range(3)]
            tiles += [(SEG[2], SEG[2] + 96, 2), (SEG[2] + 96, SEG[3], 2), (SEG[3], SEG[4], 3), (SEG[4], SEG[5], 4)]
            st = dict(m=None, total=None, delta=None)

            def top(lo, hi, seg, i=i, lanes=lanes, st=st):
                t = s[lo:hi, lanes]
                if seg == 0 and lo == 128 * i:
                    t = jnp.where(upper, t, NEG)
                t = jnp.max(t, axis=0, keepdims=True)
                if biases[seg] is not None:
                    t = t + biases[seg]
                st["m"] = t if st["m"] is None else jnp.maximum(st["m"], t)

            def exps(lo, hi, seg, i=i, lanes=lanes, st=st):
                m = st["m"] * c
                shift = m if biases[seg] is None else m - biases[seg]
                t = s[lo:hi, lanes] * c - shift
                if seg == 0 and lo == 128 * i:
                    t = jnp.where(upper, t, NEG)
                e = jnp.exp2(t)
                s[lo:hi, lanes] = e
                total = jnp.sum(e, axis=0, keepdims=True)
                delta = jnp.sum(e * dp[lo:hi, lanes], axis=0, keepdims=True)
                st["total"] = total if st["total"] is None else st["total"] + total
                st["delta"] = delta if st["delta"] is None else st["delta"] + delta

            def norm(st=st):
                st["inv"] = 1.0 / st["total"]
                st["delta"] = st["delta"] * st["inv"]

            def scores(lo, hi, lanes=lanes, st=st):
                prob = s[lo:hi, lanes] * st["inv"]
                p[lo:hi, lanes] = prob.astype(BF16)
                ds[lo:hi, lanes] = (prob * (dp[lo:hi, lanes] - st["delta"])).astype(BF16)

            for lo, hi, seg in tiles:
                yield functools.partial(top, lo, hi, seg)
            for lo, hi, seg in tiles:
                yield functools.partial(exps, lo, hi, seg)
            yield norm
            for lo, hi, seg in tiles:
                yield functools.partial(scores, lo, hi)

    def gradients(b):
        kv, p, ds = kvs.at[b % 2], ps.at[b % 2], dss.at[b % 2]

        def queries():
            dq_ref[0, b] = (dot(ds[...], kv[:, :HD], ((0,), (0,))) * SCALE).astype(BF16)

        def pair(lo, hi):
            dk = dot(ds[lo:hi], q_of(b), ((1,), (0,))) * SCALE
            dv = dot(p[lo:hi], g_of(b), ((1,), (0,)))
            return jnp.concatenate([dk, dv], axis=1)

        def own():
            acc_ref[0, b] = pair(0, BLK)

        def near():
            term = pair(BLK, 2 * BLK)
            if b == 0:
                prev[...] = term
            else:
                acc_ref[0, b - 1] += term

        def two():
            term = pair(SEG[2], SEG[3]).astype(BF16)
            if b == 0:
                rnext_ref[0, NEXT_L1:NEXT_L2] = term
            elif b == 1:
                prev[...] += spread(2, meta[OWN + 4 * b + 1], term)
            else:
                acc_ref[0, b - 2] += spread(2, meta[OWN + 4 * b + 1], term)

        def four():
            term = pair(SEG[3], SEG[4]).astype(BF16)
            if b < 3:
                rnext_ref[0, NEXT_L2 + 96 * b : NEXT_L2 + 96 * b + 96] = term
            else:
                rnext_ref[0, 0:BLK] = (prev[...] + spread(4, meta[OWN + 4 * b + 2], term)).astype(BF16)

        def eight():
            rfar_ref[0, 48 * b : 48 * b + 48] = pair(SEG[4], SEG[5]).astype(BF16)

        yield own
        yield near
        yield two
        yield four
        yield eight
        yield queries

    for i in range(2):
        ps[i, 0:BLK] = jnp.zeros((BLK, BLK), BF16)
        dss[i, 0:BLK] = jnp.zeros((BLK, BLK), BF16)
    emit(products(0))
    for b in range(GROUP):
        emit(softmax(b))
        if b + 1 < GROUP:
            emit(products(b + 1))
        emit(gradients(b))


def join_kernel(meta, acc_ref, dq_ref, near_ref, far_ref, z_ref):
    for b in range(GROUP):
        t = acc_ref[0, b] + spread(8, meta[AFT + 4 * b + 3], far_ref[0, 48 * b : 48 * b + 48])
        if b < 3:
            lo = NEXT_L2 + 96 * b
            t = t + spread(4, meta[NXT + 4 * b + 2], near_ref[0, lo : lo + 96])
        if b == 2:
            t = t + spread(2, meta[NXT + 1], near_ref[0, NEXT_L1:NEXT_L2])
        if b == 3:
            t = t + near_ref[0, 0:BLK].astype(F32)
        at = slice(2 * b, 2 * b + 2)
        z_ref[at, 0] = dq_ref[0, b].reshape(2, HALF, HD)
        z_ref[at, 1] = t[:, :HD].astype(BF16).reshape(2, HALF, HD)
        z_ref[at, 2] = t[:, HD:].astype(BF16).reshape(2, HALF, HD)


def columns(pair, device):
    return pl.ds((pair * LINE + device) * PAIR * HD, PAIR * HD)


def pack_kernel(pair, count, *refs):
    arrays, x_ref, (held, ins, sems) = refs[:count], refs[-4], refs[-3:]
    width = LINE * PAIR * HD
    reads = [
        pltpu.make_async_copy(a.at[:, pl.ds(pair * width, width)], held.at[i], ins.at[i])
        for i, a in enumerate(arrays)
    ]
    for read in reads:
        read.start()
    writes = []
    for i, read in enumerate(reads):
        read.wait()
        for g in range(LINE):
            write = pltpu.make_async_copy(held.at[i, :, columns(0, g)], x_ref.at[g, i], sems.at[i, g])
            write.start()
            writes.append(write)
    for write in writes:
        write.wait()


def unpack_kernel(pair, w_ref, *refs):
    outs, (held, ins, sems) = refs[-6:-3], refs[-3:]
    reads = [pltpu.make_async_copy(w_ref.at[g], held.at[g], ins.at[g]) for g in range(LINE)]
    for read in reads:
        read.start()
    writes = []
    for g, read in enumerate(reads):
        read.wait()
        for i in range(3):
            write = pltpu.make_async_copy(held.at[g, i], outs[i].at[:, columns(pair, g)], sems.at[g, i])
            write.start()
            writes.append(write)
    for write in writes:
        write.wait()


SMEM = pl.BlockSpec(memory_space=pltpu.SMEM)
ANY = pl.BlockSpec(memory_space=pl.ANY)


def params(mib, axes=1):
    return pltpu.CompilerParams(
        dimension_semantics=("arbitrary",) * axes, vmem_limit_bytes=mib * 2**20
    )


def whole(shape):
    return pl.BlockSpec(shape, lambda b: (0,) * len(shape))


def y_spec(head, arrays):
    return pl.BlockSpec((LINE, 1, arrays, HALF, HD), lambda b: (0, head, 0, 0, 0))


def cost(flops, size, exps=0):
    return pl.CostEstimate(flops=int(flops), bytes_accessed=int(size), transcendentals=int(exps))


NEAR = (PAIR, NEXT_ROWS, 2 * HD)
FAR = (PAIR, FAR_ROWS, 2 * HD)


def a_head(shape):
    return pl.BlockSpec((1, *shape[1:]), lambda h: (h,) + (0,) * (len(shape) - 1))


def lanes_of(arrays, first):
    return pl.BlockSpec((LINE, arrays, HALF, HD), lambda h: (0, first // arrays, 0, h))


def packed(arrays, pair, after=()):
    count = len(arrays)
    return pl.pallas_call(
        functools.partial(pack_kernel, pair, count),
        in_specs=[ANY] * (count + len(after)),
        out_specs=ANY,
        out_shape=jax.ShapeDtypeStruct((LINE, count, HALF, PAIR * HD), BF16),
        scratch_shapes=[
            pltpu.VMEM((count, HALF, LINE * PAIR * HD), BF16),
            pltpu.SemaphoreType.DMA((count,)),
            pltpu.SemaphoreType.DMA((count, LINE)),
        ],
        compiler_params=pltpu.CompilerParams(vmem_limit_bytes=60 * 2**20),
        cost_estimate=cost(0, 2**23),
        name="packed",
    )(*arrays, *after)


def unpacked(w, pair, into):
    into = tuple(into)
    return pl.pallas_call(
        functools.partial(unpack_kernel, pair),
        in_specs=[ANY] * (1 + len(into)),
        out_specs=[ANY] * 3,
        out_shape=[jax.ShapeDtypeStruct((HALF, 2 * LINE * PAIR * HD), BF16)] * 3,
        input_output_aliases={1 + i: i for i in range(len(into))},
        scratch_shapes=[
            pltpu.VMEM((LINE, 3, HALF, PAIR * HD), BF16),
            pltpu.SemaphoreType.DMA((LINE,)),
            pltpu.SemaphoreType.DMA((LINE, 3)),
        ],
        compiler_params=pltpu.CompilerParams(vmem_limit_bytes=8 * 2**20),
        cost_estimate=cost(0, 2**23),
        name="unpacked",
    )(w, *into)


def rows_to_send(meta, y):
    return pl.pallas_call(
        send_kernel,
        grid=(1,),
        in_specs=[SMEM, pl.BlockSpec((LINE, 2, HALF, PAIR * HD), lambda i: (0, 0, 0, 0))],
        out_specs=[whole(NEAR), whole(FAR)],
        out_shape=[jax.ShapeDtypeStruct(NEAR, BF16), jax.ShapeDtypeStruct(FAR, BF16)],
        compiler_params=params(32),
        cost_estimate=cost(2**28, 2**22),
        name="rows_to_send",
    )(meta, y)


def attention(meta, y, w, first, near, far, after=()):
    sums = (PAIR, GROUP, BLK, 2 * HD)
    queries = (PAIR, GROUP, BLK, HD)
    return pl.pallas_call(
        main_kernel,
        grid=(PAIR,),
        in_specs=[SMEM, lanes_of(2, 0), lanes_of(2, first), a_head(NEAR), a_head(FAR)] + [ANY] * len(after),
        out_specs=[a_head(queries), a_head(sums), a_head(NEAR), a_head(FAR)],
        out_shape=[
            jax.ShapeDtypeStruct(queries, BF16),
            jax.ShapeDtypeStruct(sums, F32),
            jax.ShapeDtypeStruct(NEAR, BF16),
            jax.ShapeDtypeStruct(FAR, BF16),
        ],
        scratch_shapes=[
            pltpu.VMEM((2, KEYS, 2 * HD), BF16),
            pltpu.VMEM((2, KEYS, BLK), F32),
            pltpu.VMEM((2, KEYS, BLK), F32),
            pltpu.VMEM((2, KEYS, BLK), BF16),
            pltpu.VMEM((2, KEYS, BLK), BF16),
            pltpu.VMEM((BLK, 2 * HD), F32),
        ],
        compiler_params=params(40),
        cost_estimate=cost(PAIR * GROUP * BLK * KEYS * HD * COST, 10 * 2**20, 0),
        name="attention",
    )(meta, y, w, near, far, *after)


def joined(meta, acc, dq, near, far, after=()):
    return pl.pallas_call(
        lambda *refs: join_kernel(*refs[:5], refs[-1]),
        grid=(PAIR,),
        in_specs=[SMEM, a_head(acc.shape), a_head(dq.shape), a_head(NEAR), a_head(FAR)] + [ANY] * len(after),
        out_specs=lanes_of(3, 0),
        out_shape=jax.ShapeDtypeStruct((LINE, 3, HALF, PAIR * HD), BF16),
        compiler_params=params(32),
        cost_estimate=cost(2**28, 2**22),
        name="joined",
    )(meta, acc, dq, near, far, *after)


def shift(value, steps):
    count = lax.axis_size(GROUP_AXES)
    pairs = [(i, i + steps) for i in range(count) if 0 <= i + steps < count]
    return lax.ppermute(value, GROUP_AXES, pairs)


def both(value, axis):
    other = lax.ppermute(value, axis, [(0, 1), (1, 0)])
    first = lax.axis_index(axis) == 0
    return jnp.stack([jnp.where(first, value, other), jnp.where(first, other, value)])


def rows_of(pattern, phase):
    own = jnp.concatenate([pattern, phase], axis=1)
    return jnp.concatenate([own, shift(own, -1), shift(own, -2)], axis=0)


def meta_of(rows):
    rows = both(both(rows, "core"), "yh").reshape(GROUP, 3, 2 * LEVELS)
    block = lax.axis_index(GROUP_AXES) * GROUP + jnp.arange(GROUP)
    distance = 2 ** jnp.arange(LEVELS)
    active = (rows[:, 0, :LEVELS] == 1) & (block[:, None] >= distance[None, :])
    phases = rows[:, :, LEVELS:].transpose(1, 0, 2)
    return jnp.concatenate([active.astype(jnp.int32).reshape(-1), phases.reshape(-1)])


def exchange(x):
    return lax.all_to_all(x, LINE_AXES, 0, 0, tiled=True)


def body(queries, keys, values, grad_out, pattern, phase):
    y0 = exchange(packed((keys, values, queries, grad_out), 0))
    rows = rows_of(pattern, phase)
    y1 = exchange(packed((keys, values), 1, (rows,)))
    meta = meta_of(rows)
    near0, far0 = rows_to_send(meta, y0)
    w1 = exchange(packed((queries, grad_out), 1, (near0,)))
    near1, far1 = rows_to_send(meta, y1)

    def grads(y, w, first, near, far, after=()):
        dq, acc, near, far = attention(meta, y, w, first, shift(near, 1), shift(far, 2), after)
        return acc, dq, shift(near, -1), shift(far, -2)

    g0 = grads(y0, y0, 2, near0, far0, (near1,))
    g1 = grads(y1, w1, 0, near1, far1, (g0[0],))
    z0 = joined(meta, *g0, (g1[0],))
    z1 = joined(meta, *g1, (z0,))
    out = unpacked(exchange(z0), 0, ())
    return tuple(unpacked(exchange(z1), 1, out))


def solution(mesh):
    sizes = (4, 4, 2, 2, 2)
    line = Mesh(mesh.devices.reshape(sizes), ("z", "x", "yh", "core", "yl"))
    ctx = ("z", "x", "yh", "core")
    tokens = P((*ctx, "yl"), None)
    return jax.shard_map(
        body,
        mesh=line,
        in_specs=(tokens,) * 4 + (P(ctx, None),) * 2,
        out_specs=(tokens,) * 3,
        check_vma=False,
    )
```

time: 241 us -> 222 us (0.921); the launches traced: 236 us -> 221 us
  waiting for transfers between devices: 61.9 us -> 87.9 us
  starting transfers between devices: 82.9 us -> 59.3 us
  Pallas kernels: 71.2 us -> 60.1 us
  local copies, waits for them, and re-layouts: 18.3 us -> 12 us
    all_to_all x7 -> x5, waiting for transfers between devices: 20.6 us -> 36.2 us  [exchange(): return lax.all_to_all(x, LINE_AXES, 0, 0, tiled=True)]
    ppermute x15 -> x10, starting transfers between devices: 47.6 us -> 33.5 us  [shift(): return lax.ppermute(value, GROUP_AXES, pairs)]
    pallas_call x16 -> x11, Pallas kernels: 71.2 us -> 60.1 us  [the longest x2 37.3 us: attention(): pl.pallas_call(main_kernel, grid=(PAIR,), in_specs=[SMEM, lanes_of(2, 0),...]
    all_to_all x7 -> x5, starting transfers between devices: 31.7 us -> 22.1 us  [exchange(): return lax.all_to_all(x, LINE_AXES, 0, 0, tiled=True)]
    ppermute x15 -> x10, waiting for transfers between devices: 20.9 us -> 30.3 us  [shift(): return lax.ppermute(value, GROUP_AXES, pairs)]
    unnamed x58 -> x30, local copies, waits for them, and re-layouts: 18 us -> 11.6 us
  transfers between devices with their start and end apart: 24 -> 17, of which waited for: 8 -> 8; matrix products, arithmetic and copies ran while one was open for 0% -> 0% of each run, Pallas kernels for 28% -> 23%
where the time goes in v3:
time: 222 us; the launch traced here: 221 us
  waiting for transfers between devices  87.9 us (40%)
  Pallas kernels  60.1 us (27%)
  starting transfers between devices  59.3 us (27%)
  local copies, waits for them, and re-layouts  12 us (5%)
    pallas_call x2, Pallas kernels, attention(): pl.pallas_call(main_kernel, grid=(PAIR,), in_specs=[SMEM, lanes_of(2, 0),...  37.3 us
    all_to_all x5, waiting for transfers between devices, exchange(): return lax.all_to_all(x, LINE_AXES, 0, 0, tiled=True)  36.2 us
    ppermute x10, starting transfers between devices, shift(): return lax.ppermute(value, GROUP_AXES, pairs)  33.5 us
    ppermute x10, waiting for transfers between devices, shift(): return lax.ppermute(value, GROUP_AXES, pairs)  30.3 us
    all_to_all x5, starting transfers between devices, exchange(): return lax.all_to_all(x, LINE_AXES, 0, 0, tiled=True)  22.1 us
    ppermute x2, waiting for transfers between devices, both(): other = lax.ppermute(value, axis, [(0, 1), (1, 0)])  21.4 us
    unnamed x30, local copies, waits for them, and re-layouts  11.6 us
    pallas_call x3, Pallas kernels, packed(): pl.pallas_call(functools.partial(pack_kernel, pair, count), in_specs=[ANY...  7.94 us
  transfers between devices with their start and end apart: 17, of which 8 were waited for; matrix products, arithmetic and copies ran while one was open for 0% of the time, Pallas kernels for 23%

profile of v3, /device:TPU:38, one launch (start us, length us, event | category | flops | bytes accessed | tf_op | source)
XLA Modules:
  0.0 220.8 jit_solution(13057074941751128251)
XLA Ops:
  0.6 3.1 %packed.4 = bf16[8,4,192,256]{3,2,1,0:T(8,128)(2,1)} custom-call(bf16[192,4096]{1,0:T(8,128)(2,1)} %refs_0_.4, bf16[192,4096]{1,0:T(8,128)(2,1)} %refs_1_.4, bf16[192,4096]{1,0:T(8,128)(2,1)} %refs_0_.5, bf16[192,4096]{1,0:T(8,128)(2,1)} %refs_1_.5), custom_call_target="tpu_custom_call" | custom-call | bytes 8388608 | tf_op jit(solution)/shard_map/packed/pallas_call | solution.py:325
  3.8 4.5 %all-to-all-start.1 = ((bf16[8,4,192,256]{3,2,1,0:T(8,128)(2,1)}), bf16[8,4,192,256]{3,2,1,0:T(8,128)(2,1)S(1)}, u32[]{:S(2)}, u32[]{:S(2)}) async-start(bf16[8,4,192,256]{3,2,1,0:T(8,128)(2,1)} %packed.4), calls=%async_computation.1 | async-start | bytes 6291456 | tf_op jit(solution)/shard_map/all_to_all | solution.py:441
  8.3 3.3 %collective-permute-start.1 = (s32[1,8]{1,0:T(1,128)S(1)}, s32[1,8]{1,0:T(1,128)S(1)}, u32[]{:S(2)}, u32[]{:S(2)}) collective-permute-start(s32[1,8]{1,0:T(1,128)S(1)} %pad_add_fusion.3), channel_id=1, source_target_pairs={{16,0},{24,8},{32,16},{40,24},{48,32},{56,40},{64,48},{72,56},{80,... | collective-permute-start | bytes 104 | tf_op jit(solution)/shard_map/ppermute | solution.py:417
  11.7 1.9 collective-permute-start
  13.7 2.5 %collective-permute-done.1 = s32[1,8]{1,0:T(1,128)S(1)} collective-permute-done((s32[1,8]{1,0:T(1,128)S(1)}, s32[1,8]{1,0:T(1,128)S(1)}, u32[]{:S(2)}, u32[]{:S(2)}) %collective-permute-start.1) | collective-permute-done | bytes 64 | tf_op jit(solution)/shard_map/ppermute | solution.py:417
  16.2 3.0 %collective-permute-done = s32[1,8]{1,0:T(1,128)S(1)} collective-permute-done((s32[1,8]{1,0:T(1,128)S(1)}, s32[1,8]{1,0:T(1,128)S(1)}, u32[]{:S(2)}, u32[]{:S(2)}) %collective-permute-start) | collective-permute-done | bytes 64 | tf_op jit(solution)/shard_map/ppermute | solution.py:417
  20.5 3.5 %collective-permute-start.3 = (s32[2,3,8]{2,1,0:T(4,128)S(1)}, s32[2,3,8]{2,1,0:T(4,128)S(1)}, u32[]{:S(2)}, u32[]{:S(2)}) collective-permute-start(s32[2,3,8]{2,1,0:T(4,128)S(1)} %pad_add_fusion.1), channel_id=1, source_target_pairs={{0,4},{4,0},{1,5},{5,1},{2,6},{6,2},{3,7},{7,3},{8,12},{12,8},{9,1... | collective-permute-start | bytes 584 | tf_op jit(solution)/shard_map/ppermute | solution.py:421
  24.2 2.4 %packed.3 = bf16[8,2,192,256]{3,2,1,0:T(8,128)(2,1)} custom-call(bf16[192,4096]{1,0:T(8,128)(2,1)} %refs_0_.4, bf16[192,4096]{1,0:T(8,128)(2,1)} %refs_1_.4, s32[3,8]{1,0:T(4,128)} %copy-done.12), custom_call_target="tpu_custom_call" | custom-call | bytes 8388608 | tf_op jit(solution)/shard_map/packed/pallas_call | solution.py:325
  26.6 20.2 %collective-permute-done.3 = s32[2,3,8]{2,1,0:T(4,128)S(1)} collective-permute-done((s32[2,3,8]{2,1,0:T(4,128)S(1)}, s32[2,3,8]{2,1,0:T(4,128)S(1)}, u32[]{:S(2)}, u32[]{:S(2)}) %collective-permute-start.3) | collective-permute-done | bytes 224 | tf_op jit(solution)/shard_map/ppermute | solution.py:421
  46.9 4.3 %all-to-all-start = ((bf16[8,2,192,256]{3,2,1,0:T(8,128)(2,1)}), bf16[8,2,192,256]{3,2,1,0:T(8,128)(2,1)}, u32[]{:S(2)}, u32[]{:S(2)}) async-start(bf16[8,2,192,256]{3,2,1,0:T(8,128)(2,1)} %packed.3), calls=%async_computation | async-start | bytes 3145728 | tf_op jit(solution)/shard_map/all_to_all | solution.py:441
  51.5 2.1 rows_to_send.2
  53.7 3.8 %collective-permute-start.6 = (bf16[2,864,256]{2,1,0:T(8,128)(2,1)}, bf16[2,864,256]{2,1,0:T(8,128)(2,1)}, u32[]{:S(2)}, u32[]{:S(2)}) collective-permute-start(bf16[2,864,256]{2,1,0:T(8,128)(2,1)} %get-tuple-element.18.refs_2_), channel_id=1, source_target_pairs={{0,8},{8,16},{16,24},{24,32},{32,40},{40,48},{48,56},{56,64},{64,7... | collective-permute-start | bytes 2654216 | tf_op jit(solution)/shard_map/ppermute | solution.py:417
  57.4 4.3 %collective-permute-start.7 = (bf16[2,192,256]{2,1,0:T(8,128)(2,1)}, bf16[2,192,256]{2,1,0:T(8,128)(2,1)S(1)}, u32[]{:S(2)}, u32[]{:S(2)}) collective-permute-start(bf16[2,192,256]{2,1,0:T(8,128)(2,1)} %get-tuple-element.21), channel_id=1, source_target_pairs={{0,16},{8,24},{16,32},{24,40},{32,48},{40,56},{48,64},{56,72},{64,... | collective-permute-start | bytes 589832 | tf_op jit(solution)/shard_map/ppermute | solution.py:417
  61.8 2.4 %packed.5 = bf16[8,2,192,256]{3,2,1,0:T(8,128)(2,1)} custom-call(bf16[192,4096]{1,0:T(8,128)(2,1)} %refs_0_.5, bf16[192,4096]{1,0:T(8,128)(2,1)} %refs_1_.5, bf16[2,864,256]{2,1,0:T(8,128)(2,1)} %get-tuple-element.18.refs_2_), custom_call_target="tpu_custom_call" | custom-call | bytes 8388608 | tf_op jit(solution)/shard_map/packed/pallas_call | solution.py:325
  64.2 8.6 %all-to-all-done.y_ref = bf16[8,2,192,256]{3,2,1,0:T(8,128)(2,1)} async-done(((bf16[8,2,192,256]{3,2,1,0:T(8,128)(2,1)}), bf16[8,2,192,256]{3,2,1,0:T(8,128)(2,1)}, u32[]{:S(2)}, u32[]{:S(2)}) %all-to-all-start) | async-done | bytes 1572896 | tf_op jit(solution)/shard_map/all_to_all | solution.py:441
  72.8 4.3 %all-to-all-start.2 = ((bf16[8,2,192,256]{3,2,1,0:T(8,128)(2,1)}), bf16[8,2,192,256]{3,2,1,0:T(8,128)(2,1)}, u32[]{:S(2)}, u32[]{:S(2)}) async-start(bf16[8,2,192,256]{3,2,1,0:T(8,128)(2,1)} %packed.5), calls=%async_computation.2 | async-start | bytes 3145728 | tf_op jit(solution)/shard_map/all_to_all | solution.py:441
  77.1 2.1 rows_to_send.3
  79.3 4.7 %collective-permute-start.5 = (bf16[2,192,256]{2,1,0:T(8,128)(2,1)S(1)}, bf16[2,192,256]{2,1,0:T(8,128)(2,1)S(1)}, u32[]{:S(2)}, u32[]{:S(2)}) collective-permute-start(bf16[2,192,256]{2,1,0:T(8,128)(2,1)S(1)} %get-tuple-element.20), channel_id=1, source_target_pairs={{0,16},{8,24},{16,32},{24,40},{32,48},{40,56},{48,64},{56,72},{64,... | collective-permute-start | bytes 589832 | tf_op jit(solution)/shard_map/ppermute | solution.py:417
  84.0 4.2 %collective-permute-start.4 = (bf16[2,864,256]{2,1,0:T(8,128)(2,1)S(1)}, bf16[2,864,256]{2,1,0:T(8,128)(2,1)S(1)}, u32[]{:S(2)}, u32[]{:S(2)}) collective-permute-start(bf16[2,864,256]{2,1,0:T(8,128)(2,1)S(1)} %get-tuple-element.19.refs_0_), channel_id=1, source_target_pairs={{0,8},{8,16},{16,24},{24,32},{32,40},{40,48},{48,56},{56,64},{64,7... | collective-permute-start | bytes 2654216 | tf_op jit(solution)/shard_map/ppermute | solution.py:417
  88.2 18.7 %attention.2 = (bf16[2,4,384,128]{3,2,1,0:T(8,128)(2,1)S(1)}, f32[2,4,384,256]{3,2,1,0:T(8,128)S(1)}, bf16[2,864,256]{2,1,0:T(8,128)(2,1)}, bf16[2,192,256]{2,1,0:T(8,128)(2,1)}) custom-call(s32[64]{0:T(128)S(1)} %pad_add_fusion.4.meta.refs_0_, bf16[8,4,192,256]{3,2,1,0:T(8,128)(2,1)S(1)} %all-to-all-done.1.y_ref.w_ref, ...), custom_call_target="tpu_custom_call" | custom-call | flops 13023313920 | bytes 10485760 | tf_op jit(solution)/shard_map/attention/pallas_call | solution.py:376
  111.4 2.2 %collective-permute-start.10 = (bf16[2,864,256]{2,1,0:T(8,128)(2,1)}, bf16[2,864,256]{2,1,0:T(8,128)(2,1)}, u32[]{:S(2)}, u32[]{:S(2)}) collective-permute-start(bf16[2,864,256]{2,1,0:T(8,128)(2,1)} %get-tuple-element.28), channel_id=1, source_target_pairs={{8,0},{16,8},{24,16},{32,24},{40,32},{48,40},{56,48},{64,56},{72,6... | collective-permute-start | bytes 2654216 | tf_op jit(solution)/shard_map/ppermute | solution.py:417
  117.7 18.6 %attention.3 = (bf16[2,4,384,128]{3,2,1,0:T(8,128)(2,1)S(1)}, f32[2,4,384,256]{3,2,1,0:T(8,128)S(1)}, bf16[2,864,256]{2,1,0:T(8,128)(2,1)S(1)}, bf16[2,192,256]{2,1,0:T(8,128)(2,1)S(1)}) custom-call(s32[64]{0:T(128)S(1)} %pad_add_fusion.4.meta.refs_0_, bf16[8,2,192,256]{3,2,1,0:T(8,128)(2,1)} %all-to-all-done.y_ref, ...), custom_call_target="tpu_custom_call" | custom-call | flops 13023313920 | bytes 10485760 | tf_op jit(solution)/shard_map/attention/pallas_call | solution.py:376
  139.7 3.3 %joined.2.refs_5_ = bf16[8,3,192,256]{3,2,1,0:T(8,128)(2,1)} custom-call(s32[64]{0:T(128)S(1)} %pad_add_fusion.4.meta.refs_0_, f32[2,4,384,256]{3,2,1,0:T(8,128)S(1)} %copy-done.2, bf16[2,4,384,128]{3,2,1,0:T(8,128)(2,1)S(1)} %copy-done.6, bf16[2,864,256]{2,1,0:T(8,128)(2,1)} %collective-permute-done.10.refs_3_, ...), custom_call_target="tpu_custom_call" | custom-call | flops 268435456 | bytes 4194304 | tf_op jit(solution)/shard_map/joined/pallas_call | solution.py:402
  142.9 4.6 %all-to-all-start.4 = ((bf16[8,3,192,256]{3,2,1,0:T(8,128)(2,1)}), bf16[8,3,192,256]{3,2,1,0:T(8,128)(2,1)}, u32[]{:S(2)}, u32[]{:S(2)}) async-start(bf16[8,3,192,256]{3,2,1,0:T(8,128)(2,1)} %joined.2.refs_5_), calls=%async_computation.4 | async-start | bytes 4718592 | tf_op jit(solution)/shard_map/all_to_all | solution.py:441
  147.5 4.1 %collective-permute-start.8 = (bf16[2,864,256]{2,1,0:T(8,128)(2,1)}, bf16[2,864,256]{2,1,0:T(8,128)(2,1)S(1)}, u32[]{:S(2)}, u32[]{:S(2)}) collective-permute-start(bf16[2,864,256]{2,1,0:T(8,128)(2,1)} %copy-done.9), channel_id=1, source_target_pairs={{8,0},{16,8},{24,16},{32,24},{40,32},{48,40},{56,48},{64,56},{72,6... | collective-permute-start | bytes 2654216 | tf_op jit(solution)/shard_map/ppermute | solution.py:417
  151.7 3.1 %collective-permute-start.9 = (bf16[2,192,256]{2,1,0:T(8,128)(2,1)S(1)}, bf16[2,192,256]{2,1,0:T(8,128)(2,1)S(1)}, u32[]{:S(2)}, u32[]{:S(2)}) collective-permute-start(bf16[2,192,256]{2,1,0:T(8,128)(2,1)S(1)} %copy-done.11), channel_id=1, source_target_pairs={{16,0},{24,8},{32,16},{40,24},{48,32},{56,40},{64,48},{72,56},{80,... | collective-permute-start | bytes 589832 | tf_op jit(solution)/shard_map/ppermute | solution.py:417
  154.8 23.9 %collective-permute-done.9.refs_4_ = bf16[2,192,256]{2,1,0:T(8,128)(2,1)S(1)} collective-permute-done((bf16[2,192,256]{2,1,0:T(8,128)(2,1)S(1)}, bf16[2,192,256]{2,1,0:T(8,128)(2,1)S(1)}, u32[]{:S(2)}, u32[]{:S(2)}) %collective-permute-start.9) | collective-permute-done | bytes 196640 | tf_op jit(solution)/shard_map/ppermute | solution.py:417
  179.8 2.1 joined.3
  183.3 4.4 %all-to-all-start.3 = ((bf16[8,3,192,256]{3,2,1,0:T(8,128)(2,1)}), bf16[8,3,192,256]{3,2,1,0:T(8,128)(2,1)}, u32[]{:S(2)}, u32[]{:S(2)}) async-start(bf16[8,3,192,256]{3,2,1,0:T(8,128)(2,1)} %copy-done), calls=%async_computation.3 | async-start | bytes 4718592 | tf_op jit(solution)/shard_map/all_to_all | solution.py:441
  187.8 2.6 %unpacked.2 = (bf16[192,4096]{1,0:T(8,128)(2,1)}, bf16[192,4096]{1,0:T(8,128)(2,1)}, bf16[192,4096]{1,0:T(8,128)(2,1)}) custom-call(bf16[8,3,192,256]{3,2,1,0:T(8,128)(2,1)} %all-to-all-done.4.w_ref), custom_call_target="tpu_custom_call" | custom-call | bytes 8388608 | tf_op jit(solution)/shard_map/unpacked/pallas_call | solution.py:343
  190.4 27.5 %all-to-all-done.3.w_ref = bf16[8,3,192,256]{3,2,1,0:T(8,128)(2,1)} async-done(((bf16[8,3,192,256]{3,2,1,0:T(8,128)(2,1)}), bf16[8,3,192,256]{3,2,1,0:T(8,128)(2,1)}, u32[]{:S(2)}, u32[]{:S(2)}) %all-to-all-start.3) | async-done | bytes 2359328 | tf_op jit(solution)/shard_map/all_to_all | solution.py:441
  217.9 2.6 %unpacked.3 = (bf16[192,4096]{1,0:T(8,128)(2,1)}, bf16[192,4096]{1,0:T(8,128)(2,1)}, bf16[192,4096]{1,0:T(8,128)(2,1)}) custom-call(bf16[8,3,192,256]{3,2,1,0:T(8,128)(2,1)} %all-to-all-done.3.w_ref, bf16[192,4096]{1,0:T(8,128)(2,1)} %get-tuple-element.30.refs_0_, ...), custom_call_target="tpu_custom_call", output_to_operand_aliasing={{0}: (1, {}), {1}: (2, {}), {2}: (3, {})} | custom-call | bytes 8388608 | tf_op jit(solution)/shard_map/unpacked/pallas_call | solution.py:343
  (60 shorter events, 16.4 us)
Async XLA Ops:
  3.7 4.5 %copy-start.13 = (s32[1,4]{1,0:T(1,128)S(1)}, s32[1,4]{1,0:T(1,128)}, u32[]{:S(2)}) copy-start(s32[1,4]{1,0:T(1,128)} %param.11) | copy-start | bytes 52
  3.8 4.5 %copy-start.14 = (s32[1,4]{1,0:T(1,128)S(1)}, s32[1,4]{1,0:T(1,128)}, u32[]{:S(2)}) copy-start(s32[1,4]{1,0:T(1,128)} %param.10) | copy-start | bytes 52
  3.8 43.1 %all-to-all-start.1 = ((bf16[8,4,192,256]{3,2,1,0:T(8,128)(2,1)}), bf16[8,4,192,256]{3,2,1,0:T(8,128)(2,1)S(1)}, u32[]{:S(2)}, u32[]{:S(2)}) async-start(bf16[8,4,192,256]{3,2,1,0:T(8,128)(2,1)} %packed.4), calls=%async_computation.1 | async-start | bytes 6291456 | tf_op jit(solution)/shard_map/all_to_all | solution.py:441
  8.3 7.8 %collective-permute-start.1 = (s32[1,8]{1,0:T(1,128)S(1)}, s32[1,8]{1,0:T(1,128)S(1)}, u32[]{:S(2)}, u32[]{:S(2)}) collective-permute-start(s32[1,8]{1,0:T(1,128)S(1)} %pad_add_fusion.3), channel_id=1, source_target_pairs={{16,0},{24,8},{32,16},{40,24},{48,32},{56,40},{64,48},{72,56},{80,... | collective-permute-start | bytes 104 | tf_op jit(solution)/shard_map/ppermute | solution.py:417
  11.7 7.5 %collective-permute-start = (s32[1,8]{1,0:T(1,128)S(1)}, s32[1,8]{1,0:T(1,128)S(1)}, u32[]{:S(2)}, u32[]{:S(2)}) collective-permute-start(s32[1,8]{1,0:T(1,128)S(1)} %pad_add_fusion.3), channel_id=1, source_target_pairs={{8,0},{16,8},{24,16},{32,24},{40,32},{48,40},{56,48},{64,56},{72,6... | collective-permute-start | bytes 104 | tf_op jit(solution)/shard_map/ppermute | solution.py:417
  19.3 4.9 %copy-start.12 = (s32[3,8]{1,0:T(4,128)}, s32[3,8]{1,0:T(4,128)S(1)}, u32[]{:S(2)}) copy-start(s32[3,8]{1,0:T(4,128)S(1)} %pad_add_fusion.2.refs_2_) | copy-start | bytes 292
  19.3 1.2 collective-permute-start.2
  20.5 26.3 %collective-permute-start.3 = (s32[2,3,8]{2,1,0:T(4,128)S(1)}, s32[2,3,8]{2,1,0:T(4,128)S(1)}, u32[]{:S(2)}, u32[]{:S(2)}) collective-permute-start(s32[2,3,8]{2,1,0:T(4,128)S(1)} %pad_add_fusion.1), channel_id=1, source_target_pairs={{0,4},{4,0},{1,5},{5,1},{2,6},{6,2},{3,7},{7,3},{8,12},{12,8},{9,1... | collective-permute-start | bytes 584 | tf_op jit(solution)/shard_map/ppermute | solution.py:421
  46.9 25.9 %all-to-all-start = ((bf16[8,2,192,256]{3,2,1,0:T(8,128)(2,1)}), bf16[8,2,192,256]{3,2,1,0:T(8,128)(2,1)}, u32[]{:S(2)}, u32[]{:S(2)}) async-start(bf16[8,2,192,256]{3,2,1,0:T(8,128)(2,1)} %packed.3), calls=%async_computation | async-start | bytes 3145728 | tf_op jit(solution)/shard_map/all_to_all | solution.py:441
  53.7 34.5 %collective-permute-start.6 = (bf16[2,864,256]{2,1,0:T(8,128)(2,1)}, bf16[2,864,256]{2,1,0:T(8,128)(2,1)}, u32[]{:S(2)}, u32[]{:S(2)}) collective-permute-start(bf16[2,864,256]{2,1,0:T(8,128)(2,1)} %get-tuple-element.18.refs_2_), channel_id=1, source_target_pairs={{0,8},{8,16},{16,24},{24,32},{32,40},{40,48},{48,56},{56,64},{64,7... | collective-permute-start | bytes 2654216 | tf_op jit(solution)/shard_map/ppermute | solution.py:417
  57.4 30.7 %collective-permute-start.7 = (bf16[2,192,256]{2,1,0:T(8,128)(2,1)}, bf16[2,192,256]{2,1,0:T(8,128)(2,1)S(1)}, u32[]{:S(2)}, u32[]{:S(2)}) collective-permute-start(bf16[2,192,256]{2,1,0:T(8,128)(2,1)} %get-tuple-element.21), channel_id=1, source_target_pairs={{0,16},{8,24},{16,32},{24,40},{32,48},{40,56},{48,64},{56,72},{64,... | collective-permute-start | bytes 589832 | tf_op jit(solution)/shard_map/ppermute | solution.py:417
  72.8 41.8 %all-to-all-start.2 = ((bf16[8,2,192,256]{3,2,1,0:T(8,128)(2,1)}), bf16[8,2,192,256]{3,2,1,0:T(8,128)(2,1)}, u32[]{:S(2)}, u32[]{:S(2)}) async-start(bf16[8,2,192,256]{3,2,1,0:T(8,128)(2,1)} %packed.5), calls=%async_computation.2 | async-start | bytes 3145728 | tf_op jit(solution)/shard_map/all_to_all | solution.py:441
  79.3 34.4 %collective-permute-start.5 = (bf16[2,192,256]{2,1,0:T(8,128)(2,1)S(1)}, bf16[2,192,256]{2,1,0:T(8,128)(2,1)S(1)}, u32[]{:S(2)}, u32[]{:S(2)}) collective-permute-start(bf16[2,192,256]{2,1,0:T(8,128)(2,1)S(1)} %get-tuple-element.20), channel_id=1, source_target_pairs={{0,16},{8,24},{16,32},{24,40},{32,48},{40,56},{48,64},{56,72},{64,... | collective-permute-start | bytes 589832 | tf_op jit(solution)/shard_map/ppermute | solution.py:417
  84.0 29.7 %collective-permute-start.4 = (bf16[2,864,256]{2,1,0:T(8,128)(2,1)S(1)}, bf16[2,864,256]{2,1,0:T(8,128)(2,1)S(1)}, u32[]{:S(2)}, u32[]{:S(2)}) collective-permute-start(bf16[2,864,256]{2,1,0:T(8,128)(2,1)S(1)} %get-tuple-element.19.refs_0_), channel_id=1, source_target_pairs={{0,8},{8,16},{16,24},{24,32},{32,40},{40,48},{48,56},{56,64},{64,7... | collective-permute-start | bytes 2654216 | tf_op jit(solution)/shard_map/ppermute | solution.py:417
  106.9 1.7 copy-start.1
  108.6 1.0 copy-start.5
  109.5 29.2 %collective-permute-start.11 = (bf16[2,192,256]{2,1,0:T(8,128)(2,1)}, bf16[2,192,256]{2,1,0:T(8,128)(2,1)S(1)}, u32[]{:S(2)}, u32[]{:S(2)}) collective-permute-start(bf16[2,192,256]{2,1,0:T(8,128)(2,1)} %get-tuple-element.29), channel_id=1, source_target_pairs={{16,0},{24,8},{32,16},{40,24},{48,32},{56,40},{64,48},{72,56},{80,... | collective-permute-start | bytes 589832 | tf_op jit(solution)/shard_map/ppermute | solution.py:417
  111.4 28.2 %collective-permute-start.10 = (bf16[2,864,256]{2,1,0:T(8,128)(2,1)}, bf16[2,864,256]{2,1,0:T(8,128)(2,1)}, u32[]{:S(2)}, u32[]{:S(2)}) collective-permute-start(bf16[2,864,256]{2,1,0:T(8,128)(2,1)} %get-tuple-element.28), channel_id=1, source_target_pairs={{8,0},{16,8},{24,16},{32,24},{40,32},{48,40},{56,48},{64,56},{72,6... | collective-permute-start | bytes 2654216 | tf_op jit(solution)/shard_map/ppermute | solution.py:417
  113.7 0.9 copy-start.7
  114.6 1.9 copy-start.2
  116.5 1.2 copy-start.8
  117.7 22.0 %copy-start.6 = (bf16[2,4,384,128]{3,2,1,0:T(8,128)(2,1)S(1)}, bf16[2,4,384,128]{3,2,1,0:T(8,128)(2,1)}, u32[]{:S(2)}) copy-start(bf16[2,4,384,128]{3,2,1,0:T(8,128)(2,1)} %copy-done.5) | copy-start | bytes 2359300
  136.2 0.9 copy-start.3
  137.1 0.9 copy-start.9
  138.0 0.7 copy-start.10
  142.9 8.7 %copy-start.11 = (bf16[2,192,256]{2,1,0:T(8,128)(2,1)S(1)}, bf16[2,192,256]{2,1,0:T(8,128)(2,1)}, u32[]{:S(2)}) copy-start(bf16[2,192,256]{2,1,0:T(8,128)(2,1)} %copy-done.10) | copy-start | bytes 589828
  142.9 40.4 %all-to-all-start.4 = ((bf16[8,3,192,256]{3,2,1,0:T(8,128)(2,1)}), bf16[8,3,192,256]{3,2,1,0:T(8,128)(2,1)}, u32[]{:S(2)}, u32[]{:S(2)}) async-start(bf16[8,3,192,256]{3,2,1,0:T(8,128)(2,1)} %joined.2.refs_5_), calls=%async_computation.4 | async-start | bytes 4718592 | tf_op jit(solution)/shard_map/all_to_all | solution.py:441
  147.5 31.2 %collective-permute-start.8 = (bf16[2,864,256]{2,1,0:T(8,128)(2,1)}, bf16[2,864,256]{2,1,0:T(8,128)(2,1)S(1)}, u32[]{:S(2)}, u32[]{:S(2)}) collective-permute-start(bf16[2,864,256]{2,1,0:T(8,128)(2,1)} %copy-done.9), channel_id=1, source_target_pairs={{8,0},{16,8},{24,16},{32,24},{40,32},{48,40},{56,48},{64,56},{72,6... | collective-permute-start | bytes 2654216 | tf_op jit(solution)/shard_map/ppermute | solution.py:417
  151.7 27.0 %collective-permute-start.9 = (bf16[2,192,256]{2,1,0:T(8,128)(2,1)S(1)}, bf16[2,192,256]{2,1,0:T(8,128)(2,1)S(1)}, u32[]{:S(2)}, u32[]{:S(2)}) collective-permute-start(bf16[2,192,256]{2,1,0:T(8,128)(2,1)S(1)} %copy-done.11), channel_id=1, source_target_pairs={{16,0},{24,8},{32,16},{40,24},{48,32},{56,40},{64,48},{72,56},{80,... | collective-permute-start | bytes 589832 | tf_op jit(solution)/shard_map/ppermute | solution.py:417
  178.7 1.1 copy-start.4
  181.9 1.4 copy-start
  183.3 34.6 %all-to-all-start.3 = ((bf16[8,3,192,256]{3,2,1,0:T(8,128)(2,1)}), bf16[8,3,192,256]{3,2,1,0:T(8,128)(2,1)}, u32[]{:S(2)}, u32[]{:S(2)}) async-start(bf16[8,3,192,256]{3,2,1,0:T(8,128)(2,1)} %copy-done), calls=%async_computation.3 | async-start | bytes 4718592 | tf_op jit(solution)/shard_map/all_to_all | solution.py:441

commit v4 on v3

--- a/solution.py
+++ b/solution.py
@@ -176,7 +176,8 @@
         kv, p, ds = kvs.at[b % 2], ps.at[b % 2], dss.at[b % 2]
 
         def queries():
-            dq_ref[0, b] = (dot(ds[...], kv[:, :HD], ((0,), (0,))) * SCALE).astype(BF16)
+            part = dot(ds[...], kv[:, :HD], ((0,), (0,))) * SCALE
+            dq_ref[2 * b : 2 * b + 2] = part.astype(BF16).reshape(2, HALF, HD)
 
         def pair(lo, hi):
             dk = dot(ds[lo:hi], q_of(b), ((1,), (0,))) * SCALE
@@ -230,7 +231,9 @@
         emit(gradients(b))
 
 
-def join_kernel(meta, acc_ref, dq_ref, near_ref, far_ref, z_ref):
+def join_kernel(meta, acc_ref, near_ref, far_ref, *refs):
+    z_ref = refs[-1]
+    with_queries = z_ref.shape[1] == 3
     for b in range(GROUP):
         t = acc_ref[0, b] + spread(8, meta[AFT + 4 * b + 3], far_ref[0, 48 * b : 48 * b + 48])
         if b < 3:
@@ -241,9 +244,10 @@
         if b == 3:
             t = t + near_ref[0, 0:BLK].astype(F32)
         at = slice(2 * b, 2 * b + 2)
-        z_ref[at, 0] = dq_ref[0, b].reshape(2, HALF, HD)
-        z_ref[at, 1] = t[:, :HD].astype(BF16).reshape(2, HALF, HD)
-        z_ref[at, 2] = t[:, HD:].astype(BF16).reshape(2, HALF, HD)
+        if with_queries:
+            z_ref[at, 0] = refs[0][at]
+        z_ref[at, z_ref.shape[1] - 2] = t[:, :HD].astype(BF16).reshape(2, HALF, HD)
+        z_ref[at, z_ref.shape[1] - 1] = t[:, HD:].astype(BF16).reshape(2, HALF, HD)
 
 
 def columns(pair, device):
@@ -271,14 +275,15 @@
 
 
 def unpack_kernel(pair, w_ref, *refs):
-    outs, (held, ins, sems) = refs[-6:-3], refs[-3:]
+    (held, ins, sems), count = refs[-3:], w_ref.shape[1]
+    outs = refs[-3 - count : -3]
     reads = [pltpu.make_async_copy(w_ref.at[g], held.at[g], ins.at[g]) for g in range(LINE)]
     for read in reads:
         read.start()
     writes = []
     for g, read in enumerate(reads):
         read.wait()
-        for i in range(3):
+        for i in range(count):
             write = pltpu.make_async_copy(held.at[g, i], outs[i].at[:, columns(pair, g)], sems.at[g, i])
             write.start()
             writes.append(write)
@@ -314,6 +319,9 @@
 
 def a_head(shape):
     return pl.BlockSpec((1, *shape[1:]), lambda h: (h,) + (0,) * (len(shape) - 1))
+
+
+QUERY_GRADS = pl.BlockSpec((LINE, HALF, HD), lambda h: (0, 0, h))
 
 
 def lanes_of(arrays, first):
@@ -338,18 +346,18 @@
     )(*arrays, *after)
 
 
-def unpacked(w, pair, into):
-    into = tuple(into)
+def unpacked(w, pair, into=()):
+    into, count = tuple(into), w.shape[1]
     return pl.pallas_call(
         functools.partial(unpack_kernel, pair),
         in_specs=[ANY] * (1 + len(into)),
-        out_specs=[ANY] * 3,
-        out_shape=[jax.ShapeDtypeStruct((HALF, 2 * LINE * PAIR * HD), BF16)] * 3,
+        out_specs=[ANY] * count,
+        out_shape=[jax.ShapeDtypeStruct((HALF, 2 * LINE * PAIR * HD), BF16)] * count,
         input_output_aliases={1 + i: i for i in range(len(into))},
         scratch_shapes=[
-            pltpu.VMEM((LINE, 3, HALF, PAIR * HD), BF16),
+            pltpu.VMEM((LINE, count, HALF, PAIR * HD), BF16),
             pltpu.SemaphoreType.DMA((LINE,)),
-            pltpu.SemaphoreType.DMA((LINE, 3)),
+            pltpu.SemaphoreType.DMA((LINE, count)),
         ],
         compiler_params=pltpu.CompilerParams(vmem_limit_bytes=8 * 2**20),
         cost_estimate=cost(0, 2**23),
@@ -372,17 +380,16 @@
 
 def attention(meta, y, w, first, near, far, after=()):
     sums = (PAIR, GROUP, BLK, 2 * HD)
-    queries = (PAIR, GROUP, BLK, HD)
     return pl.pallas_call(
         main_kernel,
         grid=(PAIR,),
         in_specs=[SMEM, lanes_of(2, 0), lanes_of(2, first), a_head(NEAR), a_head(FAR)] + [ANY] * len(after),
-        out_specs=[a_head(queries), a_head(sums), a_head(NEAR), a_head(FAR)],
+        out_specs=[QUERY_GRADS, a_head(sums), a_head(NEAR), a_head(FAR)],
         out_shape=[
-            jax.ShapeDtypeStruct(queries, BF16),
-            jax.ShapeDtypeStruct(sums, F32),
-            jax.ShapeDtypeStruct(NEAR, BF16),
-            jax.ShapeDtypeStruct(FAR, BF16),
+            pltpu.HBM((LINE, HALF, PAIR * HD), BF16),
+            pltpu.HBM(sums, F32),
+            pltpu.HBM(NEAR, BF16),
+            pltpu.HBM(FAR, BF16),
         ],
         scratch_shapes=[
             pltpu.VMEM((2, KEYS, 2 * HD), BF16),
@@ -392,23 +399,26 @@
             pltpu.VMEM((2, KEYS, BLK), BF16),
             pltpu.VMEM((BLK, 2 * HD), F32),
         ],
-        compiler_params=params(40),
+        compiler_params=params(60),
         cost_estimate=cost(PAIR * GROUP * BLK * KEYS * HD * COST, 10 * 2**20, 0),
         name="attention",
     )(meta, y, w, near, far, *after)
 
 
-def joined(meta, acc, dq, near, far, after=()):
+def joined(meta, acc, near, far, queries=(), after=()):
+    arrays = 2 + len(queries)
     return pl.pallas_call(
-        lambda *refs: join_kernel(*refs[:5], refs[-1]),
+        join_kernel,
         grid=(PAIR,),
-        in_specs=[SMEM, a_head(acc.shape), a_head(dq.shape), a_head(NEAR), a_head(FAR)] + [ANY] * len(after),
-        out_specs=lanes_of(3, 0),
-        out_shape=jax.ShapeDtypeStruct((LINE, 3, HALF, PAIR * HD), BF16),
-        compiler_params=params(32),
-        cost_estimate=cost(2**28, 2**22),
+        in_specs=[SMEM, a_head(acc.shape), a_head(NEAR), a_head(FAR)]
+        + [QUERY_GRADS] * len(queries)
+        + [ANY] * len(after),
+        out_specs=lanes_of(arrays, 0),
+        out_shape=pltpu.HBM((LINE, arrays, HALF, PAIR * HD), BF16),
+        compiler_params=params(60),
+        cost_estimate=cost(2**36, 2**22),
         name="joined",
-    )(meta, acc, dq, near, far, *after)
+    )(meta, acc, near, far, *queries, *after)
 
 
 def shift(value, steps):
@@ -452,14 +462,16 @@
 
     def grads(y, w, first, near, far, after=()):
         dq, acc, near, far = attention(meta, y, w, first, shift(near, 1), shift(far, 2), after)
-        return acc, dq, shift(near, -1), shift(far, -2)
-
-    g0 = grads(y0, y0, 2, near0, far0, (near1,))
-    g1 = grads(y1, w1, 0, near1, far1, (g0[0],))
-    z0 = joined(meta, *g0, (g1[0],))
-    z1 = joined(meta, *g1, (z0,))
-    out = unpacked(exchange(z0), 0, ())
-    return tuple(unpacked(exchange(z1), 1, out))
+        return dq, (acc, shift(near, -1), shift(far, -2))
+
+    dq0, g0 = grads(y0, y0, 2, near0, far0, (near1,))
+    moved_q = exchange(dq0)
+    dq1, g1 = grads(y1, w1, 0, near1, far1, (dq0,))
+    z0 = joined(meta, *g0, (), (dq1, moved_q))
+    z1 = joined(meta, *g1, (dq1,), (z0,))
+    out_q = unpacked(moved_q[:, None], 0)
+    out_kv = unpacked(exchange(z0), 0)
+    return tuple(unpacked(exchange(z1), 1, (*out_q, *out_kv)))
 
 
 def solution(mesh):

time: 222 us -> 215 us (0.968)
  waiting for transfers between devices: 87.9 us -> 76.5 us
  local copies, waits for them, and re-layouts: 12 us -> 4.71 us
  Pallas kernels: 60.1 us -> 66.6 us
  starting transfers between devices: 59.3 us -> 64.2 us
    ppermute x10, waiting for transfers between devices: 30.3 us -> 18.9 us  [shift(): return lax.ppermute(value, GROUP_AXES, pairs)]
    unnamed x30, local copies, waits for them, and re-layouts: 11.6 us -> 4.36 us
    all_to_all x5 -> x6, starting transfers between devices: 22.1 us -> 26.2 us  [exchange(): return lax.all_to_all(x, LINE_AXES, 0, 0, tiled=True)]
    pallas_call x2, Pallas kernels: 5.33 us -> 7.64 us  [joined(): pl.pallas_call(join_kernel, grid=(PAIR,), in_specs=[SMEM, a_head(acc.shap...]
    pallas_call x2 -> x3, Pallas kernels: 5.25 us -> 7.53 us  [unpacked(): pl.pallas_call(functools.partial(unpack_kernel, pair), in_specs=[ANY] * (...]
    all_to_all x5 -> x6, waiting for transfers between devices: 36.2 us -> 36 us  [exchange(): return lax.all_to_all(x, LINE_AXES, 0, 0, tiled=True)]
  transfers between devices with their start and end apart: 17 -> 18, of which waited for: 8 -> 8; matrix products, arithmetic and copies ran while one was open for 0% -> 0% of each run, Pallas kernels for 23% -> 29%
where the time goes in v4:
time: 215 us; the launch traced here: 214 us
  waiting for transfers between devices  76.5 us (36%)
  Pallas kernels  66.6 us (31%)
  starting transfers between devices  64.2 us (30%)
  local copies, waits for them, and re-layouts  4.71 us (2%)
    pallas_call x2, Pallas kernels, attention(): pl.pallas_call(main_kernel, grid=(PAIR,), in_specs=[SMEM, lanes_of(2, 0),...  39.3 us
    all_to_all x6, waiting for transfers between devices, exchange(): return lax.all_to_all(x, LINE_AXES, 0, 0, tiled=True)  36 us
    ppermute x10, starting transfers between devices, shift(): return lax.ppermute(value, GROUP_AXES, pairs)  34.5 us
    all_to_all x6, starting transfers between devices, exchange(): return lax.all_to_all(x, LINE_AXES, 0, 0, tiled=True)  26.2 us
    ppermute x2, waiting for transfers between devices, both(): other = lax.ppermute(value, axis, [(0, 1), (1, 0)])  21.6 us
    ppermute x10, waiting for transfers between devices, shift(): return lax.ppermute(value, GROUP_AXES, pairs)  18.9 us
    pallas_call x3, Pallas kernels, packed(): pl.pallas_call(functools.partial(pack_kernel, pair, count), in_specs=[ANY...  7.92 us
    pallas_call x2, Pallas kernels, joined(): pl.pallas_call(join_kernel, grid=(PAIR,), in_specs=[SMEM, a_head(acc.shap...  7.64 us
  transfers between devices with their start and end apart: 18, of which 8 were waited for; matrix products, arithmetic and copies ran while one was open for 0% of the time, Pallas kernels for 29%

profile of v4, /device:TPU:38, one launch (start us, length us, event | category | flops | bytes accessed | tf_op | source)
XLA Modules:
  0.0 213.7 jit_solution(11765351489871591290)
XLA Ops:
  0.6 3.1 %packed.4 = bf16[8,4,192,256]{3,2,1,0:T(8,128)(2,1)} custom-call(bf16[192,4096]{1,0:T(8,128)(2,1)} %refs_0_.4, bf16[192,4096]{1,0:T(8,128)(2,1)} %refs_1_.4, bf16[192,4096]{1,0:T(8,128)(2,1)} %refs_0_.5, bf16[192,4096]{1,0:T(8,128)(2,1)} %refs_1_.5), custom_call_target="tpu_custom_call" | custom-call | bytes 8388608 | tf_op jit(solution)/shard_map/packed/pallas_call | solution.py:333
  3.8 4.5 %all-to-all-start.1 = ((bf16[8,4,192,256]{3,2,1,0:T(8,128)(2,1)}), bf16[8,4,192,256]{3,2,1,0:T(8,128)(2,1)S(1)}, u32[]{:S(2)}, u32[]{:S(2)}) async-start(bf16[8,4,192,256]{3,2,1,0:T(8,128)(2,1)} %packed.4), calls=%async_computation.1 | async-start | bytes 6291456 | tf_op jit(solution)/shard_map/all_to_all | solution.py:451
  8.3 2.7 %collective-permute-start = (s32[1,8]{1,0:T(1,128)S(1)}, s32[1,8]{1,0:T(1,128)S(1)}, u32[]{:S(2)}, u32[]{:S(2)}) collective-permute-start(s32[1,8]{1,0:T(1,128)S(1)} %pad_add_fusion.3), channel_id=1, source_target_pairs={{8,0},{16,8},{24,16},{32,24},{40,32},{48,40},{56,48},{64,56},{72,6... | collective-permute-start | bytes 104 | tf_op jit(solution)/shard_map/ppermute | solution.py:427
  11.1 3.0 %collective-permute-start.1 = (s32[1,8]{1,0:T(1,128)S(1)}, s32[1,8]{1,0:T(1,128)S(1)}, u32[]{:S(2)}, u32[]{:S(2)}) collective-permute-start(s32[1,8]{1,0:T(1,128)S(1)} %pad_add_fusion.3), channel_id=1, source_target_pairs={{16,0},{24,8},{32,16},{40,24},{48,32},{56,40},{64,48},{72,56},{80,... | collective-permute-start | bytes 104 | tf_op jit(solution)/shard_map/ppermute | solution.py:427
  15.9 3.0 %collective-permute-done.1 = s32[1,8]{1,0:T(1,128)S(1)} collective-permute-done((s32[1,8]{1,0:T(1,128)S(1)}, s32[1,8]{1,0:T(1,128)S(1)}, u32[]{:S(2)}, u32[]{:S(2)}) %collective-permute-start.1) | collective-permute-done | bytes 64 | tf_op jit(solution)/shard_map/ppermute | solution.py:427
  20.2 3.5 %collective-permute-start.3 = (s32[2,3,8]{2,1,0:T(4,128)S(1)}, s32[2,3,8]{2,1,0:T(4,128)S(1)}, u32[]{:S(2)}, u32[]{:S(2)}) collective-permute-start(s32[2,3,8]{2,1,0:T(4,128)S(1)} %pad_add_fusion.1), channel_id=1, source_target_pairs={{0,4},{4,0},{1,5},{5,1},{2,6},{6,2},{3,7},{7,3},{8,12},{12,8},{9,1... | collective-permute-start | bytes 584 | tf_op jit(solution)/shard_map/ppermute | solution.py:431
  23.9 2.4 %packed.3 = bf16[8,2,192,256]{3,2,1,0:T(8,128)(2,1)} custom-call(bf16[192,4096]{1,0:T(8,128)(2,1)} %refs_0_.4, bf16[192,4096]{1,0:T(8,128)(2,1)} %refs_1_.4, s32[3,8]{1,0:T(4,128)} %copy-done.7), custom_call_target="tpu_custom_call" | custom-call | bytes 8388608 | tf_op jit(solution)/shard_map/packed/pallas_call | solution.py:333
  26.3 20.5 %collective-permute-done.3 = s32[2,3,8]{2,1,0:T(4,128)S(1)} collective-permute-done((s32[2,3,8]{2,1,0:T(4,128)S(1)}, s32[2,3,8]{2,1,0:T(4,128)S(1)}, u32[]{:S(2)}, u32[]{:S(2)}) %collective-permute-start.3) | collective-permute-done | bytes 224 | tf_op jit(solution)/shard_map/ppermute | solution.py:431
  46.9 4.3 %all-to-all-start = ((bf16[8,2,192,256]{3,2,1,0:T(8,128)(2,1)}), bf16[8,2,192,256]{3,2,1,0:T(8,128)(2,1)}, u32[]{:S(2)}, u32[]{:S(2)}) async-start(bf16[8,2,192,256]{3,2,1,0:T(8,128)(2,1)} %packed.3), calls=%async_computation | async-start | bytes 3145728 | tf_op jit(solution)/shard_map/all_to_all | solution.py:451
  53.6 3.8 %collective-permute-start.6 = (bf16[2,864,256]{2,1,0:T(8,128)(2,1)}, bf16[2,864,256]{2,1,0:T(8,128)(2,1)}, u32[]{:S(2)}, u32[]{:S(2)}) collective-permute-start(bf16[2,864,256]{2,1,0:T(8,128)(2,1)} %get-tuple-element.17.refs_2_), channel_id=1, source_target_pairs={{0,8},{8,16},{16,24},{24,32},{32,40},{40,48},{48,56},{56,64},{64,7... | collective-permute-start | bytes 2654216 | tf_op jit(solution)/shard_map/ppermute | solution.py:427
  57.4 4.3 %collective-permute-start.7 = (bf16[2,192,256]{2,1,0:T(8,128)(2,1)S(1)}, bf16[2,192,256]{2,1,0:T(8,128)(2,1)S(1)}, u32[]{:S(2)}, u32[]{:S(2)}) collective-permute-start(bf16[2,192,256]{2,1,0:T(8,128)(2,1)S(1)} %get-tuple-element.20), channel_id=1, source_target_pairs={{0,16},{8,24},{16,32},{24,40},{32,48},{40,56},{48,64},{56,72},{64,... | collective-permute-start | bytes 589832 | tf_op jit(solution)/shard_map/ppermute | solution.py:427
  61.7 2.4 %packed.5 = bf16[8,2,192,256]{3,2,1,0:T(8,128)(2,1)} custom-call(bf16[192,4096]{1,0:T(8,128)(2,1)} %refs_0_.5, bf16[192,4096]{1,0:T(8,128)(2,1)} %refs_1_.5, bf16[2,864,256]{2,1,0:T(8,128)(2,1)} %get-tuple-element.17.refs_2_), custom_call_target="tpu_custom_call" | custom-call | bytes 8388608 | tf_op jit(solution)/shard_map/packed/pallas_call | solution.py:333
  64.1 8.7 %all-to-all-done.y_ref = bf16[8,2,192,256]{3,2,1,0:T(8,128)(2,1)} async-done(((bf16[8,2,192,256]{3,2,1,0:T(8,128)(2,1)}), bf16[8,2,192,256]{3,2,1,0:T(8,128)(2,1)}, u32[]{:S(2)}, u32[]{:S(2)}) %all-to-all-start) | async-done | bytes 1572896 | tf_op jit(solution)/shard_map/all_to_all | solution.py:451
  72.8 4.3 %all-to-all-start.2 = ((bf16[8,2,192,256]{3,2,1,0:T(8,128)(2,1)}), bf16[8,2,192,256]{3,2,1,0:T(8,128)(2,1)}, u32[]{:S(2)}, u32[]{:S(2)}) async-start(bf16[8,2,192,256]{3,2,1,0:T(8,128)(2,1)} %packed.5), calls=%async_computation.2 | async-start | bytes 3145728 | tf_op jit(solution)/shard_map/all_to_all | solution.py:451
  77.1 2.1 rows_to_send.3
  79.3 3.8 %collective-permute-start.4 = (bf16[2,864,256]{2,1,0:T(8,128)(2,1)S(1)}, bf16[2,864,256]{2,1,0:T(8,128)(2,1)}, u32[]{:S(2)}, u32[]{:S(2)}) collective-permute-start(bf16[2,864,256]{2,1,0:T(8,128)(2,1)S(1)} %get-tuple-element.18.refs_0_), channel_id=1, source_target_pairs={{0,8},{8,16},{16,24},{24,32},{32,40},{40,48},{48,56},{56,64},{64,7... | collective-permute-start | bytes 2654216 | tf_op jit(solution)/shard_map/ppermute | solution.py:427
  83.0 4.3 %collective-permute-start.5 = (bf16[2,192,256]{2,1,0:T(8,128)(2,1)S(1)}, bf16[2,192,256]{2,1,0:T(8,128)(2,1)S(1)}, u32[]{:S(2)}, u32[]{:S(2)}) collective-permute-start(bf16[2,192,256]{2,1,0:T(8,128)(2,1)S(1)} %get-tuple-element.19), channel_id=1, source_target_pairs={{0,16},{8,24},{16,32},{24,40},{32,48},{40,56},{48,64},{56,72},{64,... | collective-permute-start | bytes 589832 | tf_op jit(solution)/shard_map/ppermute | solution.py:427
  88.1 19.7 %attention.2 = (bf16[8,192,256]{2,1,0:T(8,128)(2,1)}, f32[2,4,384,256]{3,2,1,0:T(8,128)}, bf16[2,864,256]{2,1,0:T(8,128)(2,1)}, bf16[2,192,256]{2,1,0:T(8,128)(2,1)}) custom-call(s32[64]{0:T(128)} %copy-done.5, bf16[8,4,192,256]{3,2,1,0:T(8,128)(2,1)} %copy-done, bf16[8,4,192,256]{3,2,1,0:T(8,128)(2,1)} %copy-done, ...), custom_call_target="tpu_custom_call" | custom-call | flops 13023313920 | bytes 10485760 | tf_op jit(solution)/shard_map/attention/pallas_call | solution.py:383
  109.8 3.8 %collective-permute-start.11 = (bf16[2,192,256]{2,1,0:T(8,128)(2,1)}, bf16[2,192,256]{2,1,0:T(8,128)(2,1)S(1)}, u32[]{:S(2)}, u32[]{:S(2)}) collective-permute-start(bf16[2,192,256]{2,1,0:T(8,128)(2,1)} %get-tuple-element.28), channel_id=1, source_target_pairs={{16,0},{24,8},{32,16},{40,24},{48,32},{56,40},{64,48},{72,56},{80,... | collective-permute-start | bytes 589832 | tf_op jit(solution)/shard_map/ppermute | solution.py:427
  113.6 4.7 %all-to-all-start.3 = ((bf16[8,192,256]{2,1,0:T(8,128)(2,1)}), bf16[8,192,256]{2,1,0:T(8,128)(2,1)S(1)}, u32[]{:S(2)}, u32[]{:S(2)}) async-start(bf16[8,192,256]{2,1,0:T(8,128)(2,1)} %get-tuple-element.21.refs_0_), calls=%async_computation.3 | async-start | bytes 1572864 | tf_op jit(solution)/shard_map/all_to_all | solution.py:451
  119.0 19.6 %attention.3 = (bf16[8,192,256]{2,1,0:T(8,128)(2,1)}, f32[2,4,384,256]{3,2,1,0:T(8,128)}, bf16[2,864,256]{2,1,0:T(8,128)(2,1)}, bf16[2,192,256]{2,1,0:T(8,128)(2,1)}) custom-call(s32[64]{0:T(128)} %copy-done.5, bf16[8,2,192,256]{3,2,1,0:T(8,128)(2,1)} %all-to-all-done.y_ref, bf16[8,2,192,256]{3,2,1,0:T(8,128)(2,1)} %all-to-all-done.2.w_ref, ...), custom_call_target="tpu_custom_call" | custom-call | flops 13023313920 | bytes 10485760 | tf_op jit(solution)/shard_map/attention/pallas_call | solution.py:383
  138.6 3.6 %collective-permute-start.8 = (bf16[2,864,256]{2,1,0:T(8,128)(2,1)}, bf16[2,864,256]{2,1,0:T(8,128)(2,1)}, u32[]{:S(2)}, u32[]{:S(2)}) collective-permute-start(bf16[2,864,256]{2,1,0:T(8,128)(2,1)} %get-tuple-element.23), channel_id=1, source_target_pairs={{8,0},{16,8},{24,16},{32,24},{40,32},{48,40},{56,48},{64,56},{72,6... | collective-permute-start | bytes 2654216 | tf_op jit(solution)/shard_map/ppermute | solution.py:427
  142.3 3.0 %collective-permute-start.9 = (bf16[2,192,256]{2,1,0:T(8,128)(2,1)}, bf16[2,192,256]{2,1,0:T(8,128)(2,1)S(1)}, u32[]{:S(2)}, u32[]{:S(2)}) collective-permute-start(bf16[2,192,256]{2,1,0:T(8,128)(2,1)} %get-tuple-element.24), channel_id=1, source_target_pairs={{16,0},{24,8},{32,16},{40,24},{48,32},{56,40},{64,48},{72,56},{80,... | collective-permute-start | bytes 589832 | tf_op jit(solution)/shard_map/ppermute | solution.py:427
  146.6 3.6 %joined.2.refs_1_ = bf16[8,2,192,256]{3,2,1,0:T(8,128)(2,1)} custom-call(s32[64]{0:T(128)} %copy-done.5, f32[2,4,384,256]{3,2,1,0:T(8,128)} %get-tuple-element.26.acc_ref, bf16[2,864,256]{2,1,0:T(8,128)(2,1)} %copy-done.10, bf16[2,192,256]{2,1,0:T(8,128)(2,1)} %copy-done.11, bf16[8,192,256]{2,1,0:T(8,128)(2,1)} %get-tuple-element.25.refs_0_, ...), custom_call_target="tpu_custom_call" | custom-call | flops 68719476736 | bytes 4194304 | tf_op jit(solution)/shard_map/joined/pallas_call | solution.py:410
  150.2 4.8 %all-to-all-start.5 = ((bf16[8,2,192,256]{3,2,1,0:T(8,128)(2,1)}), bf16[8,2,192,256]{3,2,1,0:T(8,128)(2,1)S(1)}, u32[]{:S(2)}, u32[]{:S(2)}) async-start(bf16[8,2,192,256]{3,2,1,0:T(8,128)(2,1)} %joined.2.refs_1_), calls=%async_computation.5 | async-start | bytes 3145728 | tf_op jit(solution)/shard_map/all_to_all | solution.py:451
  155.0 14.2 %collective-permute-done.9.far_ref = bf16[2,192,256]{2,1,0:T(8,128)(2,1)S(1)} collective-permute-done((bf16[2,192,256]{2,1,0:T(8,128)(2,1)}, bf16[2,192,256]{2,1,0:T(8,128)(2,1)S(1)}, u32[]{:S(2)}, u32[]{:S(2)}) %collective-permute-start.9) | collective-permute-done | bytes 196640 | tf_op jit(solution)/shard_map/ppermute | solution.py:427
  169.9 4.0 %joined.3 = bf16[8,3,192,256]{3,2,1,0:T(8,128)(2,1)} custom-call(s32[64]{0:T(128)} %copy-done.5, f32[2,4,384,256]{3,2,1,0:T(8,128)} %get-tuple-element.22.acc_ref, bf16[2,864,256]{2,1,0:T(8,128)(2,1)} %collective-permute-done.8.near_ref, bf16[2,192,256]{2,1,0:T(8,128)(2,1)} %copy-done.14, bf16[8,192,256]{2,1,0:T(8,128)(2,1)} %get-tuple-element.25.refs_0_, ...), custom_call_target="tpu_custom_call" | custom-call | flops 68719476736 | bytes 4194304 | tf_op jit(solution)/shard_map/joined/pallas_call | solution.py:410
  173.9 2.8 %all-to-all-done.5.w_ref = bf16[8,2,192,256]{3,2,1,0:T(8,128)(2,1)S(1)} async-done(((bf16[8,2,192,256]{3,2,1,0:T(8,128)(2,1)}), bf16[8,2,192,256]{3,2,1,0:T(8,128)(2,1)S(1)}, u32[]{:S(2)}, u32[]{:S(2)}) %all-to-all-start.5) | async-done | bytes 1572896 | tf_op jit(solution)/shard_map/all_to_all | solution.py:451
  177.8 3.6 %all-to-all-start.4 = ((bf16[8,3,192,256]{3,2,1,0:T(8,128)(2,1)}), bf16[8,3,192,256]{3,2,1,0:T(8,128)(2,1)S(1)}, u32[]{:S(2)}, u32[]{:S(2)}) async-start(bf16[8,3,192,256]{3,2,1,0:T(8,128)(2,1)} %joined.3), calls=%async_computation.4 | async-start | bytes 4718592 | tf_op jit(solution)/shard_map/all_to_all | solution.py:451
  183.5 3.4 %unpacked.4 = (bf16[192,4096]{1,0:T(8,128)(2,1)}, bf16[192,4096]{1,0:T(8,128)(2,1)}) custom-call(bf16[8,2,192,256]{3,2,1,0:T(8,128)(2,1)S(1)} %copy-done.2), custom_call_target="tpu_custom_call" | custom-call | bytes 8388608 | tf_op jit(solution)/shard_map/unpacked/pallas_call | solution.py:351
  186.8 24.5 %all-to-all-done.4.w_ref = bf16[8,3,192,256]{3,2,1,0:T(8,128)(2,1)S(1)} async-done(((bf16[8,3,192,256]{3,2,1,0:T(8,128)(2,1)}), bf16[8,3,192,256]{3,2,1,0:T(8,128)(2,1)S(1)}, u32[]{:S(2)}, u32[]{:S(2)}) %all-to-all-start.4) | async-done | bytes 2359328 | tf_op jit(solution)/shard_map/all_to_all | solution.py:451
  211.4 2.1 %unpacked.5 = (bf16[192,4096]{1,0:T(8,128)(2,1)}, bf16[192,4096]{1,0:T(8,128)(2,1)}, bf16[192,4096]{1,0:T(8,128)(2,1)}) custom-call(bf16[8,3,192,256]{3,2,1,0:T(8,128)(2,1)S(1)} %all-to-all-done.4.w_ref, bf16[192,4096]{1,0:T(8,128)(2,1)} %unpacked.3.refs_0_, ...), custom_call_target="tpu_custom_call", output_to_operand_aliasing={{0}: (1, {}), {1}: (2, {}), {2}: (3, {})} | custom-call | bytes 8388608 | tf_op jit(solution)/shard_map/unpacked/pallas_call | solution.py:351
  (63 shorter events, 14.2 us)
Async XLA Ops:
  3.7 4.5 %copy-start.8 = (s32[1,4]{1,0:T(1,128)S(1)}, s32[1,4]{1,0:T(1,128)}, u32[]{:S(2)}) copy-start(s32[1,4]{1,0:T(1,128)} %param.11) | copy-start | bytes 52
  3.7 4.5 %copy-start.9 = (s32[1,4]{1,0:T(1,128)S(1)}, s32[1,4]{1,0:T(1,128)}, u32[]{:S(2)}) copy-start(s32[1,4]{1,0:T(1,128)} %param.10) | copy-start | bytes 52
  3.8 43.1 %all-to-all-start.1 = ((bf16[8,4,192,256]{3,2,1,0:T(8,128)(2,1)}), bf16[8,4,192,256]{3,2,1,0:T(8,128)(2,1)S(1)}, u32[]{:S(2)}, u32[]{:S(2)}) async-start(bf16[8,4,192,256]{3,2,1,0:T(8,128)(2,1)} %packed.4), calls=%async_computation.1 | async-start | bytes 6291456 | tf_op jit(solution)/shard_map/all_to_all | solution.py:451
  8.3 7.5 %collective-permute-start = (s32[1,8]{1,0:T(1,128)S(1)}, s32[1,8]{1,0:T(1,128)S(1)}, u32[]{:S(2)}, u32[]{:S(2)}) collective-permute-start(s32[1,8]{1,0:T(1,128)S(1)} %pad_add_fusion.3), channel_id=1, source_target_pairs={{8,0},{16,8},{24,16},{32,24},{40,32},{48,40},{56,48},{64,56},{72,6... | collective-permute-start | bytes 104 | tf_op jit(solution)/shard_map/ppermute | solution.py:427
  11.1 7.8 %collective-permute-start.1 = (s32[1,8]{1,0:T(1,128)S(1)}, s32[1,8]{1,0:T(1,128)S(1)}, u32[]{:S(2)}, u32[]{:S(2)}) collective-permute-start(s32[1,8]{1,0:T(1,128)S(1)} %pad_add_fusion.3), channel_id=1, source_target_pairs={{16,0},{24,8},{32,16},{40,24},{48,32},{56,40},{64,48},{72,56},{80,... | collective-permute-start | bytes 104 | tf_op jit(solution)/shard_map/ppermute | solution.py:427
  19.0 4.9 %copy-start.7 = (s32[3,8]{1,0:T(4,128)}, s32[3,8]{1,0:T(4,128)S(1)}, u32[]{:S(2)}) copy-start(s32[3,8]{1,0:T(4,128)S(1)} %pad_add_fusion.2.refs_2_) | copy-start | bytes 292
  19.0 1.2 collective-permute-start.2
  20.2 26.6 %collective-permute-start.3 = (s32[2,3,8]{2,1,0:T(4,128)S(1)}, s32[2,3,8]{2,1,0:T(4,128)S(1)}, u32[]{:S(2)}, u32[]{:S(2)}) collective-permute-start(s32[2,3,8]{2,1,0:T(4,128)S(1)} %pad_add_fusion.1), channel_id=1, source_target_pairs={{0,4},{4,0},{1,5},{5,1},{2,6},{6,2},{3,7},{7,3},{8,12},{12,8},{9,1... | collective-permute-start | bytes 584 | tf_op jit(solution)/shard_map/ppermute | solution.py:431
  46.9 4.7 %copy-start = (bf16[8,4,192,256]{3,2,1,0:T(8,128)(2,1)}, bf16[8,4,192,256]{3,2,1,0:T(8,128)(2,1)S(1)}, u32[]{:S(2)}) copy-start(bf16[8,4,192,256]{3,2,1,0:T(8,128)(2,1)S(1)} %all-to-all-done.1.y_ref.w_ref) | copy-start | bytes 9437188
  46.9 25.9 %all-to-all-start = ((bf16[8,2,192,256]{3,2,1,0:T(8,128)(2,1)}), bf16[8,2,192,256]{3,2,1,0:T(8,128)(2,1)}, u32[]{:S(2)}, u32[]{:S(2)}) async-start(bf16[8,2,192,256]{3,2,1,0:T(8,128)(2,1)} %packed.3), calls=%async_computation | async-start | bytes 3145728 | tf_op jit(solution)/shard_map/all_to_all | solution.py:451
  51.5 25.6 %copy-start.5 = (s32[64]{0:T(128)}, s32[64]{0:T(128)S(1)}, u32[]{:S(2)}) copy-start(s32[64]{0:T(128)S(1)} %pad_add_fusion.4.meta) | copy-start | bytes 772
  53.6 33.8 %collective-permute-start.6 = (bf16[2,864,256]{2,1,0:T(8,128)(2,1)}, bf16[2,864,256]{2,1,0:T(8,128)(2,1)}, u32[]{:S(2)}, u32[]{:S(2)}) collective-permute-start(bf16[2,864,256]{2,1,0:T(8,128)(2,1)} %get-tuple-element.17.refs_2_), channel_id=1, source_target_pairs={{0,8},{8,16},{16,24},{24,32},{32,40},{40,48},{48,56},{56,64},{64,7... | collective-permute-start | bytes 2654216 | tf_op jit(solution)/shard_map/ppermute | solution.py:427
  57.4 30.0 %collective-permute-start.7 = (bf16[2,192,256]{2,1,0:T(8,128)(2,1)S(1)}, bf16[2,192,256]{2,1,0:T(8,128)(2,1)S(1)}, u32[]{:S(2)}, u32[]{:S(2)}) collective-permute-start(bf16[2,192,256]{2,1,0:T(8,128)(2,1)S(1)} %get-tuple-element.20), channel_id=1, source_target_pairs={{0,16},{8,24},{16,32},{24,40},{32,48},{40,56},{48,64},{56,72},{64,... | collective-permute-start | bytes 589832 | tf_op jit(solution)/shard_map/ppermute | solution.py:427
  72.8 40.8 %all-to-all-start.2 = ((bf16[8,2,192,256]{3,2,1,0:T(8,128)(2,1)}), bf16[8,2,192,256]{3,2,1,0:T(8,128)(2,1)}, u32[]{:S(2)}, u32[]{:S(2)}) async-start(bf16[8,2,192,256]{3,2,1,0:T(8,128)(2,1)} %packed.5), calls=%async_computation.2 | async-start | bytes 3145728 | tf_op jit(solution)/shard_map/all_to_all | solution.py:451
  79.2 8.1 %copy-start.6 = (bf16[2,864,256]{2,1,0:T(8,128)(2,1)}, bf16[2,864,256]{2,1,0:T(8,128)(2,1)S(1)}, u32[]{:S(2)}) copy-start(bf16[2,864,256]{2,1,0:T(8,128)(2,1)S(1)} %get-tuple-element.18.refs_0_) | copy-start | bytes 2654212
  79.3 39.1 %collective-permute-start.4 = (bf16[2,864,256]{2,1,0:T(8,128)(2,1)S(1)}, bf16[2,864,256]{2,1,0:T(8,128)(2,1)}, u32[]{:S(2)}, u32[]{:S(2)}) collective-permute-start(bf16[2,864,256]{2,1,0:T(8,128)(2,1)S(1)} %get-tuple-element.18.refs_0_), channel_id=1, source_target_pairs={{0,8},{8,16},{16,24},{24,32},{32,40},{40,48},{48,56},{56,64},{64,7... | collective-permute-start | bytes 2654216 | tf_op jit(solution)/shard_map/ppermute | solution.py:427
  83.0 35.3 %collective-permute-start.5 = (bf16[2,192,256]{2,1,0:T(8,128)(2,1)S(1)}, bf16[2,192,256]{2,1,0:T(8,128)(2,1)S(1)}, u32[]{:S(2)}, u32[]{:S(2)}) collective-permute-start(bf16[2,192,256]{2,1,0:T(8,128)(2,1)S(1)} %get-tuple-element.19), channel_id=1, source_target_pairs={{0,16},{8,24},{16,32},{24,40},{32,48},{40,56},{48,64},{56,72},{64,... | collective-permute-start | bytes 589832 | tf_op jit(solution)/shard_map/ppermute | solution.py:427
  87.4 0.7 copy-start.13
  107.7 37.6 %collective-permute-start.10 = (bf16[2,864,256]{2,1,0:T(8,128)(2,1)}, bf16[2,864,256]{2,1,0:T(8,128)(2,1)S(1)}, u32[]{:S(2)}, u32[]{:S(2)}) collective-permute-start(bf16[2,864,256]{2,1,0:T(8,128)(2,1)} %get-tuple-element.27), channel_id=1, source_target_pairs={{8,0},{16,8},{24,16},{32,24},{40,32},{48,40},{56,48},{64,56},{72,6... | collective-permute-start | bytes 2654216 | tf_op jit(solution)/shard_map/ppermute | solution.py:427
  109.8 35.5 %collective-permute-start.11 = (bf16[2,192,256]{2,1,0:T(8,128)(2,1)}, bf16[2,192,256]{2,1,0:T(8,128)(2,1)S(1)}, u32[]{:S(2)}, u32[]{:S(2)}) collective-permute-start(bf16[2,192,256]{2,1,0:T(8,128)(2,1)} %get-tuple-element.28), channel_id=1, source_target_pairs={{16,0},{24,8},{32,16},{40,24},{48,32},{56,40},{64,48},{72,56},{80,... | collective-permute-start | bytes 589832 | tf_op jit(solution)/shard_map/ppermute | solution.py:427
  113.6 31.7 %all-to-all-start.3 = ((bf16[8,192,256]{2,1,0:T(8,128)(2,1)}), bf16[8,192,256]{2,1,0:T(8,128)(2,1)S(1)}, u32[]{:S(2)}, u32[]{:S(2)}) async-start(bf16[8,192,256]{2,1,0:T(8,128)(2,1)} %get-tuple-element.21.refs_0_), calls=%async_computation.3 | async-start | bytes 1572864 | tf_op jit(solution)/shard_map/all_to_all | solution.py:451
  118.3 0.7 copy-start.12
  138.6 30.5 %collective-permute-start.8 = (bf16[2,864,256]{2,1,0:T(8,128)(2,1)}, bf16[2,864,256]{2,1,0:T(8,128)(2,1)}, u32[]{:S(2)}, u32[]{:S(2)}) collective-permute-start(bf16[2,864,256]{2,1,0:T(8,128)(2,1)} %get-tuple-element.23), channel_id=1, source_target_pairs={{8,0},{16,8},{24,16},{32,24},{40,32},{48,40},{56,48},{64,56},{72,6... | collective-permute-start | bytes 2654216 | tf_op jit(solution)/shard_map/ppermute | solution.py:427
  142.3 26.9 %collective-permute-start.9 = (bf16[2,192,256]{2,1,0:T(8,128)(2,1)}, bf16[2,192,256]{2,1,0:T(8,128)(2,1)S(1)}, u32[]{:S(2)}, u32[]{:S(2)}) collective-permute-start(bf16[2,192,256]{2,1,0:T(8,128)(2,1)} %get-tuple-element.24), channel_id=1, source_target_pairs={{16,0},{24,8},{32,16},{40,24},{48,32},{56,40},{64,48},{72,56},{80,... | collective-permute-start | bytes 589832 | tf_op jit(solution)/shard_map/ppermute | solution.py:427
  145.3 0.7 copy-start.11
  145.4 1.0 copy-start.3
  145.4 1.2 copy-start.10
  150.2 26.4 %all-to-all-start.5 = ((bf16[8,2,192,256]{3,2,1,0:T(8,128)(2,1)}), bf16[8,2,192,256]{3,2,1,0:T(8,128)(2,1)S(1)}, u32[]{:S(2)}, u32[]{:S(2)}) async-start(bf16[8,2,192,256]{3,2,1,0:T(8,128)(2,1)} %joined.2.refs_1_), calls=%async_computation.5 | async-start | bytes 3145728 | tf_op jit(solution)/shard_map/all_to_all | solution.py:451
  173.9 7.5 %copy-start.4 = (bf16[8,192,256]{2,1,0:T(8,128)(2,1)S(1)}, bf16[8,192,256]{2,1,0:T(8,128)(2,1)}, u32[]{:S(2)}) copy-start(bf16[8,192,256]{2,1,0:T(8,128)(2,1)} %copy-done.3) | copy-start | bytes 2359300
  176.6 1.1 copy-start.1
  177.8 33.6 %all-to-all-start.4 = ((bf16[8,3,192,256]{3,2,1,0:T(8,128)(2,1)}), bf16[8,3,192,256]{3,2,1,0:T(8,128)(2,1)S(1)}, u32[]{:S(2)}, u32[]{:S(2)}) async-start(bf16[8,3,192,256]{3,2,1,0:T(8,128)(2,1)} %joined.3), calls=%async_computation.4 | async-start | bytes 4718592 | tf_op jit(solution)/shard_map/all_to_all | solution.py:451
  181.4 2.1 copy-start.2
  (1 other events, 0.7 us)

commit v5 on v4

--- a/solution.py
+++ b/solution.py
@@ -116,8 +116,7 @@
                 s[lo:hi] = dot(kv[lo:hi, :HD], q_of(b), ((1,), (1,)))
 
         for which in (0, 1):
-            for lo, hi in ((0, BLK), (BLK, KEYS)):
-                yield functools.partial(tile, lo, hi, which)
+            yield functools.partial(tile, 0, KEYS, which)
 
     def softmax(b):
         s, dp, p, ds = ss.at[b % 2], dps.at[b % 2], ps.at[b % 2], dss.at[b % 2]
@@ -184,6 +183,13 @@
             dv = dot(p[lo:hi], g_of(b), ((1,), (0,)))
             return jnp.concatenate([dk, dv], axis=1)
 
+        kept = []
+
+        def thinned(lo, hi):
+            if not kept:
+                kept.append(pair(SEG[2], KEYS))
+            return kept[0][lo - SEG[2] : hi - SEG[2]].astype(BF16)
+
         def own():
             acc_ref[0, b] = pair(0, BLK)
 
@@ -195,7 +201,7 @@
                 acc_ref[0, b - 1] += term
 
         def two():
-            term = pair(SEG[2], SEG[3]).astype(BF16)
+            term = thinned(SEG[2], SEG[3])
             if b == 0:
                 rnext_ref[0, NEXT_L1:NEXT_L2] = term
             elif b == 1:
@@ -204,14 +210,14 @@
                 acc_ref[0, b - 2] += spread(2, meta[OWN + 4 * b + 1], term)
 
         def four():
-            term = pair(SEG[3], SEG[4]).astype(BF16)
+            term = thinned(SEG[3], SEG[4])
             if b < 3:
                 rnext_ref[0, NEXT_L2 + 96 * b : NEXT_L2 + 96 * b + 96] = term
             else:
                 rnext_ref[0, 0:BLK] = (prev[...] + spread(4, meta[OWN + 4 * b + 2], term)).astype(BF16)
 
         def eight():
-            rfar_ref[0, 48 * b : 48 * b + 48] = pair(SEG[4], SEG[5]).astype(BF16)
+            rfar_ref[0, 48 * b : 48 * b + 48] = thinned(SEG[4], SEG[5])
 
         yield own
         yield near

time: 215 us -> 215 us (level)
  no operation moved by 1% of the time
where the time goes in v5:
time: 215 us; the launch traced here: 214 us
  waiting for transfers between devices  76.5 us (36%)
  Pallas kernels  66.6 us (31%)
  starting transfers between devices  64.1 us (30%)
  local copies, waits for them, and re-layouts  4.71 us (2%)
    pallas_call x2, Pallas kernels, attention(): pl.pallas_call(main_kernel, grid=(PAIR,), in_specs=[SMEM, lanes_of(2, 0),...  39.3 us
    all_to_all x6, waiting for transfers between devices, exchange(): return lax.all_to_all(x, LINE_AXES, 0, 0, tiled=True)  36 us
    ppermute x10, starting transfers between devices, shift(): return lax.ppermute(value, GROUP_AXES, pairs)  34.3 us
    all_to_all x6, starting transfers between devices, exchange(): return lax.all_to_all(x, LINE_AXES, 0, 0, tiled=True)  26.2 us
    ppermute x2, waiting for transfers between devices, both(): other = lax.ppermute(value, axis, [(0, 1), (1, 0)])  21.6 us
    ppermute x10, waiting for transfers between devices, shift(): return lax.ppermute(value, GROUP_AXES, pairs)  18.9 us
    pallas_call x3, Pallas kernels, packed(): pl.pallas_call(functools.partial(pack_kernel, pair, count), in_specs=[ANY...  7.92 us
    pallas_call x2, Pallas kernels, joined(): pl.pallas_call(join_kernel, grid=(PAIR,), in_specs=[SMEM, a_head(acc.shap...  7.65 us
  transfers between devices with their start and end apart: 18, of which 8 were waited for; matrix products, arithmetic and copies ran while one was open for 0% of the time, Pallas kernels for 29%

profile of v5, /device:TPU:38, one launch (start us, length us, event | category | flops | bytes accessed | tf_op | source)
XLA Modules:
  0.0 213.5 jit_solution(9127077969718147316)
XLA Ops:
  0.6 3.1 %packed.4 = bf16[8,4,192,256]{3,2,1,0:T(8,128)(2,1)} custom-call(bf16[192,4096]{1,0:T(8,128)(2,1)} %refs_0_.4, bf16[192,4096]{1,0:T(8,128)(2,1)} %refs_1_.4, bf16[192,4096]{1,0:T(8,128)(2,1)} %refs_0_.5, bf16[192,4096]{1,0:T(8,128)(2,1)} %refs_1_.5), custom_call_target="tpu_custom_call" | custom-call | bytes 8388608 | tf_op jit(solution)/shard_map/packed/pallas_call | solution.py:339
  3.8 4.5 %all-to-all-start.1 = ((bf16[8,4,192,256]{3,2,1,0:T(8,128)(2,1)}), bf16[8,4,192,256]{3,2,1,0:T(8,128)(2,1)S(1)}, u32[]{:S(2)}, u32[]{:S(2)}) async-start(bf16[8,4,192,256]{3,2,1,0:T(8,128)(2,1)} %packed.4), calls=%async_computation.1 | async-start | bytes 6291456 | tf_op jit(solution)/shard_map/all_to_all | solution.py:457
  8.3 2.7 %collective-permute-start = (s32[1,8]{1,0:T(1,128)S(1)}, s32[1,8]{1,0:T(1,128)S(1)}, u32[]{:S(2)}, u32[]{:S(2)}) collective-permute-start(s32[1,8]{1,0:T(1,128)S(1)} %pad_add_fusion.3), channel_id=1, source_target_pairs={{8,0},{16,8},{24,16},{32,24},{40,32},{48,40},{56,48},{64,56},{72,6... | collective-permute-start | bytes 104 | tf_op jit(solution)/shard_map/ppermute | solution.py:433
  11.1 3.0 %collective-permute-start.1 = (s32[1,8]{1,0:T(1,128)S(1)}, s32[1,8]{1,0:T(1,128)S(1)}, u32[]{:S(2)}, u32[]{:S(2)}) collective-permute-start(s32[1,8]{1,0:T(1,128)S(1)} %pad_add_fusion.3), channel_id=1, source_target_pairs={{16,0},{24,8},{32,16},{40,24},{48,32},{56,40},{64,48},{72,56},{80,... | collective-permute-start | bytes 104 | tf_op jit(solution)/shard_map/ppermute | solution.py:433
  15.9 3.0 %collective-permute-done.1 = s32[1,8]{1,0:T(1,128)S(1)} collective-permute-done((s32[1,8]{1,0:T(1,128)S(1)}, s32[1,8]{1,0:T(1,128)S(1)}, u32[]{:S(2)}, u32[]{:S(2)}) %collective-permute-start.1) | collective-permute-done | bytes 64 | tf_op jit(solution)/shard_map/ppermute | solution.py:433
  20.2 3.5 %collective-permute-start.3 = (s32[2,3,8]{2,1,0:T(4,128)S(1)}, s32[2,3,8]{2,1,0:T(4,128)S(1)}, u32[]{:S(2)}, u32[]{:S(2)}) collective-permute-start(s32[2,3,8]{2,1,0:T(4,128)S(1)} %pad_add_fusion.1), channel_id=1, source_target_pairs={{0,4},{4,0},{1,5},{5,1},{2,6},{6,2},{3,7},{7,3},{8,12},{12,8},{9,1... | collective-permute-start | bytes 584 | tf_op jit(solution)/shard_map/ppermute | solution.py:437
  23.9 2.4 %packed.3 = bf16[8,2,192,256]{3,2,1,0:T(8,128)(2,1)} custom-call(bf16[192,4096]{1,0:T(8,128)(2,1)} %refs_0_.4, bf16[192,4096]{1,0:T(8,128)(2,1)} %refs_1_.4, s32[3,8]{1,0:T(4,128)} %copy-done.7), custom_call_target="tpu_custom_call" | custom-call | bytes 8388608 | tf_op jit(solution)/shard_map/packed/pallas_call | solution.py:339
  26.3 20.5 %collective-permute-done.3 = s32[2,3,8]{2,1,0:T(4,128)S(1)} collective-permute-done((s32[2,3,8]{2,1,0:T(4,128)S(1)}, s32[2,3,8]{2,1,0:T(4,128)S(1)}, u32[]{:S(2)}, u32[]{:S(2)}) %collective-permute-start.3) | collective-permute-done | bytes 224 | tf_op jit(solution)/shard_map/ppermute | solution.py:437
  46.9 4.3 %all-to-all-start = ((bf16[8,2,192,256]{3,2,1,0:T(8,128)(2,1)}), bf16[8,2,192,256]{3,2,1,0:T(8,128)(2,1)}, u32[]{:S(2)}, u32[]{:S(2)}) async-start(bf16[8,2,192,256]{3,2,1,0:T(8,128)(2,1)} %packed.3), calls=%async_computation | async-start | bytes 3145728 | tf_op jit(solution)/shard_map/all_to_all | solution.py:457
  53.6 3.8 %collective-permute-start.6 = (bf16[2,864,256]{2,1,0:T(8,128)(2,1)}, bf16[2,864,256]{2,1,0:T(8,128)(2,1)}, u32[]{:S(2)}, u32[]{:S(2)}) collective-permute-start(bf16[2,864,256]{2,1,0:T(8,128)(2,1)} %get-tuple-element.17.refs_2_), channel_id=1, source_target_pairs={{0,8},{8,16},{16,24},{24,32},{32,40},{40,48},{48,56},{56,64},{64,7... | collective-permute-start | bytes 2654216 | tf_op jit(solution)/shard_map/ppermute | solution.py:433
  57.4 4.3 %collective-permute-start.7 = (bf16[2,192,256]{2,1,0:T(8,128)(2,1)S(1)}, bf16[2,192,256]{2,1,0:T(8,128)(2,1)S(1)}, u32[]{:S(2)}, u32[]{:S(2)}) collective-permute-start(bf16[2,192,256]{2,1,0:T(8,128)(2,1)S(1)} %get-tuple-element.20), channel_id=1, source_target_pairs={{0,16},{8,24},{16,32},{24,40},{32,48},{40,56},{48,64},{56,72},{64,... | collective-permute-start | bytes 589832 | tf_op jit(solution)/shard_map/ppermute | solution.py:433
  61.7 2.4 %packed.5 = bf16[8,2,192,256]{3,2,1,0:T(8,128)(2,1)} custom-call(bf16[192,4096]{1,0:T(8,128)(2,1)} %refs_0_.5, bf16[192,4096]{1,0:T(8,128)(2,1)} %refs_1_.5, bf16[2,864,256]{2,1,0:T(8,128)(2,1)} %get-tuple-element.17.refs_2_), custom_call_target="tpu_custom_call" | custom-call | bytes 8388608 | tf_op jit(solution)/shard_map/packed/pallas_call | solution.py:339
  64.1 8.7 %all-to-all-done.y_ref = bf16[8,2,192,256]{3,2,1,0:T(8,128)(2,1)} async-done(((bf16[8,2,192,256]{3,2,1,0:T(8,128)(2,1)}), bf16[8,2,192,256]{3,2,1,0:T(8,128)(2,1)}, u32[]{:S(2)}, u32[]{:S(2)}) %all-to-all-start) | async-done | bytes 1572896 | tf_op jit(solution)/shard_map/all_to_all | solution.py:457
  72.8 4.3 %all-to-all-start.2 = ((bf16[8,2,192,256]{3,2,1,0:T(8,128)(2,1)}), bf16[8,2,192,256]{3,2,1,0:T(8,128)(2,1)}, u32[]{:S(2)}, u32[]{:S(2)}) async-start(bf16[8,2,192,256]{3,2,1,0:T(8,128)(2,1)} %packed.5), calls=%async_computation.2 | async-start | bytes 3145728 | tf_op jit(solution)/shard_map/all_to_all | solution.py:457
  77.1 2.1 rows_to_send.3
  79.3 3.8 %collective-permute-start.4 = (bf16[2,864,256]{2,1,0:T(8,128)(2,1)S(1)}, bf16[2,864,256]{2,1,0:T(8,128)(2,1)}, u32[]{:S(2)}, u32[]{:S(2)}) collective-permute-start(bf16[2,864,256]{2,1,0:T(8,128)(2,1)S(1)} %get-tuple-element.18.refs_0_), channel_id=1, source_target_pairs={{0,8},{8,16},{16,24},{24,32},{32,40},{40,48},{48,56},{56,64},{64,7... | collective-permute-start | bytes 2654216 | tf_op jit(solution)/shard_map/ppermute | solution.py:433
  83.0 4.3 %collective-permute-start.5 = (bf16[2,192,256]{2,1,0:T(8,128)(2,1)S(1)}, bf16[2,192,256]{2,1,0:T(8,128)(2,1)S(1)}, u32[]{:S(2)}, u32[]{:S(2)}) collective-permute-start(bf16[2,192,256]{2,1,0:T(8,128)(2,1)S(1)} %get-tuple-element.19), channel_id=1, source_target_pairs={{0,16},{8,24},{16,32},{24,40},{32,48},{40,56},{48,64},{56,72},{64,... | collective-permute-start | bytes 589832 | tf_op jit(solution)/shard_map/ppermute | solution.py:433
  88.1 19.7 %attention.2 = (bf16[8,192,256]{2,1,0:T(8,128)(2,1)}, f32[2,4,384,256]{3,2,1,0:T(8,128)}, bf16[2,864,256]{2,1,0:T(8,128)(2,1)}, bf16[2,192,256]{2,1,0:T(8,128)(2,1)}) custom-call(s32[64]{0:T(128)} %copy-done.5, bf16[8,4,192,256]{3,2,1,0:T(8,128)(2,1)} %copy-done, bf16[8,4,192,256]{3,2,1,0:T(8,128)(2,1)} %copy-done, ...), custom_call_target="tpu_custom_call" | custom-call | flops 13023313920 | bytes 10485760 | tf_op jit(solution)/shard_map/attention/pallas_call | solution.py:389
  109.7 3.8 %collective-permute-start.11 = (bf16[2,192,256]{2,1,0:T(8,128)(2,1)}, bf16[2,192,256]{2,1,0:T(8,128)(2,1)S(1)}, u32[]{:S(2)}, u32[]{:S(2)}) collective-permute-start(bf16[2,192,256]{2,1,0:T(8,128)(2,1)} %get-tuple-element.28), channel_id=1, source_target_pairs={{16,0},{24,8},{32,16},{40,24},{48,32},{56,40},{64,48},{72,56},{80,... | collective-permute-start | bytes 589832 | tf_op jit(solution)/shard_map/ppermute | solution.py:433
  113.5 4.7 %all-to-all-start.3 = ((bf16[8,192,256]{2,1,0:T(8,128)(2,1)}), bf16[8,192,256]{2,1,0:T(8,128)(2,1)S(1)}, u32[]{:S(2)}, u32[]{:S(2)}) async-start(bf16[8,192,256]{2,1,0:T(8,128)(2,1)} %get-tuple-element.21.refs_0_), calls=%async_computation.3 | async-start | bytes 1572864 | tf_op jit(solution)/shard_map/all_to_all | solution.py:457
  118.9 19.7 %attention.3 = (bf16[8,192,256]{2,1,0:T(8,128)(2,1)}, f32[2,4,384,256]{3,2,1,0:T(8,128)}, bf16[2,864,256]{2,1,0:T(8,128)(2,1)}, bf16[2,192,256]{2,1,0:T(8,128)(2,1)}) custom-call(s32[64]{0:T(128)} %copy-done.5, bf16[8,2,192,256]{3,2,1,0:T(8,128)(2,1)} %all-to-all-done.y_ref, bf16[8,2,192,256]{3,2,1,0:T(8,128)(2,1)} %all-to-all-done.2.w_ref, ...), custom_call_target="tpu_custom_call" | custom-call | flops 13023313920 | bytes 10485760 | tf_op jit(solution)/shard_map/attention/pallas_call | solution.py:389
  138.5 3.6 %collective-permute-start.8 = (bf16[2,864,256]{2,1,0:T(8,128)(2,1)}, bf16[2,864,256]{2,1,0:T(8,128)(2,1)}, u32[]{:S(2)}, u32[]{:S(2)}) collective-permute-start(bf16[2,864,256]{2,1,0:T(8,128)(2,1)} %get-tuple-element.23), channel_id=1, source_target_pairs={{8,0},{16,8},{24,16},{32,24},{40,32},{48,40},{56,48},{64,56},{72,6... | collective-permute-start | bytes 2654216 | tf_op jit(solution)/shard_map/ppermute | solution.py:433
  142.2 3.0 %collective-permute-start.9 = (bf16[2,192,256]{2,1,0:T(8,128)(2,1)}, bf16[2,192,256]{2,1,0:T(8,128)(2,1)S(1)}, u32[]{:S(2)}, u32[]{:S(2)}) collective-permute-start(bf16[2,192,256]{2,1,0:T(8,128)(2,1)} %get-tuple-element.24), channel_id=1, source_target_pairs={{16,0},{24,8},{32,16},{40,24},{48,32},{56,40},{64,48},{72,56},{80,... | collective-permute-start | bytes 589832 | tf_op jit(solution)/shard_map/ppermute | solution.py:433
  146.4 3.6 %joined.2.refs_1_ = bf16[8,2,192,256]{3,2,1,0:T(8,128)(2,1)} custom-call(s32[64]{0:T(128)} %copy-done.5, f32[2,4,384,256]{3,2,1,0:T(8,128)} %get-tuple-element.26.acc_ref, bf16[2,864,256]{2,1,0:T(8,128)(2,1)} %copy-done.10, bf16[2,192,256]{2,1,0:T(8,128)(2,1)} %copy-done.11, bf16[8,192,256]{2,1,0:T(8,128)(2,1)} %get-tuple-element.25.refs_0_, ...), custom_call_target="tpu_custom_call" | custom-call | flops 68719476736 | bytes 4194304 | tf_op jit(solution)/shard_map/joined/pallas_call | solution.py:416
  150.1 4.8 %all-to-all-start.5 = ((bf16[8,2,192,256]{3,2,1,0:T(8,128)(2,1)}), bf16[8,2,192,256]{3,2,1,0:T(8,128)(2,1)S(1)}, u32[]{:S(2)}, u32[]{:S(2)}) async-start(bf16[8,2,192,256]{3,2,1,0:T(8,128)(2,1)} %joined.2.refs_1_), calls=%async_computation.5 | async-start | bytes 3145728 | tf_op jit(solution)/shard_map/all_to_all | solution.py:457
  154.9 14.2 %collective-permute-done.9.far_ref = bf16[2,192,256]{2,1,0:T(8,128)(2,1)S(1)} collective-permute-done((bf16[2,192,256]{2,1,0:T(8,128)(2,1)}, bf16[2,192,256]{2,1,0:T(8,128)(2,1)S(1)}, u32[]{:S(2)}, u32[]{:S(2)}) %collective-permute-start.9) | collective-permute-done | bytes 196640 | tf_op jit(solution)/shard_map/ppermute | solution.py:433
  169.7 4.0 %joined.3 = bf16[8,3,192,256]{3,2,1,0:T(8,128)(2,1)} custom-call(s32[64]{0:T(128)} %copy-done.5, f32[2,4,384,256]{3,2,1,0:T(8,128)} %get-tuple-element.22.acc_ref, bf16[2,864,256]{2,1,0:T(8,128)(2,1)} %collective-permute-done.8.near_ref, bf16[2,192,256]{2,1,0:T(8,128)(2,1)} %copy-done.14, bf16[8,192,256]{2,1,0:T(8,128)(2,1)} %get-tuple-element.25.refs_0_, ...), custom_call_target="tpu_custom_call" | custom-call | flops 68719476736 | bytes 4194304 | tf_op jit(solution)/shard_map/joined/pallas_call | solution.py:416
  173.7 2.8 %all-to-all-done.5.w_ref = bf16[8,2,192,256]{3,2,1,0:T(8,128)(2,1)S(1)} async-done(((bf16[8,2,192,256]{3,2,1,0:T(8,128)(2,1)}), bf16[8,2,192,256]{3,2,1,0:T(8,128)(2,1)S(1)}, u32[]{:S(2)}, u32[]{:S(2)}) %all-to-all-start.5) | async-done | bytes 1572896 | tf_op jit(solution)/shard_map/all_to_all | solution.py:457
  177.6 3.6 %all-to-all-start.4 = ((bf16[8,3,192,256]{3,2,1,0:T(8,128)(2,1)}), bf16[8,3,192,256]{3,2,1,0:T(8,128)(2,1)S(1)}, u32[]{:S(2)}, u32[]{:S(2)}) async-start(bf16[8,3,192,256]{3,2,1,0:T(8,128)(2,1)} %joined.3), calls=%async_computation.4 | async-start | bytes 4718592 | tf_op jit(solution)/shard_map/all_to_all | solution.py:457
  183.3 3.4 %unpacked.4 = (bf16[192,4096]{1,0:T(8,128)(2,1)}, bf16[192,4096]{1,0:T(8,128)(2,1)}) custom-call(bf16[8,2,192,256]{3,2,1,0:T(8,128)(2,1)S(1)} %copy-done.2), custom_call_target="tpu_custom_call" | custom-call | bytes 8388608 | tf_op jit(solution)/shard_map/unpacked/pallas_call | solution.py:357
  186.7 24.5 %all-to-all-done.4.w_ref = bf16[8,3,192,256]{3,2,1,0:T(8,128)(2,1)S(1)} async-done(((bf16[8,3,192,256]{3,2,1,0:T(8,128)(2,1)}), bf16[8,3,192,256]{3,2,1,0:T(8,128)(2,1)S(1)}, u32[]{:S(2)}, u32[]{:S(2)}) %all-to-all-start.4) | async-done | bytes 2359328 | tf_op jit(solution)/shard_map/all_to_all | solution.py:457
  211.2 2.1 %unpacked.5 = (bf16[192,4096]{1,0:T(8,128)(2,1)}, bf16[192,4096]{1,0:T(8,128)(2,1)}, bf16[192,4096]{1,0:T(8,128)(2,1)}) custom-call(bf16[8,3,192,256]{3,2,1,0:T(8,128)(2,1)S(1)} %all-to-all-done.4.w_ref, bf16[192,4096]{1,0:T(8,128)(2,1)} %unpacked.3.refs_0_, ...), custom_call_target="tpu_custom_call", output_to_operand_aliasing={{0}: (1, {}), {1}: (2, {}), {2}: (3, {})} | custom-call | bytes 8388608 | tf_op jit(solution)/shard_map/unpacked/pallas_call | solution.py:357
  (63 shorter events, 14.0 us)
Async XLA Ops:
  3.7 4.5 %copy-start.8 = (s32[1,4]{1,0:T(1,128)S(1)}, s32[1,4]{1,0:T(1,128)}, u32[]{:S(2)}) copy-start(s32[1,4]{1,0:T(1,128)} %param.11) | copy-start | bytes 52
  3.7 4.5 %copy-start.9 = (s32[1,4]{1,0:T(1,128)S(1)}, s32[1,4]{1,0:T(1,128)}, u32[]{:S(2)}) copy-start(s32[1,4]{1,0:T(1,128)} %param.10) | copy-start | bytes 52
  3.8 43.1 %all-to-all-start.1 = ((bf16[8,4,192,256]{3,2,1,0:T(8,128)(2,1)}), bf16[8,4,192,256]{3,2,1,0:T(8,128)(2,1)S(1)}, u32[]{:S(2)}, u32[]{:S(2)}) async-start(bf16[8,4,192,256]{3,2,1,0:T(8,128)(2,1)} %packed.4), calls=%async_computation.1 | async-start | bytes 6291456 | tf_op jit(solution)/shard_map/all_to_all | solution.py:457
  8.3 7.5 %collective-permute-start = (s32[1,8]{1,0:T(1,128)S(1)}, s32[1,8]{1,0:T(1,128)S(1)}, u32[]{:S(2)}, u32[]{:S(2)}) collective-permute-start(s32[1,8]{1,0:T(1,128)S(1)} %pad_add_fusion.3), channel_id=1, source_target_pairs={{8,0},{16,8},{24,16},{32,24},{40,32},{48,40},{56,48},{64,56},{72,6... | collective-permute-start | bytes 104 | tf_op jit(solution)/shard_map/ppermute | solution.py:433
  11.1 7.8 %collective-permute-start.1 = (s32[1,8]{1,0:T(1,128)S(1)}, s32[1,8]{1,0:T(1,128)S(1)}, u32[]{:S(2)}, u32[]{:S(2)}) collective-permute-start(s32[1,8]{1,0:T(1,128)S(1)} %pad_add_fusion.3), channel_id=1, source_target_pairs={{16,0},{24,8},{32,16},{40,24},{48,32},{56,40},{64,48},{72,56},{80,... | collective-permute-start | bytes 104 | tf_op jit(solution)/shard_map/ppermute | solution.py:433
  19.0 4.9 %copy-start.7 = (s32[3,8]{1,0:T(4,128)}, s32[3,8]{1,0:T(4,128)S(1)}, u32[]{:S(2)}) copy-start(s32[3,8]{1,0:T(4,128)S(1)} %pad_add_fusion.2.refs_2_) | copy-start | bytes 292
  19.0 1.2 collective-permute-start.2
  20.2 26.6 %collective-permute-start.3 = (s32[2,3,8]{2,1,0:T(4,128)S(1)}, s32[2,3,8]{2,1,0:T(4,128)S(1)}, u32[]{:S(2)}, u32[]{:S(2)}) collective-permute-start(s32[2,3,8]{2,1,0:T(4,128)S(1)} %pad_add_fusion.1), channel_id=1, source_target_pairs={{0,4},{4,0},{1,5},{5,1},{2,6},{6,2},{3,7},{7,3},{8,12},{12,8},{9,1... | collective-permute-start | bytes 584 | tf_op jit(solution)/shard_map/ppermute | solution.py:437
  46.9 4.7 %copy-start = (bf16[8,4,192,256]{3,2,1,0:T(8,128)(2,1)}, bf16[8,4,192,256]{3,2,1,0:T(8,128)(2,1)S(1)}, u32[]{:S(2)}) copy-start(bf16[8,4,192,256]{3,2,1,0:T(8,128)(2,1)S(1)} %all-to-all-done.1.y_ref.w_ref) | copy-start | bytes 9437188
  46.9 25.9 %all-to-all-start = ((bf16[8,2,192,256]{3,2,1,0:T(8,128)(2,1)}), bf16[8,2,192,256]{3,2,1,0:T(8,128)(2,1)}, u32[]{:S(2)}, u32[]{:S(2)}) async-start(bf16[8,2,192,256]{3,2,1,0:T(8,128)(2,1)} %packed.3), calls=%async_computation | async-start | bytes 3145728 | tf_op jit(solution)/shard_map/all_to_all | solution.py:457
  51.5 25.6 %copy-start.5 = (s32[64]{0:T(128)}, s32[64]{0:T(128)S(1)}, u32[]{:S(2)}) copy-start(s32[64]{0:T(128)S(1)} %pad_add_fusion.4.meta) | copy-start | bytes 772
  53.6 33.8 %collective-permute-start.6 = (bf16[2,864,256]{2,1,0:T(8,128)(2,1)}, bf16[2,864,256]{2,1,0:T(8,128)(2,1)}, u32[]{:S(2)}, u32[]{:S(2)}) collective-permute-start(bf16[2,864,256]{2,1,0:T(8,128)(2,1)} %get-tuple-element.17.refs_2_), channel_id=1, source_target_pairs={{0,8},{8,16},{16,24},{24,32},{32,40},{40,48},{48,56},{56,64},{64,7... | collective-permute-start | bytes 2654216 | tf_op jit(solution)/shard_map/ppermute | solution.py:433
  57.4 30.0 %collective-permute-start.7 = (bf16[2,192,256]{2,1,0:T(8,128)(2,1)S(1)}, bf16[2,192,256]{2,1,0:T(8,128)(2,1)S(1)}, u32[]{:S(2)}, u32[]{:S(2)}) collective-permute-start(bf16[2,192,256]{2,1,0:T(8,128)(2,1)S(1)} %get-tuple-element.20), channel_id=1, source_target_pairs={{0,16},{8,24},{16,32},{24,40},{32,48},{40,56},{48,64},{56,72},{64,... | collective-permute-start | bytes 589832 | tf_op jit(solution)/shard_map/ppermute | solution.py:433
  72.8 40.7 %all-to-all-start.2 = ((bf16[8,2,192,256]{3,2,1,0:T(8,128)(2,1)}), bf16[8,2,192,256]{3,2,1,0:T(8,128)(2,1)}, u32[]{:S(2)}, u32[]{:S(2)}) async-start(bf16[8,2,192,256]{3,2,1,0:T(8,128)(2,1)} %packed.5), calls=%async_computation.2 | async-start | bytes 3145728 | tf_op jit(solution)/shard_map/all_to_all | solution.py:457
  79.2 8.1 %copy-start.6 = (bf16[2,864,256]{2,1,0:T(8,128)(2,1)}, bf16[2,864,256]{2,1,0:T(8,128)(2,1)S(1)}, u32[]{:S(2)}) copy-start(bf16[2,864,256]{2,1,0:T(8,128)(2,1)S(1)} %get-tuple-element.18.refs_0_) | copy-start | bytes 2654212
  79.3 38.9 %collective-permute-start.4 = (bf16[2,864,256]{2,1,0:T(8,128)(2,1)S(1)}, bf16[2,864,256]{2,1,0:T(8,128)(2,1)}, u32[]{:S(2)}, u32[]{:S(2)}) collective-permute-start(bf16[2,864,256]{2,1,0:T(8,128)(2,1)S(1)} %get-tuple-element.18.refs_0_), channel_id=1, source_target_pairs={{0,8},{8,16},{16,24},{24,32},{32,40},{40,48},{48,56},{56,64},{64,7... | collective-permute-start | bytes 2654216 | tf_op jit(solution)/shard_map/ppermute | solution.py:433
  83.0 35.2 %collective-permute-start.5 = (bf16[2,192,256]{2,1,0:T(8,128)(2,1)S(1)}, bf16[2,192,256]{2,1,0:T(8,128)(2,1)S(1)}, u32[]{:S(2)}, u32[]{:S(2)}) collective-permute-start(bf16[2,192,256]{2,1,0:T(8,128)(2,1)S(1)} %get-tuple-element.19), channel_id=1, source_target_pairs={{0,16},{8,24},{16,32},{24,40},{32,48},{40,56},{48,64},{56,72},{64,... | collective-permute-start | bytes 589832 | tf_op jit(solution)/shard_map/ppermute | solution.py:433
  87.4 0.7 copy-start.13
  107.7 37.5 %collective-permute-start.10 = (bf16[2,864,256]{2,1,0:T(8,128)(2,1)}, bf16[2,864,256]{2,1,0:T(8,128)(2,1)S(1)}, u32[]{:S(2)}, u32[]{:S(2)}) collective-permute-start(bf16[2,864,256]{2,1,0:T(8,128)(2,1)} %get-tuple-element.27), channel_id=1, source_target_pairs={{8,0},{16,8},{24,16},{32,24},{40,32},{48,40},{56,48},{64,56},{72,6... | collective-permute-start | bytes 2654216 | tf_op jit(solution)/shard_map/ppermute | solution.py:433
  109.7 35.5 %collective-permute-start.11 = (bf16[2,192,256]{2,1,0:T(8,128)(2,1)}, bf16[2,192,256]{2,1,0:T(8,128)(2,1)S(1)}, u32[]{:S(2)}, u32[]{:S(2)}) collective-permute-start(bf16[2,192,256]{2,1,0:T(8,128)(2,1)} %get-tuple-element.28), channel_id=1, source_target_pairs={{16,0},{24,8},{32,16},{40,24},{48,32},{56,40},{64,48},{72,56},{80,... | collective-permute-start | bytes 589832 | tf_op jit(solution)/shard_map/ppermute | solution.py:433
  113.5 31.7 %all-to-all-start.3 = ((bf16[8,192,256]{2,1,0:T(8,128)(2,1)}), bf16[8,192,256]{2,1,0:T(8,128)(2,1)S(1)}, u32[]{:S(2)}, u32[]{:S(2)}) async-start(bf16[8,192,256]{2,1,0:T(8,128)(2,1)} %get-tuple-element.21.refs_0_), calls=%async_computation.3 | async-start | bytes 1572864 | tf_op jit(solution)/shard_map/all_to_all | solution.py:457
  118.2 0.7 copy-start.12
  138.5 30.5 %collective-permute-start.8 = (bf16[2,864,256]{2,1,0:T(8,128)(2,1)}, bf16[2,864,256]{2,1,0:T(8,128)(2,1)}, u32[]{:S(2)}, u32[]{:S(2)}) collective-permute-start(bf16[2,864,256]{2,1,0:T(8,128)(2,1)} %get-tuple-element.23), channel_id=1, source_target_pairs={{8,0},{16,8},{24,16},{32,24},{40,32},{48,40},{56,48},{64,56},{72,6... | collective-permute-start | bytes 2654216 | tf_op jit(solution)/shard_map/ppermute | solution.py:433
  142.2 26.9 %collective-permute-start.9 = (bf16[2,192,256]{2,1,0:T(8,128)(2,1)}, bf16[2,192,256]{2,1,0:T(8,128)(2,1)S(1)}, u32[]{:S(2)}, u32[]{:S(2)}) collective-permute-start(bf16[2,192,256]{2,1,0:T(8,128)(2,1)} %get-tuple-element.24), channel_id=1, source_target_pairs={{16,0},{24,8},{32,16},{40,24},{48,32},{56,40},{64,48},{72,56},{80,... | collective-permute-start | bytes 589832 | tf_op jit(solution)/shard_map/ppermute | solution.py:433
  145.2 0.7 copy-start.11
  145.2 1.0 copy-start.3
  145.2 1.2 copy-start.10
  150.1 26.4 %all-to-all-start.5 = ((bf16[8,2,192,256]{3,2,1,0:T(8,128)(2,1)}), bf16[8,2,192,256]{3,2,1,0:T(8,128)(2,1)S(1)}, u32[]{:S(2)}, u32[]{:S(2)}) async-start(bf16[8,2,192,256]{3,2,1,0:T(8,128)(2,1)} %joined.2.refs_1_), calls=%async_computation.5 | async-start | bytes 3145728 | tf_op jit(solution)/shard_map/all_to_all | solution.py:457
  173.7 7.5 %copy-start.4 = (bf16[8,192,256]{2,1,0:T(8,128)(2,1)S(1)}, bf16[8,192,256]{2,1,0:T(8,128)(2,1)}, u32[]{:S(2)}) copy-start(bf16[8,192,256]{2,1,0:T(8,128)(2,1)} %copy-done.3) | copy-start | bytes 2359300
  176.5 1.1 copy-start.1
  177.6 33.6 %all-to-all-start.4 = ((bf16[8,3,192,256]{3,2,1,0:T(8,128)(2,1)}), bf16[8,3,192,256]{3,2,1,0:T(8,128)(2,1)S(1)}, u32[]{:S(2)}, u32[]{:S(2)}) async-start(bf16[8,3,192,256]{3,2,1,0:T(8,128)(2,1)} %joined.3), calls=%async_computation.4 | async-start | bytes 4718592 | tf_op jit(solution)/shard_map/all_to_all | solution.py:457
  181.3 2.1 copy-start.2
  (1 other events, 0.7 us)
